TPU v7x, 32 devices: a whole 2x2x4 slice. The times are simulated.
32 devices in a mesh: groups: 2 (over y), left: 4 (over z), right: 2 (over x), mpo: 2 (over core).
Axes of the slice: x: 2, y: 2, z: 4, core: 2. Of those that a mesh axis runs over, the one named last changes fastest.
Arguments:
- theta: bfloat16 [16, 128, 128], P(('groups', 'left', 'right')), parts along dimension 0, may hold values from -6 to 6
- left_env: bfloat16 [8, 64, 128, 128], P(('groups', 'mpo'), 'left'), parts along dimension 0, may hold values from -1 to 1
- right_env: bfloat16 [8, 32, 128, 128], P(('groups', 'mpo'), 'right'), parts along dimension 0, may hold values from -1 to 1
- terms: int32 [8, 2, 2, 16, 14], P(('groups', 'left'), 'right', 'mpo'), parts along dimension 0, may hold values from 0 to 31, as said below
Outputs:
- h_theta: float32 [16, 128, 128], P(('groups', 'left', 'right')), parts along dimension 0
- h_second: float32 [16, 128, 128], P(('groups', 'left', 'right')), parts along dimension 0
There are 2 independent parts, one for each index of `groups`. A program takes and returns all parts, laid end to end along the dimension named above; each array names one. Nothing has to cross between parts.
Inputs may be any that keep to these rules, and one draw needn't show every extreme that they name: `terms`: field 0 is below 32, field 1 below 2, the 6 right tiles below 16, the 6 output left indices below 4. In the list of every device, at most 8 entries name one target right index, and some target is named by exactly 8 entries.
All inputs are finite; a program needn't handle non-finite values.
Results may differ from a plain program's by a relative error of at most 0.0016.
Values may be sent and summed in bfloat16 or wider, within the bound.
No kernel may reach another device: no remote copies, remote signals or barrier semaphores. Data moves between devices by JAX's collectives and lax.ppermute only.
A program may use at most 64 MiB of HBM per device.

v0:
```python
import jax
import jax.numpy as jnp
from jax import lax
from jax.sharding import PartitionSpec as P


def slot_of(target_right, right_count):
    hits = (target_right[..., None] == jnp.arange(right_count, dtype=jnp.int32)).astype(jnp.int32)
    return jnp.sum((jnp.cumsum(hits, axis=-2) - 1) * hits, axis=-1)


def accumulate(inter_tiles, meta_rows, right_flat, rt_dev, left_count, right_per):
    tile_size = inter_tiles.shape[-1]
    accum = jnp.zeros((left_count, tile_size, tile_size), jnp.float32)
    for which in range(right_per):
        right_pick = right_flat[meta_rows[:, 0] * rt_dev + meta_rows[:, 1 + which]]
        products = jnp.einsum(
            "sij,sjk->sik", inter_tiles, right_pick, preferred_element_type=jnp.float32
        )
        accum = accum.at[meta_rows[:, 1 + right_per + which]].add(products)
    return accum


def local(theta, left_env, right_env, terms):
    tile_size = theta.shape[-1]
    lt_dev = left_env.shape[1]
    rt_dev = right_env.shape[1]
    left_flat = left_env.reshape(-1, tile_size, tile_size)
    right_flat = right_env.reshape(-1, tile_size, tile_size)
    left_count = lax.axis_size("left")
    right_count = lax.axis_size("right")
    entries = terms[0, 0, 0]
    rows_dev = entries.shape[0]
    capacity = rows_dev // 2
    right_per = (entries.shape[1] - 2) // 2
    target_right = entries[:, 1]
    slot_rank = slot_of(target_right, right_count)
    meta = jnp.concatenate([(entries[:, 0] // lt_dev)[:, None], entries[:, 2:]], axis=-1)
    meta_buffer = (
        jnp.zeros((right_count, capacity, 1 + 2 * right_per), jnp.int32)
        .at[target_right, slot_rank]
        .set(meta)
    )
    got_meta = lax.all_to_all(meta_buffer, "right", split_axis=0, concat_axis=0, tiled=True)
    meta_rows = got_meta.reshape(-1, 1 + 2 * right_per)
    left_pick = left_flat[entries[:, 0]]

    def apply_ham(vector):
        inter = jnp.einsum(
            "sik,kj->sij", left_pick, vector[0], preferred_element_type=jnp.float32
        ).astype(jnp.bfloat16)
        buffer = (
            jnp.zeros((right_count, capacity, tile_size, tile_size), jnp.bfloat16)
            .at[target_right, slot_rank]
            .set(inter)
        )
        got_tiles = lax.all_to_all(buffer, "right", split_axis=0, concat_axis=0, tiled=True)
        return accumulate(
            got_tiles.reshape(-1, tile_size, tile_size),
            meta_rows,
            right_flat,
            rt_dev,
            left_count,
            right_per,
        )

    def combine(accum):
        own_tile = lax.psum_scatter(accum, "left", scatter_dimension=0, tiled=True)
        summed = lax.psum(own_tile, "mpo")
        return summed

    h_theta = combine(apply_ham(theta))
    square_sum = lax.psum(jnp.sum(h_theta * h_theta), ("left", "right"))
    norm_scale = jnp.sqrt(square_sum / (left_count * right_count * tile_size * tile_size) + 1e-06)
    second = (h_theta / norm_scale).astype(jnp.bfloat16)
    h_second = combine(apply_ham(second))
    return (h_theta, h_second)


def solution(mesh):
    in_specs = (
        P(("groups", "left", "right"), None, None),
        P(("groups", "mpo"), "left", None, None),
        P(("groups", "mpo"), "right", None, None),
        P(("groups", "left"), "right", "mpo", None, None),
    )
    out_specs = (
        P(("groups", "left", "right"), None, None),
        P(("groups", "left", "right"), None, None),
    )
    return jax.shard_map(local, mesh=mesh, in_specs=in_specs, out_specs=out_specs, check_vma=False)
```

profile of v0, /device:TPU:0, one launch (start us, length us, event | category | flops | bytes accessed | tf_op | source)
XLA Modules:
  0.0 198.8 jit_solution(5798821225082747869)
XLA Ops:
  9.0 2.4 %scatter_fusion = s32[2,8,13]{2,1,0:T(8,128)} fusion(s32[2,8,13]{2,1,0:T(8,128)} %broadcast_in_dim.2, s32[16]{0:T(128)S(1)} %get-tuple-element.16, s32[16,13]{1,0:T(8,128)S(1)} %copy.6), kind=kCustom, calls=%fused_computation.7 | custom fusion | bytes 2624 | tf_op jit(solution)/shard_map/scatter | solution.py:42
  11.4 4.2 %all-to-all-start = ((s32[2,8,13]{2,1,0:T(8,128)}), s32[2,8,13]{2,1,0:T(8,128)S(1)}, u32[]{:S(2)}, u32[]{:S(2)}) async-start(s32[2,8,13]{2,1,0:T(8,128)} %scatter_fusion), calls=%async_computation | async-start | bytes 16384 | tf_op jit(solution)/shard_map/all_to_all | solution.py:44
  15.6 1.9 gather_fusion
  18.7 2.7 %scatter_fusion.1 = bf16[2,8,128,128]{3,2,1,0:T(8,128)(2,1)} fusion(bf16[2,8,128,128]{3,2,1,0:T(8,128)(2,1)} %broadcast.99.clone, s32[16]{0:T(128)S(1)} %get-tuple-element.16, bf16[16,128,128]{2,1,0:T(8,128)(2,1)S(1)} %convolution_convert_fusion.1), kind=kCustom, calls=%fused_computation.8 | custom fusion | bytes 1572992 | tf_op jit(solution)/shard_map/scatter | solution.py:55
  21.4 3.5 %all-to-all-start.1 = ((bf16[2,8,128,128]{3,2,1,0:T(8,128)(2,1)}), bf16[2,8,128,128]{3,2,1,0:T(8,128)(2,1)S(1)}, u32[]{:S(2)}, u32[]{:S(2)}) async-start(bf16[2,8,128,128]{3,2,1,0:T(8,128)(2,1)} %scatter_fusion.1), calls=%async_computation.1 | async-start | bytes 1048576 | tf_op jit(solution)/shard_map/all_to_all | solution.py:57
  41.3 2.6 %scatter_fusion.2 = f32[4,128,128]{2,1,0:T(8,128)S(1)} fusion(f32[4,128,128]{2,1,0:T(8,128)S(1)} %broadcast.92.clone, s32[16]{0:T(128)S(1)} %fusion.5, f32[16,128,128]{2,1,0:T(8,128)} %fusion.19), kind=kCustom, calls=%fused_computation.9 | custom fusion | flops 262144 | bytes 3145792 | tf_op jit(solution)/shard_map/scatter-add | solution.py:20
  43.9 2.6 %scatter_fusion.3 = f32[4,128,128]{2,1,0:T(8,128)S(1)} fusion(f32[4,128,128]{2,1,0:T(8,128)S(1)} %scatter_fusion.2, s32[16]{0:T(128)S(1)} %fusion.7, f32[16,128,128]{2,1,0:T(8,128)} %fusion.20), kind=kCustom, calls=%fused_computation.10 | custom fusion | flops 262144 | bytes 3145792 | tf_op jit(solution)/shard_map/scatter-add | solution.py:20
  46.5 2.6 %scatter_fusion.4 = f32[4,128,128]{2,1,0:T(8,128)S(1)} fusion(f32[4,128,128]{2,1,0:T(8,128)S(1)} %scatter_fusion.3, s32[16]{0:T(128)S(1)} %fusion.9, f32[16,128,128]{2,1,0:T(8,128)} %fusion.21), kind=kCustom, calls=%fused_computation.11 | custom fusion | flops 262144 | bytes 3145792 | tf_op jit(solution)/shard_map/scatter-add | solution.py:20
  49.1 2.6 %scatter_fusion.5 = f32[4,128,128]{2,1,0:T(8,128)S(1)} fusion(f32[4,128,128]{2,1,0:T(8,128)S(1)} %scatter_fusion.4, s32[16]{0:T(128)S(1)} %fusion.11, f32[16,128,128]{2,1,0:T(8,128)} %fusion.22), kind=kCustom, calls=%fused_computation.12 | custom fusion | flops 262144 | bytes 3145792 | tf_op jit(solution)/shard_map/scatter-add | solution.py:20
  51.7 2.6 %scatter_fusion.6 = f32[4,128,128]{2,1,0:T(8,128)S(1)} fusion(f32[4,128,128]{2,1,0:T(8,128)S(1)} %scatter_fusion.5, s32[16]{0:T(128)S(1)} %fusion.13, f32[16,128,128]{2,1,0:T(8,128)} %fusion.23), kind=kCustom, calls=%fused_computation.13 | custom fusion | flops 262144 | bytes 3145792 | tf_op jit(solution)/shard_map/scatter-add | solution.py:20
  54.3 2.6 %scatter_fusion.7 = f32[4,128,128]{2,1,0:T(8,128)S(1)} fusion(f32[4,128,128]{2,1,0:T(8,128)S(1)} %scatter_fusion.6, s32[16]{0:T(128)S(1)} %fusion.15, f32[16,128,128]{2,1,0:T(8,128)} %fusion.24), kind=kCustom, calls=%fused_computation.14 | custom fusion | flops 262144 | bytes 3145792 | tf_op jit(solution)/shard_map/scatter-add | solution.py:20
  57.7 21.8 %reduce-scatter.3.cloned.1.call-done = f32[1,128,128]{2,1,0:T(8,128)} async-done(((f32[4,128,128]{2,1,0:T(8,128)}), f32[1,128,128]{2,1,0:T(8,128)}) %reduce-scatter.3.cloned.1.call-update) | async-done | bytes 65552 | tf_op jit(solution)/shard_map/reduce_scatter | solution.py:68
  79.6 18.3 %all-reduce.3.cloned.1.call-done = f32[1,128,128]{2,1,0:T(8,128)} async-done(((f32[1,128,128]{2,1,0:T(8,128)}), f32[1,128,128]{2,1,0:T(8,128)}) %all-reduce.3.cloned.1.call-update) | async-done | bytes 65552 | tf_op jit(solution)/shard_map/psum | solution.py:69
  97.8 1.5 multiply_reduce_fusion
  99.4 22.2 %psum.22 = f32[]{:T(128)} all-reduce(f32[]{:T(128)} %multiply_reduce_fusion), channel_id=1, replica_groups=mesh['groups'=2,'left'=4,'right'=2,'mpo'=2] {'left','right'}, use_global_device_ids=true, to_apply=%region_13.14 | all-reduce | flops 1 | bytes 8 | tf_op jit(solution)/shard_map/psum | solution.py:73
  125.7 9.0 %all_to_all.15 = bf16[2,8,128,128]{3,2,1,0:T(8,128)(2,1)S(1)} all-to-all(bf16[2,8,128,128]{3,2,1,0:T(8,128)(2,1)S(1)} %scatter_fusion.8), channel_id=1, replica_groups=mesh['groups'=2,'left'=4,'right'=2,'mpo'=2] {'right'}, dimensions={0} | all-to-all | bytes 1048576 | tf_op jit(solution)/shard_map/all_to_all | solution.py:57
  141.3 2.6 %scatter_fusion.9 = f32[4,128,128]{2,1,0:T(8,128)S(1)} fusion(f32[4,128,128]{2,1,0:T(8,128)S(1)} %broadcast.92, s32[16]{0:T(128)S(1)} %fusion.5, f32[16,128,128]{2,1,0:T(8,128)} %fusion.25), kind=kCustom, calls=%fused_computation.16 | custom fusion | flops 262144 | bytes 3145792 | tf_op jit(solution)/shard_map/scatter-add | solution.py:20
  143.9 2.6 %scatter_fusion.10 = f32[4,128,128]{2,1,0:T(8,128)S(1)} fusion(f32[4,128,128]{2,1,0:T(8,128)S(1)} %scatter_fusion.9, s32[16]{0:T(128)S(1)} %fusion.7, f32[16,128,128]{2,1,0:T(8,128)} %fusion.26), kind=kCustom, calls=%fused_computation.17 | custom fusion | flops 262144 | bytes 3145792 | tf_op jit(solution)/shard_map/scatter-add | solution.py:20
  146.5 2.6 %scatter_fusion.11 = f32[4,128,128]{2,1,0:T(8,128)S(1)} fusion(f32[4,128,128]{2,1,0:T(8,128)S(1)} %scatter_fusion.10, s32[16]{0:T(128)S(1)} %fusion.9, f32[16,128,128]{2,1,0:T(8,128)} %fusion.27), kind=kCustom, calls=%fused_computation.18 | custom fusion | flops 262144 | bytes 3145792 | tf_op jit(solution)/shard_map/scatter-add | solution.py:20
  149.1 2.6 %scatter_fusion.12 = f32[4,128,128]{2,1,0:T(8,128)S(1)} fusion(f32[4,128,128]{2,1,0:T(8,128)S(1)} %scatter_fusion.11, s32[16]{0:T(128)S(1)} %fusion.11, f32[16,128,128]{2,1,0:T(8,128)} %fusion.28), kind=kCustom, calls=%fused_computation.19 | custom fusion | flops 262144 | bytes 3145792 | tf_op jit(solution)/shard_map/scatter-add | solution.py:20
  151.7 1.6 scatter_fusion.13
  153.3 1.6 scatter_fusion.14
  155.7 17.0 %reduce-scatter.5.cloned.1.call-done = f32[1,128,128]{2,1,0:T(8,128)} async-done(((f32[4,128,128]{2,1,0:T(8,128)}), f32[1,128,128]{2,1,0:T(8,128)}) %reduce-scatter.5.cloned.1.call-update) | async-done | bytes 65552 | tf_op jit(solution)/shard_map/reduce_scatter | solution.py:68
  172.7 18.1 %all-reduce.5.cloned.1.call-done = f32[1,128,128]{2,1,0:T(8,128)} async-done(((f32[1,128,128]{2,1,0:T(8,128)}), f32[1,128,128]{2,1,0:T(8,128)}) %all-reduce.5.cloned.1.call-update) | async-done | bytes 65552 | tf_op jit(solution)/shard_map/psum | solution.py:69
  (102 shorter events, 32.2 us)
Async XLA Ops:
  7.2 19.0 %copy-start = (bf16[2,16,128,128]{3,2,1,0:T(8,128)(2,1)S(1)}, bf16[2,16,128,128]{3,2,1,0:T(8,128)(2,1)}, u32[]{:S(2)}) copy-start(bf16[2,16,128,128]{3,2,1,0:T(8,128)(2,1)} %param.6) | copy-start | bytes 3145732
  11.4 10.1 %all-to-all-start = ((s32[2,8,13]{2,1,0:T(8,128)}), s32[2,8,13]{2,1,0:T(8,128)S(1)}, u32[]{:S(2)}, u32[]{:S(2)}) async-start(s32[2,8,13]{2,1,0:T(8,128)} %scatter_fusion), calls=%async_computation | async-start | bytes 16384 | tf_op jit(solution)/shard_map/all_to_all | solution.py:44
  15.6 1.9 copy-start.14
  21.4 12.0 %all-to-all-start.1 = ((bf16[2,8,128,128]{3,2,1,0:T(8,128)(2,1)}), bf16[2,8,128,128]{3,2,1,0:T(8,128)(2,1)S(1)}, u32[]{:S(2)}, u32[]{:S(2)}) async-start(bf16[2,8,128,128]{3,2,1,0:T(8,128)(2,1)} %scatter_fusion.1), calls=%async_computation.1 | async-start | bytes 1048576 | tf_op jit(solution)/shard_map/all_to_all | solution.py:57
  24.9 54.6 %reduce-scatter.3.cloned.1.call-start = ((), (), s32[]{:S(2)}) async-start(), calls=%async_computation.5 | async-start | bytes 327680 | tf_op jit(solution)/shard_map/reduce_scatter | solution.py:68
  34.7 1.3 copy-start.3
  36.0 1.3 copy-start.5
  37.3 1.3 copy-start.7
  38.6 1.3 copy-start.9
  56.9 0.7 copy-start.2
  57.6 40.2 %all-reduce.3.cloned.1.call-start = ((), (), s32[]{:S(2)}) async-start(), calls=%async_computation.6 | async-start | bytes 131072 | tf_op jit(solution)/shard_map/psum | solution.py:69
  79.5 93.2 %reduce-scatter.5.cloned.1.call-start = ((), (), s32[]{:S(2)}) async-start(), calls=%async_computation.7 | async-start | bytes 327680 | tf_op jit(solution)/shard_map/reduce_scatter | solution.py:68
  97.8 24.5 %copy-start.12 = (f32[1,128,128]{2,1,0:T(8,128)S(1)}, f32[1,128,128]{2,1,0:T(8,128)}, u32[]{:S(2)}) copy-start(f32[1,128,128]{2,1,0:T(8,128)} %all-reduce.3.cloned.1.call-done) | copy-start | bytes 196612
  123.4 1.0 copy-start.11
  136.0 1.3 copy-start.4
  137.4 1.3 copy-start.6
  138.6 1.3 copy-start.8
  139.9 1.0 copy-start.10
  154.9 0.7 copy-start.1
  155.6 35.2 %all-reduce.5.cloned.1.call-start = ((), (), s32[]{:S(2)}) async-start(), calls=%async_computation.8 | async-start | bytes 131072 | tf_op jit(solution)/shard_map/psum | solution.py:69
  190.8 0.9 copy-start.13
Sparse Core Ops, SparseCore 0:
  57.7 21.7 reduce-scatter.2
  81.9 15.9 all-reduce.2
  155.8 16.9 reduce-scatter.4
  174.9 15.8 all-reduce.4
where the time goes:
time: 200 us; the launch traced here: 199 us
  waiting for transfers between devices  75.4 us (38%)
  blocking collectives  31.2 us (16%)
  other arithmetic  31.1 us (16%)
  local copies, waits for them, and re-layouts  23.5 us (12%)
  matrix products  14.9 us (7%)
  between operations  14.8 us (7%)
  starting transfers between devices  7.86 us (4%)
    reduce_scatter x2, waiting for transfers between devices, combine(): own_tile = lax.psum_scatter(accum, 'left', scatter_dimension=0, tiled=True)  38.8 us
    psum x2, waiting for transfers between devices, combine(): summed = lax.psum(own_tile, 'mpo')  36.3 us
    scatter-add x12, other arithmetic, accumulate(): accum = accum.at[meta_rows[:, 1 + right_per + which]].add(products)  29.2 us
    psum x1, blocking collectives, local(): square_sum = lax.psum(jnp.sum(h_theta * h_theta), ('left', 'right'))  22.2 us
    dot_general x12, matrix products, accumulate(): jnp.einsum('sij,sjk->sik', inter_tiles, right_pick, preferred_element_typ...  13.5 us
    all_to_all x1, blocking collectives, apply_ham(): lax.all_to_all(buffer, 'right', split_axis=0, concat_axis=0, tiled=True)  8.99 us
    gather x6, local copies, waits for them, and re-layouts, accumulate(): right_pick = right_flat[meta_rows[:, 0] * rt_dev + meta_rows[:, 1 + which]]  6.97 us
    unnamed x46, local copies, waits for them, and re-layouts  6.4 us
  transfers between devices with their start and end apart: 6, of which 5 were waited for; matrix products, arithmetic and copies ran while one was open for 7% of the time, Pallas kernels for 0%

commit v1 on v0

v1 whole, which is shorter than its diff:
```python
import functools

import jax
import jax.numpy as jnp
from jax import lax
from jax.experimental import pallas as pl
from jax.experimental.pallas import tpu as pltpu
from jax.sharding import PartitionSpec as P

CAP = 8
VMEM = pl.BlockSpec(memory_space=pltpu.VMEM)
SMEM = pl.BlockSpec(memory_space=pltpu.SMEM)


def apply_entries(lists, vecs, left_ref, right_ref, acc, sel, rt_dev, lt_dev):
    me_left = lax.axis_index("left")
    me_right = lax.axis_index("right")
    rows, fields = lists[0].shape
    per = (fields - 2) // 2
    exact = CAP * len(lists) == rows
    acc[...] = jnp.zeros_like(acc)
    counts = []
    for q, terms in enumerate(lists):
        count = jnp.int32(0)
        for e in range(rows):
            sel[q, count] = jnp.int32(e)
            count = count + (terms[e, 1] == me_right).astype(jnp.int32)
        counts.append(count)

    def entry(q, n):
        terms = lists[q]
        e = sel[q, n]
        k = terms[e, 0]
        inter = jnp.dot(
            left_ref[k], vecs[q], preferred_element_type=jnp.float32
        ).astype(jnp.bfloat16)
        base = (k // lt_dev) * rt_dev
        for j in range(0, per, 2):
            pair = jnp.concatenate(
                [right_ref[base + terms[e, 2 + j]], right_ref[base + terms[e, 3 + j]]], axis=1
            )
            product = jnp.dot(inter, pair, preferred_element_type=jnp.float32)
            tile = product.shape[1] // 2
            for i in range(2):
                o = terms[e, 2 + per + j + i] ^ me_left
                acc[o] += product[:, i * tile:(i + 1) * tile]

    for q in range(len(lists)):
        if exact:
            for n in range(CAP):
                entry(q, n)
        else:
            pl.loop(0, counts[q])(functools.partial(entry, q))


def first_kernel(nr, nl, rt_dev, lt_dev, *refs):
    lists = refs[:nr]
    thetas = refs[nr:2 * nr]
    left_ref, right_ref = refs[2 * nr:2 * nr + 2]
    outs = refs[2 * nr + 2:2 * nr + 2 + nl]
    acc, sel = refs[2 * nr + 2 + nl:]
    vecs = [t[0] for t in thetas]
    apply_entries(lists, vecs, left_ref, right_ref, acc, sel, rt_dev, lt_dev)
    for s in range(nl):
        outs[s][...] = acc[s]


def second_kernel(nr, nl, rt_dev, lt_dev, count, *refs):
    lists = refs[:nr]
    tiles = refs[nr:2 * nr]
    sums = refs[2 * nr]
    left_ref, right_ref = refs[2 * nr + 1:2 * nr + 3]
    outs = refs[2 * nr + 3:2 * nr + 3 + nl]
    acc, sel = refs[2 * nr + 3 + nl:]
    square_sum = jnp.sum(sums[...], keepdims=True)
    scale = jnp.sqrt(square_sum / count + 1e-06)
    vecs = [(t[...] / scale).astype(jnp.bfloat16) for t in tiles]
    apply_entries(lists, vecs, left_ref, right_ref, acc, sel, rt_dev, lt_dev)
    for s in range(nl):
        outs[s][...] = acc[s]


def squares_kernel(*refs):
    out = refs[-1]
    total = None
    for ref in refs[:-1]:
        rows, tile = ref.shape
        square = ref[...] * ref[...]
        part = jnp.sum(square.reshape(rows // 8, 8, tile), axis=0)
        total = part if total is None else total + part
    out[...] = total


def swap(value, axis, offset):
    size = lax.axis_size(axis)
    return lax.ppermute(value, axis, [(i, i ^ offset) for i in range(size)])


def local(theta, left_env, right_env, terms):
    tile = theta.shape[-1]
    lt_dev = left_env.shape[1]
    rt_dev = right_env.shape[1]
    left_flat = left_env.reshape(-1, tile, tile)
    right_flat = right_env.reshape(-1, tile, tile)
    nl = lax.axis_size("left")
    nr = lax.axis_size("right")
    entries = terms[0, 0, 0]
    lists = [entries] + [swap(entries, "right", s) for s in range(1, nr)]
    thetas = [theta] + [swap(theta, "right", s) for s in range(1, nr)]
    flat = jax.ShapeDtypeStruct((tile, tile), jnp.float32)
    scratch = [pltpu.VMEM((nl, tile, tile), jnp.float32), pltpu.SMEM((nr, entries.shape[0] + 1), jnp.int32)]
    params = pltpu.CompilerParams(vmem_limit_bytes=32 << 20)

    def reduce_tiles(parts):
        own = parts[0]
        for s in range(1, nl):
            own = own + swap(parts[s], "left", s)
        return own + lax.ppermute(own, "mpo", [(0, 1), (1, 0)])

    parts = pl.pallas_call(
        functools.partial(first_kernel, nr, nl, rt_dev, lt_dev),
        out_shape=[flat] * nl,
        in_specs=[SMEM] * nr + [VMEM] * (nr + 2),
        out_specs=[VMEM] * nl,
        scratch_shapes=scratch,
        compiler_params=params,
        name="first_product",
    )(*lists, *thetas, left_flat, right_flat)
    h_theta = reduce_tiles(parts)

    tiles = [h_theta] + [swap(h_theta, "right", s) for s in range(1, nr)]
    squares = pl.pallas_call(
        squares_kernel,
        out_shape=jax.ShapeDtypeStruct((8, tile), jnp.float32),
        in_specs=[VMEM] * nr,
        out_specs=VMEM,
        name="squares",
    )(*tiles)
    sums = squares
    for s in range(1, nl):
        sums = sums + swap(squares, "left", s)

    parts = pl.pallas_call(
        functools.partial(second_kernel, nr, nl, rt_dev, lt_dev, nl * nr * tile * tile),
        out_shape=[flat] * nl,
        in_specs=[SMEM] * nr + [VMEM] * (nr + 3),
        out_specs=[VMEM] * nl,
        scratch_shapes=scratch,
        compiler_params=params,
        name="second_product",
    )(*lists, *tiles, sums, left_flat, right_flat)
    h_second = reduce_tiles(parts)
    return h_theta[None], h_second[None]


def solution(mesh):
    in_specs = (
        P(("groups", "left", "right"), None, None),
        P(("groups", "mpo"), "left", None, None),
        P(("groups", "mpo"), "right", None, None),
        P(("groups", "left"), "right", "mpo", None, None),
    )
    out_specs = (
        P(("groups", "left", "right"), None, None),
        P(("groups", "left", "right"), None, None),
    )
    return jax.shard_map(local, mesh=mesh, in_specs=in_specs, out_specs=out_specs, check_vma=False)
```

time: 200 us -> 57 us (0.28)
  waiting for transfers between devices: 75.4 us -> 22 us
  blocking collectives: 31.2 us -> 0 us
  other arithmetic: 31.1 us -> 1.36 us
  local copies, waits for them, and re-layouts: 23.5 us -> 6.29 us
  matrix products: 14.9 us -> 0 us
  between operations: 14.8 us -> 0.71 us
  starting transfers between devices: 7.86 us -> 17.1 us
  Pallas kernels: 0 us -> 9.03 us
    reduce_scatter x2 -> x0, waiting for transfers between devices: 38.8 us -> none  [combine(): own_tile = lax.psum_scatter(accum, 'left', scatter_dimension=0, tiled=True)]
    psum x2 -> x0, waiting for transfers between devices: 36.3 us -> none  [combine(): summed = lax.psum(own_tile, 'mpo')]
    scatter-add x12 -> x0, other arithmetic: 29.2 us -> none  [accumulate(): accum = accum.at[meta_rows[:, 1 + right_per + which]].add(products)]
    psum x1 -> x0, blocking collectives: 22.2 us -> none  [local(): square_sum = lax.psum(jnp.sum(h_theta * h_theta), ('left', 'right'))]
    ppermute x0 -> x14, waiting for transfers between devices: none -> 22 us  [the longest x12 19.5 us: swap(): return lax.ppermute(value, axis, [(i, i ^ offset) for i in range(size)])]
    ppermute x0 -> x14, starting transfers between devices: none -> 17.1 us  [the longest x12 17 us: swap(): return lax.ppermute(value, axis, [(i, i ^ offset) for i in range(size)])]
    dot_general x14 -> x0, matrix products: 14.9 us -> none  [the longest x12 13.5 us: accumulate(): jnp.einsum('sij,sjk->sik', inter_tiles, right_pick, preferred_element_typ...]
    pallas_call x0 -> x3, Pallas kernels: none -> 9.03 us  [the longest x1 3.81 us: local(): pl.pallas_call(functools.partial(second_kernel, nr, nl, rt_dev, lt_dev, n...]
  transfers between devices with their start and end apart: 6 -> 14, of which waited for: 5 -> 11; matrix products, arithmetic and copies ran while one was open for 7% -> 1% of each run, Pallas kernels for 0% -> 0%
where the time goes in v1:
time: 57 us; the launch traced here: 56.5 us
  waiting for transfers between devices  22 us (39%)
  starting transfers between devices  17.1 us (30%)
  Pallas kernels  9.03 us (16%)
  local copies, waits for them, and re-layouts  6.29 us (11%)
  other arithmetic  1.36 us (2%)
  between operations  0.71 us (1%)
    ppermute x12, waiting for transfers between devices, swap(): return lax.ppermute(value, axis, [(i, i ^ offset) for i in range(size)])  19.5 us
    ppermute x12, starting transfers between devices, swap(): return lax.ppermute(value, axis, [(i, i ^ offset) for i in range(size)])  17 us
    unnamed x19, local copies, waits for them, and re-layouts  6.29 us
    pallas_call x1, Pallas kernels, local(): pl.pallas_call(functools.partial(second_kernel, nr, nl, rt_dev, lt_dev, n...  3.81 us
    pallas_call x1, Pallas kernels, local(): pl.pallas_call(functools.partial(first_kernel, nr, nl, rt_dev, lt_dev), o...  3.74 us
    ppermute x2, waiting for transfers between devices, reduce_tiles(): return own + lax.ppermute(own, 'mpo', [(0, 1), (1, 0)])  2.48 us
    pallas_call x1, Pallas kernels, local(): pl.pallas_call(squares_kernel, out_shape=jax.ShapeDtypeStruct((8, tile),...  1.48 us
  transfers between devices with their start and end apart: 14, of which 11 were waited for; matrix products, arithmetic and copies ran while one was open for 1% of the time, Pallas kernels for 0%

profile of v1, /device:TPU:0, one launch (start us, length us, event | category | flops | bytes accessed | tf_op | source)
XLA Modules:
  0.0 56.5 jit_solution(15869999515475367718)
XLA Ops:
  0.6 3.0 %collective-permute-start.1 = (bf16[1,128,128]{2,1,0:T(8,128)(2,1)}, bf16[1,128,128]{2,1,0:T(8,128)(2,1)S(1)}, u32[]{:S(2)}, u32[]{:S(2)}) collective-permute-start(bf16[1,128,128]{2,1,0:T(8,128)(2,1)} %refs_2_.1), channel_id=1, source_target_pairs={{0,2},{2,0},{1,3},{3,1},{4,6},{6,4},{5,7},{7,5},{8,10},{10,8},{9,1... | collective-permute-start | bytes 98312 | tf_op jit(solution)/shard_map/ppermute | solution.py:96
  4.4 3.6 %collective-permute-done.refs_1_ = s32[16,14]{1,0:T(8,128)S(1)} collective-permute-done((s32[16,14]{1,0:T(8,128)S(1)}, s32[16,14]{1,0:T(8,128)S(1)}, u32[]{:S(2)}, u32[]{:S(2)}) %collective-permute-start) | collective-permute-done | bytes 928 | tf_op jit(solution)/shard_map/ppermute | solution.py:96
  8.1 1.2 %copy-done = bf16[2,16,128,128]{3,2,1,0:T(8,128)(2,1)S(1)} copy-done((bf16[2,16,128,128]{3,2,1,0:T(8,128)(2,1)S(1)}, bf16[2,16,128,128]{3,2,1,0:T(8,128)(2,1)}, u32[]{:S(2)}) %copy-start) | copy-done | bytes 1048600
  9.3 1.2 %copy-done.2 = bf16[2,16,128,128]{3,2,1,0:T(8,128)(2,1)S(1)} copy-done((bf16[2,16,128,128]{3,2,1,0:T(8,128)(2,1)S(1)}, bf16[2,16,128,128]{3,2,1,0:T(8,128)(2,1)}, u32[]{:S(2)}) %copy-start.2) | copy-done | bytes 1048600
  11.3 3.7 %first_product.1 = (f32[128,128]{1,0:T(8,128)S(1)}, f32[128,128]{1,0:T(8,128)S(1)}, f32[128,128]{1,0:T(8,128)S(1)}, f32[128,128]{1,0:T(8,128)S(1)}) custom-call(s32[16,14]{1,0:T(8,128)S(1)} %bitcast.12, s32[16,14]{1,0:T(8,128)S(1)} %collective-permute-done.refs_1_, bf16[1,128,128]{2,1,0:T(8,128)(2,1)S(1)} %copy-done.8, ...), custom_call_target="tpu_custom_call" | custom-call | tf_op jit(solution)/shard_map/first_product/pallas_call | solution.py:120
  15.0 1.6 %collective-permute-start.2 = (f32[128,128]{1,0:T(8,128)S(1)}, f32[128,128]{1,0:T(8,128)S(1)}, u32[]{:S(2)}, u32[]{:S(2)}) collective-permute-start(f32[128,128]{1,0:T(8,128)S(1)} %get-tuple-element.11), channel_id=1, source_target_pairs={{0,4},{4,0},{8,12},{12,8},{1,5},{5,1},{9,13},{13,9},{2,6},{6,2},{1... | collective-permute-start | bytes 196616 | tf_op jit(solution)/shard_map/ppermute | solution.py:96
  16.7 2.6 %collective-permute-start.3 = (f32[128,128]{1,0:T(8,128)S(1)}, f32[128,128]{1,0:T(8,128)S(1)}, u32[]{:S(2)}, u32[]{:S(2)}) collective-permute-start(f32[128,128]{1,0:T(8,128)S(1)} %get-tuple-element.12), channel_id=1, source_target_pairs={{0,8},{4,12},{8,0},{12,4},{1,9},{5,13},{9,1},{13,5},{2,10},{6,14},... | collective-permute-start | bytes 196616 | tf_op jit(solution)/shard_map/ppermute | solution.py:96
  19.6 3.6 %collective-permute-done.3 = f32[128,128]{1,0:T(8,128)S(1)} collective-permute-done((f32[128,128]{1,0:T(8,128)S(1)}, f32[128,128]{1,0:T(8,128)S(1)}, u32[]{:S(2)}, u32[]{:S(2)}) %collective-permute-start.3) | collective-permute-done | bytes 65568 | tf_op jit(solution)/shard_map/ppermute | solution.py:96
  23.2 2.1 %collective-permute-done.4 = f32[128,128]{1,0:T(8,128)S(1)} collective-permute-done((f32[128,128]{1,0:T(8,128)S(1)}, f32[128,128]{1,0:T(8,128)S(1)}, u32[]{:S(2)}, u32[]{:S(2)}) %collective-permute-start.4) | collective-permute-done | bytes 65568 | tf_op jit(solution)/shard_map/ppermute | solution.py:96
  25.4 1.2 %collective-permute-done.5 = f32[128,128]{1,0:T(8,128)S(1)} collective-permute-done((f32[128,128]{1,0:T(8,128)S(1)}, f32[128,128]{1,0:T(8,128)S(1)}, u32[]{:S(2)}, u32[]{:S(2)}) %collective-permute-start.5) | collective-permute-done | bytes 65568 | tf_op jit(solution)/shard_map/ppermute | solution.py:118
  27.3 3.7 %collective-permute-done.6.refs_1_.refs_3_ = f32[128,128]{1,0:T(8,128)S(1)} collective-permute-done((f32[128,128]{1,0:T(8,128)S(1)}, f32[128,128]{1,0:T(8,128)S(1)}, u32[]{:S(2)}, u32[]{:S(2)}) %collective-permute-start.6) | collective-permute-done | bytes 65568 | tf_op jit(solution)/shard_map/ppermute | solution.py:96
  31.6 1.5 %squares.1 = f32[8,128]{1,0:T(8,128)} custom-call(f32[128,128]{1,0:T(8,128)} %copy-done.4, f32[128,128]{1,0:T(8,128)} %copy-done.6), custom_call_target="tpu_custom_call" | custom-call | tf_op jit(solution)/shard_map/squares/pallas_call | solution.py:132
  33.1 0.8 %collective-permute-start.9 = (f32[8,128]{1,0:T(8,128)}, f32[8,128]{1,0:T(8,128)S(1)}, u32[]{:S(2)}, u32[]{:S(2)}) collective-permute-start(f32[8,128]{1,0:T(8,128)} %squares.1), channel_id=1, source_target_pairs={{0,12},{4,8},{8,4},{12,0},{1,13},{5,9},{9,5},{13,1},{2,14},{6,10},... | collective-permute-start | bytes 12296 | tf_op jit(solution)/shard_map/ppermute | solution.py:96
  33.9 3.6 %collective-permute-start.7 = (f32[8,128]{1,0:T(8,128)}, f32[8,128]{1,0:T(8,128)S(1)}, u32[]{:S(2)}, u32[]{:S(2)}) collective-permute-start(f32[8,128]{1,0:T(8,128)} %squares.1), channel_id=1, source_target_pairs={{0,4},{4,0},{8,12},{12,8},{1,5},{5,1},{9,13},{13,9},{2,6},{6,2},{1... | collective-permute-start | bytes 12296 | tf_op jit(solution)/shard_map/ppermute | solution.py:96
  37.5 1.2 %collective-permute-done.9 = f32[8,128]{1,0:T(8,128)S(1)} collective-permute-done((f32[8,128]{1,0:T(8,128)}, f32[8,128]{1,0:T(8,128)S(1)}, u32[]{:S(2)}, u32[]{:S(2)}) %collective-permute-start.9) | collective-permute-done | bytes 4128 | tf_op jit(solution)/shard_map/ppermute | solution.py:96
  40.0 0.8 %copy-done.5 = f32[128,128]{1,0:T(8,128)S(1)} copy-done((f32[128,128]{1,0:T(8,128)S(1)}, f32[128,128]{1,0:T(8,128)}, u32[]{:S(2)}) %copy-start.5) | copy-done | bytes 65560
  40.9 0.8 %copy-done.7 = f32[128,128]{1,0:T(8,128)S(1)} copy-done((f32[128,128]{1,0:T(8,128)S(1)}, f32[128,128]{1,0:T(8,128)}, u32[]{:S(2)}) %copy-start.7) | copy-done | bytes 65560
  41.7 3.8 %second_product.1 = (f32[128,128]{1,0:T(8,128)S(1)}, f32[128,128]{1,0:T(8,128)S(1)}, f32[128,128]{1,0:T(8,128)S(1)}, f32[128,128]{1,0:T(8,128)S(1)}) custom-call(s32[16,14]{1,0:T(8,128)S(1)} %bitcast.13, s32[16,14]{1,0:T(8,128)S(1)} %collective-permute-done.refs_1_, f32[128,128]{1,0:T(8,128)S(1)} %copy-done.5, f32[128,128]{1,0:T(8,128)S(1)} %copy-done.7, ...), custom_call_target="tpu_custom_call" | custom-call | tf_op jit(solution)/shard_map/second_product/pallas_call | solution.py:143
  45.5 2.1 %collective-permute-start.10 = (f32[128,128]{1,0:T(8,128)S(1)}, f32[128,128]{1,0:T(8,128)S(1)}, u32[]{:S(2)}, u32[]{:S(2)}) collective-permute-start(f32[128,128]{1,0:T(8,128)S(1)} %get-tuple-element.15), channel_id=1, source_target_pairs={{0,4},{4,0},{8,12},{12,8},{1,5},{5,1},{9,13},{13,9},{2,6},{6,2},{1... | collective-permute-start | bytes 196616 | tf_op jit(solution)/shard_map/ppermute | solution.py:96
  47.6 0.9 %collective-permute-start.11 = (f32[128,128]{1,0:T(8,128)S(1)}, f32[128,128]{1,0:T(8,128)S(1)}, u32[]{:S(2)}, u32[]{:S(2)}) collective-permute-start(f32[128,128]{1,0:T(8,128)S(1)} %get-tuple-element.16), channel_id=1, source_target_pairs={{0,8},{4,12},{8,0},{12,4},{1,9},{5,13},{9,1},{13,5},{2,10},{6,14},... | collective-permute-start | bytes 196616 | tf_op jit(solution)/shard_map/ppermute | solution.py:96
  48.5 1.6 %collective-permute-start.12 = (f32[128,128]{1,0:T(8,128)S(1)}, f32[128,128]{1,0:T(8,128)S(1)}, u32[]{:S(2)}, u32[]{:S(2)}) collective-permute-start(f32[128,128]{1,0:T(8,128)S(1)} %get-tuple-element.17), channel_id=1, source_target_pairs={{0,12},{4,8},{8,4},{12,0},{1,13},{5,9},{9,5},{13,1},{2,14},{6,10},... | collective-permute-start | bytes 196616 | tf_op jit(solution)/shard_map/ppermute | solution.py:96
  50.0 2.9 %collective-permute-done.11 = f32[128,128]{1,0:T(8,128)S(1)} collective-permute-done((f32[128,128]{1,0:T(8,128)S(1)}, f32[128,128]{1,0:T(8,128)S(1)}, u32[]{:S(2)}, u32[]{:S(2)}) %collective-permute-start.11) | collective-permute-done | bytes 65568 | tf_op jit(solution)/shard_map/ppermute | solution.py:96
  53.0 1.6 %collective-permute-done.12 = f32[128,128]{1,0:T(8,128)S(1)} collective-permute-done((f32[128,128]{1,0:T(8,128)S(1)}, f32[128,128]{1,0:T(8,128)S(1)}, u32[]{:S(2)}, u32[]{:S(2)}) %collective-permute-start.12) | collective-permute-done | bytes 65568 | tf_op jit(solution)/shard_map/ppermute | solution.py:96
  54.6 1.2 %collective-permute-done.13 = f32[128,128]{1,0:T(8,128)S(1)} collective-permute-done((f32[128,128]{1,0:T(8,128)S(1)}, f32[128,128]{1,0:T(8,128)S(1)}, u32[]{:S(2)}, u32[]{:S(2)}) %collective-permute-start.13) | collective-permute-done | bytes 65568 | tf_op jit(solution)/shard_map/ppermute | solution.py:118
  (31 shorter events, 5.3 us)
Async XLA Ops:
  0.6 7.4 %collective-permute-start.1 = (bf16[1,128,128]{2,1,0:T(8,128)(2,1)}, bf16[1,128,128]{2,1,0:T(8,128)(2,1)S(1)}, u32[]{:S(2)}, u32[]{:S(2)}) collective-permute-start(bf16[1,128,128]{2,1,0:T(8,128)(2,1)} %refs_2_.1), channel_id=1, source_target_pairs={{0,2},{2,0},{1,3},{3,1},{4,6},{6,4},{5,7},{7,5},{8,10},{10,8},{9,1... | collective-permute-start | bytes 98312 | tf_op jit(solution)/shard_map/ppermute | solution.py:96
  4.4 3.7 %collective-permute-start = (s32[16,14]{1,0:T(8,128)S(1)}, s32[16,14]{1,0:T(8,128)S(1)}, u32[]{:S(2)}, u32[]{:S(2)}) collective-permute-start(s32[16,14]{1,0:T(8,128)S(1)} %bitcast.11), channel_id=1, source_target_pairs={{0,2},{2,0},{1,3},{3,1},{4,6},{6,4},{5,7},{7,5},{8,10},{10,8},{9,1... | collective-permute-start | bytes 2696 | tf_op jit(solution)/shard_map/ppermute | solution.py:96
  8.1 1.2 %copy-start = (bf16[2,16,128,128]{3,2,1,0:T(8,128)(2,1)S(1)}, bf16[2,16,128,128]{3,2,1,0:T(8,128)(2,1)}, u32[]{:S(2)}) copy-start(bf16[2,16,128,128]{3,2,1,0:T(8,128)(2,1)} %param.5) | copy-start | bytes 3145732
  9.3 1.2 %copy-start.2 = (bf16[2,16,128,128]{3,2,1,0:T(8,128)(2,1)S(1)}, bf16[2,16,128,128]{3,2,1,0:T(8,128)(2,1)}, u32[]{:S(2)}) copy-start(bf16[2,16,128,128]{3,2,1,0:T(8,128)(2,1)} %param.6) | copy-start | bytes 3145732
  10.5 0.8 %copy-start.8 = (bf16[1,128,128]{2,1,0:T(8,128)(2,1)S(1)}, bf16[1,128,128]{2,1,0:T(8,128)(2,1)}, u32[]{:S(2)}) copy-start(bf16[1,128,128]{2,1,0:T(8,128)(2,1)} %refs_2_.1) | copy-start | bytes 98308
  11.3 28.7 %copy-start.1 = (bf16[2,16,128,128]{3,2,1,0:T(8,128)(2,1)S(1)}, bf16[2,16,128,128]{3,2,1,0:T(8,128)(2,1)}, u32[]{:S(2)}) copy-start(bf16[2,16,128,128]{3,2,1,0:T(8,128)(2,1)} %param.5) | copy-start | bytes 3145732
  11.3 28.7 %copy-start.3 = (bf16[2,16,128,128]{3,2,1,0:T(8,128)(2,1)S(1)}, bf16[2,16,128,128]{3,2,1,0:T(8,128)(2,1)}, u32[]{:S(2)}) copy-start(bf16[2,16,128,128]{3,2,1,0:T(8,128)(2,1)} %param.6) | copy-start | bytes 3145732
  15.0 4.6 %collective-permute-start.2 = (f32[128,128]{1,0:T(8,128)S(1)}, f32[128,128]{1,0:T(8,128)S(1)}, u32[]{:S(2)}, u32[]{:S(2)}) collective-permute-start(f32[128,128]{1,0:T(8,128)S(1)} %get-tuple-element.11), channel_id=1, source_target_pairs={{0,4},{4,0},{8,12},{12,8},{1,5},{5,1},{9,13},{13,9},{2,6},{6,2},{1... | collective-permute-start | bytes 196616 | tf_op jit(solution)/shard_map/ppermute | solution.py:96
  16.7 6.6 %collective-permute-start.3 = (f32[128,128]{1,0:T(8,128)S(1)}, f32[128,128]{1,0:T(8,128)S(1)}, u32[]{:S(2)}, u32[]{:S(2)}) collective-permute-start(f32[128,128]{1,0:T(8,128)S(1)} %get-tuple-element.12), channel_id=1, source_target_pairs={{0,8},{4,12},{8,0},{12,4},{1,9},{5,13},{9,1},{13,5},{2,10},{6,14},... | collective-permute-start | bytes 196616 | tf_op jit(solution)/shard_map/ppermute | solution.py:96
  19.2 6.1 %collective-permute-start.4 = (f32[128,128]{1,0:T(8,128)S(1)}, f32[128,128]{1,0:T(8,128)S(1)}, u32[]{:S(2)}, u32[]{:S(2)}) collective-permute-start(f32[128,128]{1,0:T(8,128)S(1)} %get-tuple-element.13), channel_id=1, source_target_pairs={{0,12},{4,8},{8,4},{12,0},{1,13},{5,9},{9,5},{13,1},{2,14},{6,10},... | collective-permute-start | bytes 196616 | tf_op jit(solution)/shard_map/ppermute | solution.py:96
  25.3 1.3 %collective-permute-start.5 = (f32[128,128]{1,0:T(8,128)S(1)}, f32[128,128]{1,0:T(8,128)S(1)}, u32[]{:S(2)}, u32[]{:S(2)}) collective-permute-start(f32[128,128]{1,0:T(8,128)S(1)} %add_add_fusion.1), channel_id=1, source_target_pairs={{0,1},{1,0},{2,3},{3,2},{4,5},{5,4},{6,7},{7,6},{8,9},{9,8},{10,11... | collective-permute-start | bytes 196616 | tf_op jit(solution)/shard_map/ppermute | solution.py:118
  26.7 4.3 %copy-start.4 = (f32[128,128]{1,0:T(8,128)}, f32[128,128]{1,0:T(8,128)S(1)}, u32[]{:S(2)}) copy-start(f32[128,128]{1,0:T(8,128)S(1)} %add.36.refs_0_.refs_2_) | copy-start | bytes 196612
  26.7 4.3 %collective-permute-start.6 = (f32[128,128]{1,0:T(8,128)S(1)}, f32[128,128]{1,0:T(8,128)S(1)}, u32[]{:S(2)}, u32[]{:S(2)}) collective-permute-start(f32[128,128]{1,0:T(8,128)S(1)} %add.36.refs_0_.refs_2_), channel_id=1, source_target_pairs={{0,2},{2,0},{1,3},{3,1},{4,6},{6,4},{5,7},{7,5},{8,10},{10,8},{9,1... | collective-permute-start | bytes 196616 | tf_op jit(solution)/shard_map/ppermute | solution.py:96
  31.0 0.6 %copy-start.6 = (f32[128,128]{1,0:T(8,128)}, f32[128,128]{1,0:T(8,128)S(1)}, u32[]{:S(2)}) copy-start(f32[128,128]{1,0:T(8,128)S(1)} %collective-permute-done.6.refs_1_.refs_3_) | copy-start | bytes 196612
  33.1 5.6 %collective-permute-start.9 = (f32[8,128]{1,0:T(8,128)}, f32[8,128]{1,0:T(8,128)S(1)}, u32[]{:S(2)}, u32[]{:S(2)}) collective-permute-start(f32[8,128]{1,0:T(8,128)} %squares.1), channel_id=1, source_target_pairs={{0,12},{4,8},{8,4},{12,0},{1,13},{5,9},{9,5},{13,1},{2,14},{6,10},... | collective-permute-start | bytes 12296 | tf_op jit(solution)/shard_map/ppermute | solution.py:96
  33.9 4.8 %collective-permute-start.8 = (f32[8,128]{1,0:T(8,128)}, f32[8,128]{1,0:T(8,128)S(1)}, u32[]{:S(2)}, u32[]{:S(2)}) collective-permute-start(f32[8,128]{1,0:T(8,128)} %squares.1), channel_id=1, source_target_pairs={{0,8},{4,12},{8,0},{12,4},{1,9},{5,13},{9,1},{13,5},{2,10},{6,14},... | collective-permute-start | bytes 12296 | tf_op jit(solution)/shard_map/ppermute | solution.py:96
  33.9 5.4 %collective-permute-start.7 = (f32[8,128]{1,0:T(8,128)}, f32[8,128]{1,0:T(8,128)S(1)}, u32[]{:S(2)}, u32[]{:S(2)}) collective-permute-start(f32[8,128]{1,0:T(8,128)} %squares.1), channel_id=1, source_target_pairs={{0,4},{4,0},{8,12},{12,8},{1,5},{5,1},{9,13},{13,9},{2,6},{6,2},{1... | collective-permute-start | bytes 12296 | tf_op jit(solution)/shard_map/ppermute | solution.py:96
  40.0 0.8 %copy-start.5 = (f32[128,128]{1,0:T(8,128)S(1)}, f32[128,128]{1,0:T(8,128)}, u32[]{:S(2)}) copy-start(f32[128,128]{1,0:T(8,128)} %copy-done.4) | copy-start | bytes 196612
  40.9 0.8 %copy-start.7 = (f32[128,128]{1,0:T(8,128)S(1)}, f32[128,128]{1,0:T(8,128)}, u32[]{:S(2)}) copy-start(f32[128,128]{1,0:T(8,128)} %copy-done.6) | copy-start | bytes 196612
  45.5 4.5 %collective-permute-start.10 = (f32[128,128]{1,0:T(8,128)S(1)}, f32[128,128]{1,0:T(8,128)S(1)}, u32[]{:S(2)}, u32[]{:S(2)}) collective-permute-start(f32[128,128]{1,0:T(8,128)S(1)} %get-tuple-element.15), channel_id=1, source_target_pairs={{0,4},{4,0},{8,12},{12,8},{1,5},{5,1},{9,13},{13,9},{2,6},{6,2},{1... | collective-permute-start | bytes 196616 | tf_op jit(solution)/shard_map/ppermute | solution.py:96
  47.6 5.4 %collective-permute-start.11 = (f32[128,128]{1,0:T(8,128)S(1)}, f32[128,128]{1,0:T(8,128)S(1)}, u32[]{:S(2)}, u32[]{:S(2)}) collective-permute-start(f32[128,128]{1,0:T(8,128)S(1)} %get-tuple-element.16), channel_id=1, source_target_pairs={{0,8},{4,12},{8,0},{12,4},{1,9},{5,13},{9,1},{13,5},{2,10},{6,14},... | collective-permute-start | bytes 196616 | tf_op jit(solution)/shard_map/ppermute | solution.py:96
  48.5 6.1 %collective-permute-start.12 = (f32[128,128]{1,0:T(8,128)S(1)}, f32[128,128]{1,0:T(8,128)S(1)}, u32[]{:S(2)}, u32[]{:S(2)}) collective-permute-start(f32[128,128]{1,0:T(8,128)S(1)} %get-tuple-element.17), channel_id=1, source_target_pairs={{0,12},{4,8},{8,4},{12,0},{1,13},{5,9},{9,5},{13,1},{2,14},{6,10},... | collective-permute-start | bytes 196616 | tf_op jit(solution)/shard_map/ppermute | solution.py:96
  54.6 1.3 %collective-permute-start.13 = (f32[128,128]{1,0:T(8,128)S(1)}, f32[128,128]{1,0:T(8,128)S(1)}, u32[]{:S(2)}, u32[]{:S(2)}) collective-permute-start(f32[128,128]{1,0:T(8,128)S(1)} %add_add_fusion), channel_id=1, source_target_pairs={{0,1},{1,0},{2,3},{3,2},{4,5},{5,4},{6,7},{7,6},{8,9},{9,8},{10,11... | collective-permute-start | bytes 196616 | tf_op jit(solution)/shard_map/ppermute | solution.py:118

commit v2 on v0

v2 whole, which is shorter than its diff:
```python
import functools

import jax
import jax.numpy as jnp
from jax import lax
from jax.experimental import pallas as pl
from jax.experimental.pallas import tpu as pltpu
from jax.sharding import PartitionSpec as P

CAP = 8
VMEM = pl.BlockSpec(memory_space=pltpu.VMEM)
HBM = pl.BlockSpec(memory_space=pltpu.HBM)
SMEM = pl.BlockSpec(memory_space=pltpu.SMEM)


def dot(a, b):
    return jnp.dot(a, b, preferred_element_type=jnp.float32)


def pick_entries(terms, sel):
    me_right = lax.axis_index("right")
    count = jnp.int32(0)
    for e in range(terms.shape[-1]):
        sel[count] = jnp.int32(e)
        count = count + (terms[1, 0, e] == me_right).astype(jnp.int32)
    return count


def apply_list(terms, sel, count, vec, left_ref, right_ref, acc, inter, dims):
    lt_dev, rt_dev, exact = dims
    me_left = lax.axis_index("left")
    fields, _, rows = terms.shape
    per = (fields - 2) // 2
    tile = vec.shape[-1]

    def spread(e, y):
        base = (terms[0, 0, e] // lt_dev) * rt_dev
        for j in range(per):
            product = dot(y, right_ref[base + terms[2 + j, 0, e]])
            acc[terms[2 + per + j, 0, e] ^ me_left] += product

    if exact:
        picks = jnp.concatenate([left_ref[terms[0, 0, sel[n]]] for n in range(CAP)], axis=0)
        inter[...] = dot(picks, vec).astype(jnp.bfloat16).reshape(CAP, tile, tile)
        for n in range(CAP):
            spread(sel[n], inter[n])
    else:

        def one(n):
            e = sel[n]
            spread(e, dot(left_ref[terms[0, 0, e]], vec).astype(jnp.bfloat16))

        pl.loop(0, count)(one)


def load_kernel(left_hbm, right_hbm, left_ref, right_ref, sems):
    copies = [
        pltpu.make_async_copy(left_hbm, left_ref, sems.at[0]),
        pltpu.make_async_copy(right_hbm, right_ref, sems.at[1]),
    ]
    for copy in copies:
        copy.start()
    for copy in copies:
        copy.wait()


def own_kernel(dims, terms, theta, left_ref, right_ref, out, sel, inter):
    out[...] = jnp.zeros_like(out)
    count = pick_entries(terms, sel)
    apply_list(terms, sel, count, theta[0], left_ref, right_ref, out, inter, dims)


def rest_kernel(dims, count, *refs):
    lists = refs[:count]
    thetas = refs[count:2 * count]
    left_ref, right_ref, start, out, sel, inter = refs[2 * count:]
    out[...] = start[...]
    for terms, theta in zip(lists, thetas):
        picked = pick_entries(terms, sel)
        apply_list(terms, sel, picked, theta[0], left_ref, right_ref, out, inter, dims)


def second_kernel(dims, nr, nl, chip_pair, elements, *refs):
    lists = refs[:nr]
    tiles = refs[nr:2 * nr]
    sums = refs[2 * nr:2 * nr + nl]
    left_ref, right_ref = refs[2 * nr + nl:2 * nr + nl + 2]
    outs = refs[2 * nr + nl + 2:-3]
    acc, sel, inter = refs[-3:]
    me = lax.axis_index("mpo")
    total = sums[0][...]
    for part in sums[1:]:
        total = total + part[...]
    scale = jnp.sqrt(jnp.sum(total, keepdims=True) / elements + 1e-06)
    values = [t[...] for t in tiles]
    if chip_pair:
        values = [jnp.where(me == 0, values[1 - i], values[i]) for i in range(2)]
    acc[...] = jnp.zeros_like(acc)
    for terms, value in zip(lists, values):
        vec = (value / scale).astype(jnp.bfloat16)
        picked = pick_entries(terms, sel)
        apply_list(terms, sel, picked, vec, left_ref, right_ref, acc, inter, dims)
    if nl == 4:
        own, keep, give = outs
        tile = own.shape[0]
        half = tile // 2
        own[...] = acc[0]
        keep[:tile] = acc[1 + me]
        keep[tile:] = acc[3, pl.ds(pl.multiple_of(half * me, half), half)]
        give[:tile] = acc[2 - me]
        give[tile:] = acc[3, pl.ds(pl.multiple_of(half - half * me, half), half)]
    else:
        for s in range(nl):
            outs[s][...] = acc[s]


def permute(value, target):
    nl, nr, nm = lax.axis_size("left"), lax.axis_size("right"), lax.axis_size("mpo")
    pairs = []
    for p in range(nl):
        for t in range(nr):
            for m in range(nm):
                to = target(p, t, m)
                pairs.append(((p * nr + t) * nm + m, (to[0] * nr + to[1]) * nm + to[2]))
    return lax.ppermute(value, ("left", "right", "mpo"), pairs)


def local(theta, left_env, right_env, terms):
    tile = theta.shape[-1]
    lt_dev = left_env.shape[1]
    rt_dev = right_env.shape[1]
    left_flat = left_env.reshape(-1, tile, tile)
    right_flat = right_env.reshape(-1, tile, tile)
    nl = lax.axis_size("left")
    nr = lax.axis_size("right")
    chip_pair = nr == 2
    rows, fields = terms.shape[-2:]
    entries = jnp.transpose(terms, (0, 1, 4, 2, 3)).reshape(fields, 1, rows)
    dims = (lt_dev, rt_dev, CAP * nr == rows)
    swap_cores = lambda x: permute(x, lambda p, t, m: (p, t, 1 - m))
    lists = [entries] + [permute(entries, lambda p, t, m, s=s: (p, t ^ s, m)) for s in range(1, nr)]
    thetas = [theta] + [permute(theta, lambda p, t, m, s=s: (p, t ^ s, 1 - m)) for s in range(1, nr)]
    stack = jax.ShapeDtypeStruct((nl, tile, tile), jnp.float32)
    scratch = [pltpu.SMEM((rows + 1,), jnp.int32), pltpu.VMEM((CAP, tile, tile), jnp.bfloat16)]
    params = pltpu.CompilerParams(vmem_limit_bytes=32 << 20)

    left_flat, right_flat = pl.pallas_call(
        load_kernel,
        out_shape=[jax.ShapeDtypeStruct(x.shape, x.dtype) for x in (left_flat, right_flat)],
        in_specs=[HBM] * 2,
        out_specs=[VMEM] * 2,
        scratch_shapes=[pltpu.SemaphoreType.DMA((2,))],
        compiler_params=pltpu.CompilerParams(vmem_limit_bytes=51 << 20),
        name="load",
    )(left_flat, right_flat)
    own_part = pl.pallas_call(
        functools.partial(own_kernel, dims),
        out_shape=stack,
        in_specs=[SMEM] + [VMEM] * 3,
        out_specs=VMEM,
        scratch_shapes=scratch,
        compiler_params=params,
        name="first_own",
    )(entries, theta, left_flat, right_flat)
    part = pl.pallas_call(
        functools.partial(rest_kernel, dims, nr - 1),
        out_shape=stack,
        in_specs=[SMEM] * (nr - 1) + [VMEM] * (nr + 2),
        out_specs=VMEM,
        scratch_shapes=scratch,
        compiler_params=params,
        name="first_rest",
    )(*lists[1:], *thetas[1:], left_flat, right_flat, own_part)

    chip = part + swap_cores(part)
    if chip_pair:
        mine = None
        for s in [*range(1, nl), 0]:
            got = permute(chip[s], lambda p, t, m: (p ^ s, t ^ m, 1 - m))
            mine = got if mine is None else mine + got
        other = swap_cores(mine)
        tiles = [mine, other]
        h_theta = jnp.where(lax.axis_index("mpo") == 1, mine, other)
    else:
        h_theta = chip[0]
        for s in range(1, nl):
            h_theta = h_theta + permute(chip[s], lambda p, t, m: (p ^ s, t, 1 - m))
        tiles = [h_theta]
        for s in range(1, nr):
            tiles.append(permute(h_theta, lambda p, t, m: (p, t ^ s, 1 - m)))
    squares = sum(jnp.sum((x * x).reshape(tile // 8, 8, tile), axis=0) for x in tiles)
    sums = [squares]
    for s in [2, 1, 3] if nl == 4 else range(1, nl):
        sums.append(permute(squares, lambda p, t, m: (p ^ s, t, 1 - m)))

    flat = lambda rows: jax.ShapeDtypeStruct((rows, tile), jnp.float32)
    out_shape = [flat(tile), flat(tile * 3 // 2), flat(tile * 3 // 2)] if nl == 4 else [flat(tile)] * nl
    parts = pl.pallas_call(
        functools.partial(second_kernel, dims, nr, nl, chip_pair, nl * nr * tile * tile),
        out_shape=out_shape,
        in_specs=[SMEM] * nr + [VMEM] * (nr + nl + 2),
        out_specs=[VMEM] * len(out_shape),
        scratch_shapes=[pltpu.VMEM((nl, tile, tile), jnp.float32)] + scratch,
        compiler_params=params,
        name="second_product",
    )(*lists, *tiles, *sums, left_flat, right_flat)
    half = parts[0]
    if nl == 4:
        _, keep, give = parts
        chip = keep + swap_cores(give)
        near = permute(chip[:tile], lambda p, t, m: (p ^ (1 + m), t, 1 - m))
        far = permute(chip[tile:], lambda p, t, m: (p ^ 3, t, 1 - m))
        first = lax.axis_index("mpo") == 1
        none = jnp.zeros_like(far)
        placed = jnp.concatenate([jnp.where(first, far, none), jnp.where(first, none, far)], axis=0)
        half = half + near + placed
    else:
        for s in range(1, nl):
            half = half + permute(parts[s], lambda p, t, m: (p ^ s, t, 1 - m))
    h_second = half + swap_cores(half)
    return h_theta[None], h_second[None]


def solution(mesh):
    in_specs = (
        P(("groups", "left", "right"), None, None),
        P(("groups", "mpo"), "left", None, None),
        P(("groups", "mpo"), "right", None, None),
        P(("groups", "left"), "right", "mpo", None, None),
    )
    out_specs = (
        P(("groups", "left", "right"), None, None),
        P(("groups", "left", "right"), None, None),
    )
    return jax.shard_map(local, mesh=mesh, in_specs=in_specs, out_specs=out_specs, check_vma=False)
```

time: 200 us -> 41.2 us (0.21)
  waiting for transfers between devices: 75.4 us -> 17 us
  blocking collectives: 31.2 us -> 0 us
  other arithmetic: 31.1 us -> 1.39 us
  local copies, waits for them, and re-layouts: 23.5 us -> 0.04 us
  matrix products: 14.9 us -> 0 us
  between operations: 14.8 us -> 0.75 us
  starting transfers between devices: 7.86 us -> 15.1 us
  Pallas kernels: 0 us -> 6.72 us
    reduce_scatter x2 -> x0, waiting for transfers between devices: 38.8 us -> none  [combine(): own_tile = lax.psum_scatter(accum, 'left', scatter_dimension=0, tiled=True)]
    psum x2 -> x0, waiting for transfers between devices: 36.3 us -> none  [combine(): summed = lax.psum(own_tile, 'mpo')]
    scatter-add x12 -> x0, other arithmetic: 29.2 us -> none  [accumulate(): accum = accum.at[meta_rows[:, 1 + right_per + which]].add(products)]
    psum x1 -> x0, blocking collectives: 22.2 us -> none  [local(): square_sum = lax.psum(jnp.sum(h_theta * h_theta), ('left', 'right'))]
    ppermute x0 -> x15, waiting for transfers between devices: none -> 17 us  [permute(): return lax.ppermute(value, ('left', 'right', 'mpo'), pairs)]
    ppermute x0 -> x15, starting transfers between devices: none -> 15.1 us  [permute(): return lax.ppermute(value, ('left', 'right', 'mpo'), pairs)]
    dot_general x14 -> x0, matrix products: 14.9 us -> none  [the longest x12 13.5 us: accumulate(): jnp.einsum('sij,sjk->sik', inter_tiles, right_pick, preferred_element_typ...]
    all_to_all x1 -> x0, blocking collectives: 8.99 us -> none  [apply_ham(): lax.all_to_all(buffer, 'right', split_axis=0, concat_axis=0, tiled=True)]
  transfers between devices with their start and end apart: 6 -> 15, of which waited for: 5 -> 12; matrix products, arithmetic and copies ran while one was open for 7% -> 2% of each run, Pallas kernels for 0% -> 7%
where the time goes in v2:
time: 41.2 us; the launch traced here: 41 us
  waiting for transfers between devices  17 us (41%)
  starting transfers between devices  15.1 us (37%)
  Pallas kernels  6.72 us (16%)
  other arithmetic  1.39 us (3%)
  between operations  0.75 us (2%)
    ppermute x15, waiting for transfers between devices, permute(): return lax.ppermute(value, ('left', 'right', 'mpo'), pairs)  17 us
    ppermute x15, starting transfers between devices, permute(): return lax.ppermute(value, ('left', 'right', 'mpo'), pairs)  15.1 us
    pallas_call x1, Pallas kernels, local(): pl.pallas_call(functools.partial(second_kernel, dims, nr, nl, chip_pair,...  2.24 us
    pallas_call x1, Pallas kernels, local(): pl.pallas_call(load_kernel, out_shape=[jax.ShapeDtypeStruct(x.shape, x.dt...  1.56 us
    pallas_call x1, Pallas kernels, local(): pl.pallas_call(functools.partial(own_kernel, dims), out_shape=stack, in_s...  1.46 us
    pallas_call x1, Pallas kernels, local(): pl.pallas_call(functools.partial(rest_kernel, dims, nr - 1), out_shape=st...  1.46 us
    broadcast_in_dim x2, other arithmetic, local(): return (h_theta[None], h_second[None])  1.28 us
  transfers between devices with their start and end apart: 15, of which 12 were waited for; matrix products, arithmetic and copies ran while one was open for 2% of the time, Pallas kernels for 7%

profile of v2, /device:TPU:0, one launch (start us, length us, event | category | flops | bytes accessed | tf_op | source)
XLA Modules:
  0.0 41.0 jit_solution(16912184930914301438)
XLA Ops:
  0.6 2.4 %collective-permute-start.1 = (bf16[1,128,128]{2,1,0:T(8,128)(2,1)}, bf16[1,128,128]{2,1,0:T(8,128)(2,1)S(1)}, u32[]{:S(2)}, u32[]{:S(2)}) collective-permute-start(bf16[1,128,128]{2,1,0:T(8,128)(2,1)} %theta.1), channel_id=1, source_target_pairs={{0,3},{1,2},{2,1},{3,0},{4,7},{5,6},{6,5},{7,4},{8,11},{9,10},{10,... | collective-permute-start | bytes 98312 | tf_op jit(solution)/shard_map/ppermute | solution.py:125
  3.1 0.6 %collective-permute-start = (s32[14,1,16]{2,1,0:T(1,128)}, s32[14,1,16]{2,1,0:T(1,128)S(1)}, u32[]{:S(2)}, u32[]{:S(2)}) collective-permute-start(s32[14,1,16]{2,1,0:T(1,128)} %bitcast.21), channel_id=1, source_target_pairs={{0,2},{1,3},{2,0},{3,1},{4,6},{5,7},{6,4},{7,5},{8,10},{9,11},{10,... | collective-permute-start | bytes 2696 | tf_op jit(solution)/shard_map/ppermute | solution.py:125
  3.7 1.6 %load.1 = (bf16[32,128,128]{2,1,0:T(8,128)(2,1)S(1)}, bf16[32,128,128]{2,1,0:T(8,128)(2,1)S(1)}) custom-call(bf16[32,128,128]{2,1,0:T(8,128)(2,1)} %bitcast.24, bf16[32,128,128]{2,1,0:T(8,128)(2,1)} %bitcast.25), custom_call_target="tpu_custom_call" | custom-call | tf_op jit(solution)/shard_map/load/pallas_call | solution.py:147
  5.3 1.5 %first_own.1.refs_4_ = f32[4,128,128]{2,1,0:T(8,128)S(1)} custom-call(s32[14,1,16]{2,1,0:T(1,128)S(1)} %bitcast.22, bf16[1,128,128]{2,1,0:T(8,128)(2,1)S(1)} %copy-done, bf16[32,128,128]{2,1,0:T(8,128)(2,1)S(1)} %get-tuple-element.7.left_ref.refs_2_.refs_8_, bf16[32,128,128]{2,1,0:T(8,128)(2,1)S(1)} %get-tuple-element.8.right_ref.refs_3_.refs_9_), custom_call_target="tpu_custom_call" | custom-call | tf_op jit(solution)/shard_map/first_own/pallas_call | solution.py:156
  6.9 1.5 %first_rest.1 = f32[4,128,128]{2,1,0:T(8,128)S(1)} custom-call(s32[14,1,16]{2,1,0:T(1,128)S(1)} %collective-permute-done.refs_0_.refs_1_, bf16[1,128,128]{2,1,0:T(8,128)(2,1)S(1)} %collective-permute-done.1.refs_1_, bf16[32,128,128]{2,1,0:T(8,128)(2,1)S(1)} %get-tuple-element.7.left_ref.refs_2_.refs_8_, ...), custom_call_target="tpu_custom_call" | custom-call | tf_op jit(solution)/shard_map/first_rest/pallas_call | solution.py:165
  8.5 1.5 %collective-permute-done.2 = f32[4,128,128]{2,1,0:T(8,128)S(1)} collective-permute-done((f32[4,128,128]{2,1,0:T(8,128)S(1)}, f32[4,128,128]{2,1,0:T(8,128)S(1)}, u32[]{:S(2)}, u32[]{:S(2)}) %collective-permute-start.2) | collective-permute-done | bytes 262176 | tf_op jit(solution)/shard_map/ppermute | solution.py:125
  10.1 1.4 %collective-permute-start.3 = (f32[128,128]{1,0:T(8,128)S(1)}, f32[128,128]{1,0:T(8,128)S(1)}, u32[]{:S(2)}, u32[]{:S(2)}) collective-permute-start(f32[128,128]{1,0:T(8,128)S(1)} %get-tuple-element.17), channel_id=1, source_target_pairs={{0,5},{1,6},{2,7},{3,4},{4,1},{5,2},{6,3},{7,0},{8,13},{9,14},{10,... | collective-permute-start | bytes 196616 | tf_op jit(solution)/shard_map/ppermute | solution.py:125
  11.4 3.3 %collective-permute-start.4 = (f32[128,128]{1,0:T(8,128)S(1)}, f32[128,128]{1,0:T(8,128)S(1)}, u32[]{:S(2)}, u32[]{:S(2)}) collective-permute-start(f32[128,128]{1,0:T(8,128)S(1)} %get-tuple-element.14), channel_id=1, source_target_pairs={{0,9},{1,10},{2,11},{3,8},{4,13},{5,14},{6,15},{7,12},{8,1},{9,2},... | collective-permute-start | bytes 196616 | tf_op jit(solution)/shard_map/ppermute | solution.py:125
  15.2 2.0 %collective-permute-done.4 = f32[128,128]{1,0:T(8,128)S(1)} collective-permute-done((f32[128,128]{1,0:T(8,128)S(1)}, f32[128,128]{1,0:T(8,128)S(1)}, u32[]{:S(2)}, u32[]{:S(2)}) %collective-permute-start.4) | collective-permute-done | bytes 65568 | tf_op jit(solution)/shard_map/ppermute | solution.py:125
  17.2 4.3 %collective-permute-done.5 = f32[128,128]{1,0:T(8,128)S(1)} collective-permute-done((f32[128,128]{1,0:T(8,128)S(1)}, f32[128,128]{1,0:T(8,128)S(1)}, u32[]{:S(2)}, u32[]{:S(2)}) %collective-permute-start.5) | collective-permute-done | bytes 65568 | tf_op jit(solution)/shard_map/ppermute | solution.py:125
  21.6 1.2 %collective-permute-done.7.refs_3_ = f32[128,128]{1,0:T(8,128)S(1)} collective-permute-done((f32[128,128]{1,0:T(8,128)S(1)}, f32[128,128]{1,0:T(8,128)S(1)}, u32[]{:S(2)}, u32[]{:S(2)}) %collective-permute-start.7) | collective-permute-done | bytes 65568 | tf_op jit(solution)/shard_map/ppermute | solution.py:125
  22.9 1.2 %collective-permute-start.10 = (f32[8,128]{1,0:T(8,128)S(1)}, f32[8,128]{1,0:T(8,128)S(1)}, u32[]{:S(2)}, u32[]{:S(2)}) collective-permute-start(f32[8,128]{1,0:T(8,128)S(1)} %add.31.refs_4_), channel_id=1, source_target_pairs={{0,13},{1,12},{2,15},{3,14},{4,9},{5,8},{6,11},{7,10},{8,5},{9,4},... | collective-permute-start | bytes 12296 | tf_op jit(solution)/shard_map/ppermute | solution.py:125
  24.1 0.9 %collective-permute-start.8 = (f32[8,128]{1,0:T(8,128)S(1)}, f32[8,128]{1,0:T(8,128)S(1)}, u32[]{:S(2)}, u32[]{:S(2)}) collective-permute-start(f32[8,128]{1,0:T(8,128)S(1)} %add.31.refs_4_), channel_id=1, source_target_pairs={{0,9},{1,8},{2,11},{3,10},{4,13},{5,12},{6,15},{7,14},{8,1},{9,0},... | collective-permute-start | bytes 12296 | tf_op jit(solution)/shard_map/ppermute | solution.py:125
  25.0 1.8 %collective-permute-start.9 = (f32[8,128]{1,0:T(8,128)S(1)}, f32[8,128]{1,0:T(8,128)S(1)}, u32[]{:S(2)}, u32[]{:S(2)}) collective-permute-start(f32[8,128]{1,0:T(8,128)S(1)} %add.31.refs_4_), channel_id=1, source_target_pairs={{0,5},{1,4},{2,7},{3,6},{4,1},{5,0},{6,3},{7,2},{8,13},{9,12},{10,... | collective-permute-start | bytes 12296 | tf_op jit(solution)/shard_map/ppermute | solution.py:125
  26.8 1.0 %collective-permute-done.10.refs_7_ = f32[8,128]{1,0:T(8,128)S(1)} collective-permute-done((f32[8,128]{1,0:T(8,128)S(1)}, f32[8,128]{1,0:T(8,128)S(1)}, u32[]{:S(2)}, u32[]{:S(2)}) %collective-permute-start.10) | collective-permute-done | bytes 4128 | tf_op jit(solution)/shard_map/ppermute | solution.py:125
  28.2 2.2 %second_product.1 = (f32[128,128]{1,0:T(8,128)S(1)}, f32[192,128]{1,0:T(8,128)S(1)}, f32[192,128]{1,0:T(8,128)S(1)}) custom-call(s32[14,1,16]{2,1,0:T(1,128)S(1)} %bitcast.23, s32[14,1,16]{2,1,0:T(1,128)S(1)} %collective-permute-done.refs_0_.refs_1_, f32[128,128]{1,0:T(8,128)S(1)} %get-tuple-element.13.refs_2_, ...), custom_call_target="tpu_custom_call" | custom-call | tf_op jit(solution)/shard_map/second_product/pallas_call | solution.py:198
  30.4 0.4 collective-permute-start.11
  30.8 1.0 %collective-permute-done.11 = f32[192,128]{1,0:T(8,128)S(1)} collective-permute-done((f32[192,128]{1,0:T(8,128)S(1)}, f32[192,128]{1,0:T(8,128)S(1)}, u32[]{:S(2)}, u32[]{:S(2)}) %collective-permute-start.11) | collective-permute-done | bytes 98336 | tf_op jit(solution)/shard_map/ppermute | solution.py:125
  31.8 2.3 %collective-permute-start.13 = (f32[64,128]{1,0:T(8,128)S(1)}, f32[64,128]{1,0:T(8,128)S(1)}, u32[]{:S(2)}, u32[]{:S(2)}) collective-permute-start(f32[64,128]{1,0:T(8,128)S(1)} %slice.29), channel_id=1, source_target_pairs={{0,13},{1,12},{2,15},{3,14},{4,9},{5,8},{6,11},{7,10},{8,5},{9,4},... | collective-permute-start | bytes 98312 | tf_op jit(solution)/shard_map/ppermute | solution.py:125
  34.2 3.0 %collective-permute-done.13 = f32[64,128]{1,0:T(8,128)S(1)} collective-permute-done((f32[64,128]{1,0:T(8,128)S(1)}, f32[64,128]{1,0:T(8,128)S(1)}, u32[]{:S(2)}, u32[]{:S(2)}) %collective-permute-start.13) | collective-permute-done | bytes 32800 | tf_op jit(solution)/shard_map/ppermute | solution.py:125
  37.1 1.9 %collective-permute-done.12 = f32[128,128]{1,0:T(8,128)S(1)} collective-permute-done((f32[128,128]{1,0:T(8,128)S(1)}, f32[128,128]{1,0:T(8,128)S(1)}, u32[]{:S(2)}, u32[]{:S(2)}) %collective-permute-start.12) | collective-permute-done | bytes 65568 | tf_op jit(solution)/shard_map/ppermute | solution.py:125
  39.2 0.6 %select_bitcast_fusion = f32[1,128,128]{2,1,0:T(8,128)} fusion(f32[128,128]{1,0:T(8,128)S(1)} %get-tuple-element.13.refs_2_, f32[128,128]{1,0:T(8,128)S(1)} %collective-permute-done.7.refs_3_, pred[]{:T(512)S(6)} %eq.4), kind=kLoop, calls=%fused_computation.8 | loop fusion | flops 16384 | bytes 196609 | tf_op jit(solution)/shard_map/broadcast_in_dim | solution.py:221
  39.8 0.6 %collective-permute-done.14 = f32[128,128]{1,0:T(8,128)S(1)} collective-permute-done((f32[128,128]{1,0:T(8,128)S(1)}, f32[128,128]{1,0:T(8,128)S(1)}, u32[]{:S(2)}, u32[]{:S(2)}) %collective-permute-start.14) | collective-permute-done | bytes 65568 | tf_op jit(solution)/shard_map/ppermute | solution.py:125
  40.4 0.6 %add_bitcast_fusion = f32[1,128,128]{2,1,0:T(8,128)} fusion(f32[128,128]{1,0:T(8,128)S(1)} %maximum_add_fusion, f32[128,128]{1,0:T(8,128)S(1)} %collective-permute-done.14), kind=kLoop, calls=%fused_computation.7 | loop fusion | flops 16384 | bytes 196608 | tf_op jit(solution)/shard_map/broadcast_in_dim | solution.py:221
  (26 shorter events, 1.4 us)
Async XLA Ops:
  0.6 6.3 %collective-permute-start.1 = (bf16[1,128,128]{2,1,0:T(8,128)(2,1)}, bf16[1,128,128]{2,1,0:T(8,128)(2,1)S(1)}, u32[]{:S(2)}, u32[]{:S(2)}) collective-permute-start(bf16[1,128,128]{2,1,0:T(8,128)(2,1)} %theta.1), channel_id=1, source_target_pairs={{0,3},{1,2},{2,1},{3,0},{4,7},{5,6},{6,5},{7,4},{8,11},{9,10},{10,... | collective-permute-start | bytes 98312 | tf_op jit(solution)/shard_map/ppermute | solution.py:125
  3.1 3.9 %collective-permute-start = (s32[14,1,16]{2,1,0:T(1,128)}, s32[14,1,16]{2,1,0:T(1,128)S(1)}, u32[]{:S(2)}, u32[]{:S(2)}) collective-permute-start(s32[14,1,16]{2,1,0:T(1,128)} %bitcast.21), channel_id=1, source_target_pairs={{0,2},{1,3},{2,0},{3,1},{4,6},{5,7},{6,4},{7,5},{8,10},{9,11},{10,... | collective-permute-start | bytes 2696 | tf_op jit(solution)/shard_map/ppermute | solution.py:125
  3.7 1.6 %copy-start = (bf16[1,128,128]{2,1,0:T(8,128)(2,1)S(1)}, bf16[1,128,128]{2,1,0:T(8,128)(2,1)}, u32[]{:S(2)}) copy-start(bf16[1,128,128]{2,1,0:T(8,128)(2,1)} %theta.1) | copy-start | bytes 98308
  3.7 1.6 %copy-start.1 = (s32[1,1,1,16,14]{3,2,4,1,0:T(1,128)S(1)}, s32[1,1,1,16,14]{3,2,4,1,0:T(1,128)}, u32[]{:S(2)}) copy-start(s32[1,1,1,16,14]{3,2,4,1,0:T(1,128)} %param.7) | copy-start | bytes 2692
  8.4 1.6 %collective-permute-start.2 = (f32[4,128,128]{2,1,0:T(8,128)S(1)}, f32[4,128,128]{2,1,0:T(8,128)S(1)}, u32[]{:S(2)}, u32[]{:S(2)}) collective-permute-start(f32[4,128,128]{2,1,0:T(8,128)S(1)} %first_rest.1), channel_id=1, source_target_pairs={{0,1},{1,0},{2,3},{3,2},{4,5},{5,4},{6,7},{7,6},{8,9},{9,8},{10,11... | collective-permute-start | bytes 786440 | tf_op jit(solution)/shard_map/ppermute | solution.py:125
  10.1 5.2 %collective-permute-start.3 = (f32[128,128]{1,0:T(8,128)S(1)}, f32[128,128]{1,0:T(8,128)S(1)}, u32[]{:S(2)}, u32[]{:S(2)}) collective-permute-start(f32[128,128]{1,0:T(8,128)S(1)} %get-tuple-element.17), channel_id=1, source_target_pairs={{0,5},{1,6},{2,7},{3,4},{4,1},{5,2},{6,3},{7,0},{8,13},{9,14},{10,... | collective-permute-start | bytes 196616 | tf_op jit(solution)/shard_map/ppermute | solution.py:125
  11.4 5.8 %collective-permute-start.4 = (f32[128,128]{1,0:T(8,128)S(1)}, f32[128,128]{1,0:T(8,128)S(1)}, u32[]{:S(2)}, u32[]{:S(2)}) collective-permute-start(f32[128,128]{1,0:T(8,128)S(1)} %get-tuple-element.14), channel_id=1, source_target_pairs={{0,9},{1,10},{2,11},{3,8},{4,13},{5,14},{6,15},{7,12},{8,1},{9,2},... | collective-permute-start | bytes 196616 | tf_op jit(solution)/shard_map/ppermute | solution.py:125
  14.7 6.8 %collective-permute-start.5 = (f32[128,128]{1,0:T(8,128)S(1)}, f32[128,128]{1,0:T(8,128)S(1)}, u32[]{:S(2)}, u32[]{:S(2)}) collective-permute-start(f32[128,128]{1,0:T(8,128)S(1)} %get-tuple-element.16), channel_id=1, source_target_pairs={{0,13},{1,14},{2,15},{3,12},{4,9},{5,10},{6,11},{7,8},{8,5},{9,6},... | collective-permute-start | bytes 196616 | tf_op jit(solution)/shard_map/ppermute | solution.py:125
  14.9 6.6 %collective-permute-start.6 = (f32[128,128]{1,0:T(8,128)S(1)}, f32[128,128]{1,0:T(8,128)S(1)}, u32[]{:S(2)}, u32[]{:S(2)}) collective-permute-start(f32[128,128]{1,0:T(8,128)S(1)} %get-tuple-element.15), channel_id=1, source_target_pairs={{0,1},{1,2},{2,3},{3,0},{4,5},{5,6},{6,7},{7,4},{8,9},{9,10},{10,1... | collective-permute-start | bytes 196616 | tf_op jit(solution)/shard_map/ppermute | solution.py:125
  21.6 1.3 %collective-permute-start.7 = (f32[128,128]{1,0:T(8,128)S(1)}, f32[128,128]{1,0:T(8,128)S(1)}, u32[]{:S(2)}, u32[]{:S(2)}) collective-permute-start(f32[128,128]{1,0:T(8,128)S(1)} %get-tuple-element.13.refs_2_), channel_id=1, source_target_pairs={{0,1},{1,0},{2,3},{3,2},{4,5},{5,4},{6,7},{7,6},{8,9},{9,8},{10,11... | collective-permute-start | bytes 196616 | tf_op jit(solution)/shard_map/ppermute | solution.py:125
  22.9 4.9 %collective-permute-start.10 = (f32[8,128]{1,0:T(8,128)S(1)}, f32[8,128]{1,0:T(8,128)S(1)}, u32[]{:S(2)}, u32[]{:S(2)}) collective-permute-start(f32[8,128]{1,0:T(8,128)S(1)} %add.31.refs_4_), channel_id=1, source_target_pairs={{0,13},{1,12},{2,15},{3,14},{4,9},{5,8},{6,11},{7,10},{8,5},{9,4},... | collective-permute-start | bytes 12296 | tf_op jit(solution)/shard_map/ppermute | solution.py:125
  24.1 3.9 %collective-permute-start.8 = (f32[8,128]{1,0:T(8,128)S(1)}, f32[8,128]{1,0:T(8,128)S(1)}, u32[]{:S(2)}, u32[]{:S(2)}) collective-permute-start(f32[8,128]{1,0:T(8,128)S(1)} %add.31.refs_4_), channel_id=1, source_target_pairs={{0,9},{1,8},{2,11},{3,10},{4,13},{5,12},{6,15},{7,14},{8,1},{9,0},... | collective-permute-start | bytes 12296 | tf_op jit(solution)/shard_map/ppermute | solution.py:125
  25.0 3.2 %collective-permute-start.9 = (f32[8,128]{1,0:T(8,128)S(1)}, f32[8,128]{1,0:T(8,128)S(1)}, u32[]{:S(2)}, u32[]{:S(2)}) collective-permute-start(f32[8,128]{1,0:T(8,128)S(1)} %add.31.refs_4_), channel_id=1, source_target_pairs={{0,5},{1,4},{2,7},{3,6},{4,1},{5,0},{6,3},{7,2},{8,13},{9,12},{10,... | collective-permute-start | bytes 12296 | tf_op jit(solution)/shard_map/ppermute | solution.py:125
  30.4 1.4 %collective-permute-start.11 = (f32[192,128]{1,0:T(8,128)S(1)}, f32[192,128]{1,0:T(8,128)S(1)}, u32[]{:S(2)}, u32[]{:S(2)}) collective-permute-start(f32[192,128]{1,0:T(8,128)S(1)} %get-tuple-element.11), channel_id=1, source_target_pairs={{0,1},{1,0},{2,3},{3,2},{4,5},{5,4},{6,7},{7,6},{8,9},{9,8},{10,11... | collective-permute-start | bytes 294920 | tf_op jit(solution)/shard_map/ppermute | solution.py:125
  31.8 5.3 %collective-permute-start.13 = (f32[64,128]{1,0:T(8,128)S(1)}, f32[64,128]{1,0:T(8,128)S(1)}, u32[]{:S(2)}, u32[]{:S(2)}) collective-permute-start(f32[64,128]{1,0:T(8,128)S(1)} %slice.29), channel_id=1, source_target_pairs={{0,13},{1,12},{2,15},{3,14},{4,9},{5,8},{6,11},{7,10},{8,5},{9,4},... | collective-permute-start | bytes 98312 | tf_op jit(solution)/shard_map/ppermute | solution.py:125
  34.2 4.9 %collective-permute-start.12 = (f32[128,128]{1,0:T(8,128)S(1)}, f32[128,128]{1,0:T(8,128)S(1)}, u32[]{:S(2)}, u32[]{:S(2)}) collective-permute-start(f32[128,128]{1,0:T(8,128)S(1)} %slice.28), channel_id=1, source_target_pairs={{0,5},{1,8},{2,7},{3,10},{4,1},{5,12},{6,3},{7,14},{8,13},{9,0},{1... | collective-permute-start | bytes 196616 | tf_op jit(solution)/shard_map/ppermute | solution.py:125
  39.1 1.3 %collective-permute-start.14 = (f32[128,128]{1,0:T(8,128)S(1)}, f32[128,128]{1,0:T(8,128)S(1)}, u32[]{:S(2)}, u32[]{:S(2)}) collective-permute-start(f32[128,128]{1,0:T(8,128)S(1)} %maximum_add_fusion), channel_id=1, source_target_pairs={{0,1},{1,0},{2,3},{3,2},{4,5},{5,4},{6,7},{7,6},{8,9},{9,8},{10,11... | collective-permute-start | bytes 196616 | tf_op jit(solution)/shard_map/ppermute | solution.py:125

commit v3 on v2

--- a/solution.py
+++ b/solution.py
@@ -175,7 +175,7 @@
     chip = part + swap_cores(part)
     if chip_pair:
         mine = None
-        for s in [*range(1, nl), 0]:
+        for s in [3, 1, 2, 0] if nl == 4 else range(nl):
             got = permute(chip[s], lambda p, t, m: (p ^ s, t ^ m, 1 - m))
             mine = got if mine is None else mine + got
         other = swap_cores(mine)

time: 41.2 us -> 40.6 us (0.985)
  waiting for transfers between devices: 17 us -> 15.9 us
  starting transfers between devices: 15.1 us -> 15.7 us
    ppermute x15, waiting for transfers between devices: 17 us -> 15.9 us  [permute(): return lax.ppermute(value, ('left', 'right', 'mpo'), pairs)]
    ppermute x15, starting transfers between devices: 15.1 us -> 15.7 us  [permute(): return lax.ppermute(value, ('left', 'right', 'mpo'), pairs)]
where the time goes in v3:
time: 40.6 us; the launch traced here: 40.4 us
  waiting for transfers between devices  15.9 us (39%)
  starting transfers between devices  15.7 us (39%)
  Pallas kernels  6.72 us (17%)
  other arithmetic  1.39 us (3%)
  between operations  0.74 us (2%)
    ppermute x15, waiting for transfers between devices, permute(): return lax.ppermute(value, ('left', 'right', 'mpo'), pairs)  15.9 us
    ppermute x15, starting transfers between devices, permute(): return lax.ppermute(value, ('left', 'right', 'mpo'), pairs)  15.7 us
    pallas_call x1, Pallas kernels, local(): pl.pallas_call(functools.partial(second_kernel, dims, nr, nl, chip_pair,...  2.24 us
    pallas_call x1, Pallas kernels, local(): pl.pallas_call(load_kernel, out_shape=[jax.ShapeDtypeStruct(x.shape, x.dt...  1.56 us
    pallas_call x1, Pallas kernels, local(): pl.pallas_call(functools.partial(own_kernel, dims), out_shape=stack, in_s...  1.46 us
    pallas_call x1, Pallas kernels, local(): pl.pallas_call(functools.partial(rest_kernel, dims, nr - 1), out_shape=st...  1.46 us
    broadcast_in_dim x2, other arithmetic, local(): return (h_theta[None], h_second[None])  1.28 us
  transfers between devices with their start and end apart: 15, of which 12 were waited for; matrix products, arithmetic and copies ran while one was open for 2% of the time, Pallas kernels for 7%

profile of v3, /device:TPU:0, one launch (start us, length us, event | category | flops | bytes accessed | tf_op | source)
XLA Modules:
  0.0 40.4 jit_solution(15597137291934447275)
XLA Ops:
  0.6 2.4 %collective-permute-start.1 = (bf16[1,128,128]{2,1,0:T(8,128)(2,1)}, bf16[1,128,128]{2,1,0:T(8,128)(2,1)S(1)}, u32[]{:S(2)}, u32[]{:S(2)}) collective-permute-start(bf16[1,128,128]{2,1,0:T(8,128)(2,1)} %theta.1), channel_id=1, source_target_pairs={{0,3},{1,2},{2,1},{3,0},{4,7},{5,6},{6,5},{7,4},{8,11},{9,10},{10,... | collective-permute-start | bytes 98312 | tf_op jit(solution)/shard_map/ppermute | solution.py:125
  3.1 0.6 %collective-permute-start = (s32[14,1,16]{2,1,0:T(1,128)}, s32[14,1,16]{2,1,0:T(1,128)S(1)}, u32[]{:S(2)}, u32[]{:S(2)}) collective-permute-start(s32[14,1,16]{2,1,0:T(1,128)} %bitcast.21), channel_id=1, source_target_pairs={{0,2},{1,3},{2,0},{3,1},{4,6},{5,7},{6,4},{7,5},{8,10},{9,11},{10,... | collective-permute-start | bytes 2696 | tf_op jit(solution)/shard_map/ppermute | solution.py:125
  3.7 1.6 %load.1 = (bf16[32,128,128]{2,1,0:T(8,128)(2,1)S(1)}, bf16[32,128,128]{2,1,0:T(8,128)(2,1)S(1)}) custom-call(bf16[32,128,128]{2,1,0:T(8,128)(2,1)} %bitcast.24, bf16[32,128,128]{2,1,0:T(8,128)(2,1)} %bitcast.25), custom_call_target="tpu_custom_call" | custom-call | tf_op jit(solution)/shard_map/load/pallas_call | solution.py:147
  5.3 1.5 %first_own.1.refs_4_ = f32[4,128,128]{2,1,0:T(8,128)S(1)} custom-call(s32[14,1,16]{2,1,0:T(1,128)S(1)} %bitcast.22, bf16[1,128,128]{2,1,0:T(8,128)(2,1)S(1)} %copy-done, bf16[32,128,128]{2,1,0:T(8,128)(2,1)S(1)} %get-tuple-element.7.left_ref.refs_2_.refs_8_, bf16[32,128,128]{2,1,0:T(8,128)(2,1)S(1)} %get-tuple-element.8.right_ref.refs_3_.refs_9_), custom_call_target="tpu_custom_call" | custom-call | tf_op jit(solution)/shard_map/first_own/pallas_call | solution.py:156
  6.9 1.5 %first_rest.1 = f32[4,128,128]{2,1,0:T(8,128)S(1)} custom-call(s32[14,1,16]{2,1,0:T(1,128)S(1)} %collective-permute-done.refs_0_.refs_1_, bf16[1,128,128]{2,1,0:T(8,128)(2,1)S(1)} %collective-permute-done.1.refs_1_, bf16[32,128,128]{2,1,0:T(8,128)(2,1)S(1)} %get-tuple-element.7.left_ref.refs_2_.refs_8_, ...), custom_call_target="tpu_custom_call" | custom-call | tf_op jit(solution)/shard_map/first_rest/pallas_call | solution.py:165
  8.5 1.5 %collective-permute-done.2 = f32[4,128,128]{2,1,0:T(8,128)S(1)} collective-permute-done((f32[4,128,128]{2,1,0:T(8,128)S(1)}, f32[4,128,128]{2,1,0:T(8,128)S(1)}, u32[]{:S(2)}, u32[]{:S(2)}) %collective-permute-start.2) | collective-permute-done | bytes 262176 | tf_op jit(solution)/shard_map/ppermute | solution.py:125
  10.1 3.4 %collective-permute-start.3 = (f32[128,128]{1,0:T(8,128)S(1)}, f32[128,128]{1,0:T(8,128)S(1)}, u32[]{:S(2)}, u32[]{:S(2)}) collective-permute-start(f32[128,128]{1,0:T(8,128)S(1)} %get-tuple-element.17), channel_id=1, source_target_pairs={{0,13},{1,14},{2,15},{3,12},{4,9},{5,10},{6,11},{7,8},{8,5},{9,6},... | collective-permute-start | bytes 196616 | tf_op jit(solution)/shard_map/ppermute | solution.py:125
  13.7 1.2 %collective-permute-start.5 = (f32[128,128]{1,0:T(8,128)S(1)}, f32[128,128]{1,0:T(8,128)S(1)}, u32[]{:S(2)}, u32[]{:S(2)}) collective-permute-start(f32[128,128]{1,0:T(8,128)S(1)} %get-tuple-element.16), channel_id=1, source_target_pairs={{0,9},{1,10},{2,11},{3,8},{4,13},{5,14},{6,15},{7,12},{8,1},{9,2},... | collective-permute-start | bytes 196616 | tf_op jit(solution)/shard_map/ppermute | solution.py:125
  15.2 1.8 %collective-permute-done.3 = f32[128,128]{1,0:T(8,128)S(1)} collective-permute-done((f32[128,128]{1,0:T(8,128)S(1)}, f32[128,128]{1,0:T(8,128)S(1)}, u32[]{:S(2)}, u32[]{:S(2)}) %collective-permute-start.3) | collective-permute-done | bytes 65568 | tf_op jit(solution)/shard_map/ppermute | solution.py:125
  17.0 1.4 %collective-permute-done.4 = f32[128,128]{1,0:T(8,128)S(1)} collective-permute-done((f32[128,128]{1,0:T(8,128)S(1)}, f32[128,128]{1,0:T(8,128)S(1)}, u32[]{:S(2)}, u32[]{:S(2)}) %collective-permute-start.4) | collective-permute-done | bytes 65568 | tf_op jit(solution)/shard_map/ppermute | solution.py:125
  18.5 1.2 %collective-permute-done.5 = f32[128,128]{1,0:T(8,128)S(1)} collective-permute-done((f32[128,128]{1,0:T(8,128)S(1)}, f32[128,128]{1,0:T(8,128)S(1)}, u32[]{:S(2)}, u32[]{:S(2)}) %collective-permute-start.5) | collective-permute-done | bytes 65568 | tf_op jit(solution)/shard_map/ppermute | solution.py:125
  20.1 0.9 %collective-permute-done.7.refs_3_ = f32[128,128]{1,0:T(8,128)S(1)} collective-permute-done((f32[128,128]{1,0:T(8,128)S(1)}, f32[128,128]{1,0:T(8,128)S(1)}, u32[]{:S(2)}, u32[]{:S(2)}) %collective-permute-start.7) | collective-permute-done | bytes 65568 | tf_op jit(solution)/shard_map/ppermute | solution.py:125
  21.0 2.7 %collective-permute-start.10 = (f32[8,128]{1,0:T(8,128)S(1)}, f32[8,128]{1,0:T(8,128)S(1)}, u32[]{:S(2)}, u32[]{:S(2)}) collective-permute-start(f32[8,128]{1,0:T(8,128)S(1)} %add.31.refs_4_), channel_id=1, source_target_pairs={{0,13},{1,12},{2,15},{3,14},{4,9},{5,8},{6,11},{7,10},{8,5},{9,4},... | collective-permute-start | bytes 12296 | tf_op jit(solution)/shard_map/ppermute | solution.py:125
  23.7 0.9 %collective-permute-start.8 = (f32[8,128]{1,0:T(8,128)S(1)}, f32[8,128]{1,0:T(8,128)S(1)}, u32[]{:S(2)}, u32[]{:S(2)}) collective-permute-start(f32[8,128]{1,0:T(8,128)S(1)} %add.31.refs_4_), channel_id=1, source_target_pairs={{0,9},{1,8},{2,11},{3,10},{4,13},{5,12},{6,15},{7,14},{8,1},{9,0},... | collective-permute-start | bytes 12296 | tf_op jit(solution)/shard_map/ppermute | solution.py:125
  25.2 0.8 %collective-permute-done.10.refs_7_ = f32[8,128]{1,0:T(8,128)S(1)} collective-permute-done((f32[8,128]{1,0:T(8,128)S(1)}, f32[8,128]{1,0:T(8,128)S(1)}, u32[]{:S(2)}, u32[]{:S(2)}) %collective-permute-start.10) | collective-permute-done | bytes 4128 | tf_op jit(solution)/shard_map/ppermute | solution.py:125
  25.9 1.7 %collective-permute-done.8.refs_5_ = f32[8,128]{1,0:T(8,128)S(1)} collective-permute-done((f32[8,128]{1,0:T(8,128)S(1)}, f32[8,128]{1,0:T(8,128)S(1)}, u32[]{:S(2)}, u32[]{:S(2)}) %collective-permute-start.8) | collective-permute-done | bytes 4128 | tf_op jit(solution)/shard_map/ppermute | solution.py:125
  27.7 2.2 %second_product.1 = (f32[128,128]{1,0:T(8,128)S(1)}, f32[192,128]{1,0:T(8,128)S(1)}, f32[192,128]{1,0:T(8,128)S(1)}) custom-call(s32[14,1,16]{2,1,0:T(1,128)S(1)} %bitcast.23, s32[14,1,16]{2,1,0:T(1,128)S(1)} %collective-permute-done.refs_0_.refs_1_, f32[128,128]{1,0:T(8,128)S(1)} %get-tuple-element.13.refs_2_, ...), custom_call_target="tpu_custom_call" | custom-call | tf_op jit(solution)/shard_map/second_product/pallas_call | solution.py:198
  30.3 1.0 %collective-permute-done.11 = f32[192,128]{1,0:T(8,128)S(1)} collective-permute-done((f32[192,128]{1,0:T(8,128)S(1)}, f32[192,128]{1,0:T(8,128)S(1)}, u32[]{:S(2)}, u32[]{:S(2)}) %collective-permute-start.11) | collective-permute-done | bytes 98336 | tf_op jit(solution)/shard_map/ppermute | solution.py:125
  31.3 1.7 %collective-permute-start.13 = (f32[64,128]{1,0:T(8,128)S(1)}, f32[64,128]{1,0:T(8,128)S(1)}, u32[]{:S(2)}, u32[]{:S(2)}) collective-permute-start(f32[64,128]{1,0:T(8,128)S(1)} %slice.29), channel_id=1, source_target_pairs={{0,13},{1,12},{2,15},{3,14},{4,9},{5,8},{6,11},{7,10},{8,5},{9,4},... | collective-permute-start | bytes 98312 | tf_op jit(solution)/shard_map/ppermute | solution.py:125
  33.0 0.6 %collective-permute-start.12 = (f32[128,128]{1,0:T(8,128)S(1)}, f32[128,128]{1,0:T(8,128)S(1)}, u32[]{:S(2)}, u32[]{:S(2)}) collective-permute-start(f32[128,128]{1,0:T(8,128)S(1)} %slice.28), channel_id=1, source_target_pairs={{0,5},{1,8},{2,7},{3,10},{4,1},{5,12},{6,3},{7,14},{8,13},{9,0},{1... | collective-permute-start | bytes 196616 | tf_op jit(solution)/shard_map/ppermute | solution.py:125
  33.7 2.9 %collective-permute-done.13 = f32[64,128]{1,0:T(8,128)S(1)} collective-permute-done((f32[64,128]{1,0:T(8,128)S(1)}, f32[64,128]{1,0:T(8,128)S(1)}, u32[]{:S(2)}, u32[]{:S(2)}) %collective-permute-start.13) | collective-permute-done | bytes 32800 | tf_op jit(solution)/shard_map/ppermute | solution.py:125
  36.5 1.9 %collective-permute-done.12 = f32[128,128]{1,0:T(8,128)S(1)} collective-permute-done((f32[128,128]{1,0:T(8,128)S(1)}, f32[128,128]{1,0:T(8,128)S(1)}, u32[]{:S(2)}, u32[]{:S(2)}) %collective-permute-start.12) | collective-permute-done | bytes 65568 | tf_op jit(solution)/shard_map/ppermute | solution.py:125
  38.5 0.6 %select_bitcast_fusion = f32[1,128,128]{2,1,0:T(8,128)} fusion(f32[128,128]{1,0:T(8,128)S(1)} %get-tuple-element.13.refs_2_, f32[128,128]{1,0:T(8,128)S(1)} %collective-permute-done.7.refs_3_, pred[]{:T(512)S(6)} %eq.4), kind=kLoop, calls=%fused_computation.8 | loop fusion | flops 16384 | bytes 196609 | tf_op jit(solution)/shard_map/broadcast_in_dim | solution.py:221
  39.8 0.6 %add_bitcast_fusion = f32[1,128,128]{2,1,0:T(8,128)} fusion(f32[128,128]{1,0:T(8,128)S(1)} %maximum_add_fusion, f32[128,128]{1,0:T(8,128)S(1)} %collective-permute-done.14), kind=kLoop, calls=%fused_computation.7 | loop fusion | flops 16384 | bytes 196608 | tf_op jit(solution)/shard_map/broadcast_in_dim | solution.py:221
  (26 shorter events, 3.0 us)
Async XLA Ops:
  0.6 6.3 %collective-permute-start.1 = (bf16[1,128,128]{2,1,0:T(8,128)(2,1)}, bf16[1,128,128]{2,1,0:T(8,128)(2,1)S(1)}, u32[]{:S(2)}, u32[]{:S(2)}) collective-permute-start(bf16[1,128,128]{2,1,0:T(8,128)(2,1)} %theta.1), channel_id=1, source_target_pairs={{0,3},{1,2},{2,1},{3,0},{4,7},{5,6},{6,5},{7,4},{8,11},{9,10},{10,... | collective-permute-start | bytes 98312 | tf_op jit(solution)/shard_map/ppermute | solution.py:125
  3.1 3.9 %collective-permute-start = (s32[14,1,16]{2,1,0:T(1,128)}, s32[14,1,16]{2,1,0:T(1,128)S(1)}, u32[]{:S(2)}, u32[]{:S(2)}) collective-permute-start(s32[14,1,16]{2,1,0:T(1,128)} %bitcast.21), channel_id=1, source_target_pairs={{0,2},{1,3},{2,0},{3,1},{4,6},{5,7},{6,4},{7,5},{8,10},{9,11},{10,... | collective-permute-start | bytes 2696 | tf_op jit(solution)/shard_map/ppermute | solution.py:125
  3.7 1.6 %copy-start = (bf16[1,128,128]{2,1,0:T(8,128)(2,1)S(1)}, bf16[1,128,128]{2,1,0:T(8,128)(2,1)}, u32[]{:S(2)}) copy-start(bf16[1,128,128]{2,1,0:T(8,128)(2,1)} %theta.1) | copy-start | bytes 98308
  3.7 1.6 %copy-start.1 = (s32[1,1,1,16,14]{3,2,4,1,0:T(1,128)S(1)}, s32[1,1,1,16,14]{3,2,4,1,0:T(1,128)}, u32[]{:S(2)}) copy-start(s32[1,1,1,16,14]{3,2,4,1,0:T(1,128)} %param.7) | copy-start | bytes 2692
  8.4 1.6 %collective-permute-start.2 = (f32[4,128,128]{2,1,0:T(8,128)S(1)}, f32[4,128,128]{2,1,0:T(8,128)S(1)}, u32[]{:S(2)}, u32[]{:S(2)}) collective-permute-start(f32[4,128,128]{2,1,0:T(8,128)S(1)} %first_rest.1), channel_id=1, source_target_pairs={{0,1},{1,0},{2,3},{3,2},{4,5},{5,4},{6,7},{7,6},{8,9},{9,8},{10,11... | collective-permute-start | bytes 786440 | tf_op jit(solution)/shard_map/ppermute | solution.py:125
  10.1 7.0 %collective-permute-start.3 = (f32[128,128]{1,0:T(8,128)S(1)}, f32[128,128]{1,0:T(8,128)S(1)}, u32[]{:S(2)}, u32[]{:S(2)}) collective-permute-start(f32[128,128]{1,0:T(8,128)S(1)} %get-tuple-element.17), channel_id=1, source_target_pairs={{0,13},{1,14},{2,15},{3,12},{4,9},{5,10},{6,11},{7,8},{8,5},{9,6},... | collective-permute-start | bytes 196616 | tf_op jit(solution)/shard_map/ppermute | solution.py:125
  13.5 5.0 %collective-permute-start.4 = (f32[128,128]{1,0:T(8,128)S(1)}, f32[128,128]{1,0:T(8,128)S(1)}, u32[]{:S(2)}, u32[]{:S(2)}) collective-permute-start(f32[128,128]{1,0:T(8,128)S(1)} %get-tuple-element.14), channel_id=1, source_target_pairs={{0,5},{1,6},{2,7},{3,4},{4,1},{5,2},{6,3},{7,0},{8,13},{9,14},{10,... | collective-permute-start | bytes 196616 | tf_op jit(solution)/shard_map/ppermute | solution.py:125
  13.7 6.0 %collective-permute-start.5 = (f32[128,128]{1,0:T(8,128)S(1)}, f32[128,128]{1,0:T(8,128)S(1)}, u32[]{:S(2)}, u32[]{:S(2)}) collective-permute-start(f32[128,128]{1,0:T(8,128)S(1)} %get-tuple-element.16), channel_id=1, source_target_pairs={{0,9},{1,10},{2,11},{3,8},{4,13},{5,14},{6,15},{7,12},{8,1},{9,2},... | collective-permute-start | bytes 196616 | tf_op jit(solution)/shard_map/ppermute | solution.py:125
  14.9 4.8 %collective-permute-start.6 = (f32[128,128]{1,0:T(8,128)S(1)}, f32[128,128]{1,0:T(8,128)S(1)}, u32[]{:S(2)}, u32[]{:S(2)}) collective-permute-start(f32[128,128]{1,0:T(8,128)S(1)} %get-tuple-element.15), channel_id=1, source_target_pairs={{0,1},{1,2},{2,3},{3,0},{4,5},{5,6},{6,7},{7,4},{8,9},{9,10},{10,1... | collective-permute-start | bytes 196616 | tf_op jit(solution)/shard_map/ppermute | solution.py:125
  19.7 1.3 %collective-permute-start.7 = (f32[128,128]{1,0:T(8,128)S(1)}, f32[128,128]{1,0:T(8,128)S(1)}, u32[]{:S(2)}, u32[]{:S(2)}) collective-permute-start(f32[128,128]{1,0:T(8,128)S(1)} %get-tuple-element.13.refs_2_), channel_id=1, source_target_pairs={{0,1},{1,0},{2,3},{3,2},{4,5},{5,4},{6,7},{7,6},{8,9},{9,8},{10,11... | collective-permute-start | bytes 196616 | tf_op jit(solution)/shard_map/ppermute | solution.py:125
  21.0 4.9 %collective-permute-start.10 = (f32[8,128]{1,0:T(8,128)S(1)}, f32[8,128]{1,0:T(8,128)S(1)}, u32[]{:S(2)}, u32[]{:S(2)}) collective-permute-start(f32[8,128]{1,0:T(8,128)S(1)} %add.31.refs_4_), channel_id=1, source_target_pairs={{0,13},{1,12},{2,15},{3,14},{4,9},{5,8},{6,11},{7,10},{8,5},{9,4},... | collective-permute-start | bytes 12296 | tf_op jit(solution)/shard_map/ppermute | solution.py:125
  23.7 4.0 %collective-permute-start.8 = (f32[8,128]{1,0:T(8,128)S(1)}, f32[8,128]{1,0:T(8,128)S(1)}, u32[]{:S(2)}, u32[]{:S(2)}) collective-permute-start(f32[8,128]{1,0:T(8,128)S(1)} %add.31.refs_4_), channel_id=1, source_target_pairs={{0,9},{1,8},{2,11},{3,10},{4,13},{5,12},{6,15},{7,14},{8,1},{9,0},... | collective-permute-start | bytes 12296 | tf_op jit(solution)/shard_map/ppermute | solution.py:125
  24.6 3.1 %collective-permute-start.9 = (f32[8,128]{1,0:T(8,128)S(1)}, f32[8,128]{1,0:T(8,128)S(1)}, u32[]{:S(2)}, u32[]{:S(2)}) collective-permute-start(f32[8,128]{1,0:T(8,128)S(1)} %add.31.refs_4_), channel_id=1, source_target_pairs={{0,5},{1,4},{2,7},{3,6},{4,1},{5,0},{6,3},{7,2},{8,13},{9,12},{10,... | collective-permute-start | bytes 12296 | tf_op jit(solution)/shard_map/ppermute | solution.py:125
  29.9 1.4 %collective-permute-start.11 = (f32[192,128]{1,0:T(8,128)S(1)}, f32[192,128]{1,0:T(8,128)S(1)}, u32[]{:S(2)}, u32[]{:S(2)}) collective-permute-start(f32[192,128]{1,0:T(8,128)S(1)} %get-tuple-element.11), channel_id=1, source_target_pairs={{0,1},{1,0},{2,3},{3,2},{4,5},{5,4},{6,7},{7,6},{8,9},{9,8},{10,11... | collective-permute-start | bytes 294920 | tf_op jit(solution)/shard_map/ppermute | solution.py:125
  31.3 5.2 %collective-permute-start.13 = (f32[64,128]{1,0:T(8,128)S(1)}, f32[64,128]{1,0:T(8,128)S(1)}, u32[]{:S(2)}, u32[]{:S(2)}) collective-permute-start(f32[64,128]{1,0:T(8,128)S(1)} %slice.29), channel_id=1, source_target_pairs={{0,13},{1,12},{2,15},{3,14},{4,9},{5,8},{6,11},{7,10},{8,5},{9,4},... | collective-permute-start | bytes 98312 | tf_op jit(solution)/shard_map/ppermute | solution.py:125
  33.0 5.4 %collective-permute-start.12 = (f32[128,128]{1,0:T(8,128)S(1)}, f32[128,128]{1,0:T(8,128)S(1)}, u32[]{:S(2)}, u32[]{:S(2)}) collective-permute-start(f32[128,128]{1,0:T(8,128)S(1)} %slice.28), channel_id=1, source_target_pairs={{0,5},{1,8},{2,7},{3,10},{4,1},{5,12},{6,3},{7,14},{8,13},{9,0},{1... | collective-permute-start | bytes 196616 | tf_op jit(solution)/shard_map/ppermute | solution.py:125
  38.5 1.3 %collective-permute-start.14 = (f32[128,128]{1,0:T(8,128)S(1)}, f32[128,128]{1,0:T(8,128)S(1)}, u32[]{:S(2)}, u32[]{:S(2)}) collective-permute-start(f32[128,128]{1,0:T(8,128)S(1)} %maximum_add_fusion), channel_id=1, source_target_pairs={{0,1},{1,0},{2,3},{3,2},{4,5},{5,4},{6,7},{7,6},{8,9},{9,8},{10,11... | collective-permute-start | bytes 196616 | tf_op jit(solution)/shard_map/ppermute | solution.py:125

commit v4 on v3

--- a/solution.py
+++ b/solution.py
@@ -7,48 +7,75 @@
 from jax.experimental.pallas import tpu as pltpu
 from jax.sharding import PartitionSpec as P
 
+BLOCKS = 4
 CAP = 8
 VMEM = pl.BlockSpec(memory_space=pltpu.VMEM)
 HBM = pl.BlockSpec(memory_space=pltpu.HBM)
-SMEM = pl.BlockSpec(memory_space=pltpu.SMEM)
 
 
 def dot(a, b):
     return jnp.dot(a, b, preferred_element_type=jnp.float32)
 
 
-def pick_entries(terms, sel):
+def pick_entries(terms, words, lt_dev, rt_dev):
     me_right = lax.axis_index("right")
-    count = jnp.int32(0)
-    for e in range(terms.shape[-1]):
-        sel[count] = jnp.int32(e)
-        count = count + (terms[1, 0, e] == me_right).astype(jnp.int32)
-    return count
-
-
-def apply_list(terms, sel, count, vec, left_ref, right_ref, acc, inter, dims):
-    lt_dev, rt_dev, exact = dims
     me_left = lax.axis_index("left")
     fields, _, rows = terms.shape
     per = (fields - 2) // 2
+    bits = lambda count: (count - 1).bit_length()
+    left_bits, target_bits = bits(2 * lt_dev), bits(lax.axis_size("right"))
+    tile_bits, out_bits = bits(rt_dev), bits(lax.axis_size("left"))
+    shift = left_bits + target_bits
+    tiles = terms[0] + (terms[1] << left_bits)
+    offsets = terms[2 + per] ^ me_left
+    for j in range(per):
+        tiles = tiles + (terms[2 + j] << (shift + j * tile_bits))
+        if j:
+            offsets = offsets + ((terms[2 + per + j] ^ me_left) << (j * out_bits))
+    count = jnp.int32(0)
+    for e in range(rows):
+        word = tiles[0, e]
+        words[0, count] = word
+        words[1, count] = offsets[0, e]
+        target = (word >> left_bits) & ((1 << target_bits) - 1)
+        count = count + (target == me_right).astype(jnp.int32)
+
+    def read(n):
+        word, outs = words[0, n], words[1, n]
+        left = word & ((1 << left_bits) - 1)
+        base = (left // lt_dev) * rt_dev
+        rights = [base + ((word >> (shift + j * tile_bits)) & ((1 << tile_bits) - 1)) for j in range(per)]
+        return left, rights, [(outs >> (j * out_bits)) & ((1 << out_bits) - 1) for j in range(per)]
+
+    return count, read
+
+
+def blocks(accs):
+    size = accs[0].shape[-2]
+    return [(slice(i * size, (i + 1) * size), acc) for i, acc in enumerate(accs)]
+
+
+def apply_list(picked, vec, left_ref, right_ref, accs, inter, exact):
+    count, read = picked
     tile = vec.shape[-1]
 
-    def spread(e, y):
-        base = (terms[0, 0, e] // lt_dev) * rt_dev
-        for j in range(per):
-            product = dot(y, right_ref[base + terms[2 + j, 0, e]])
-            acc[terms[2 + per + j, 0, e] ^ me_left] += product
+    def spread(rights, outs, y):
+        for right, out in zip(rights, outs):
+            product = dot(y, right_ref[right])
+            for rows, acc in blocks(accs):
+                acc[out] += product[rows]
 
     if exact:
-        picks = jnp.concatenate([left_ref[terms[0, 0, sel[n]]] for n in range(CAP)], axis=0)
+        entries = [read(n) for n in range(CAP)]
+        picks = jnp.concatenate([left_ref[entry[0]] for entry in entries], axis=0)
         inter[...] = dot(picks, vec).astype(jnp.bfloat16).reshape(CAP, tile, tile)
-        for n in range(CAP):
-            spread(sel[n], inter[n])
+        for n, (_, rights, outs) in enumerate(entries):
+            spread(rights, outs, inter[n])
     else:
 
         def one(n):
-            e = sel[n]
-            spread(e, dot(left_ref[terms[0, 0, e]], vec).astype(jnp.bfloat16))
+            left, rights, outs = read(n)
+            spread(rights, outs, dot(left_ref[left], vec).astype(jnp.bfloat16))
 
         pl.loop(0, count)(one)
 
@@ -64,20 +91,27 @@
         copy.wait()
 
 
-def own_kernel(dims, terms, theta, left_ref, right_ref, out, sel, inter):
-    out[...] = jnp.zeros_like(out)
-    count = pick_entries(terms, sel)
-    apply_list(terms, sel, count, theta[0], left_ref, right_ref, out, inter, dims)
+def own_kernel(dims, terms, theta, left_ref, right_ref, *refs):
+    *accs, words, inter = refs
+    picked = pick_entries(terms, words.at[0], *dims[:2])
+    for acc in accs:
+        acc[...] = jnp.zeros_like(acc)
+    apply_list(picked, theta[0], left_ref, right_ref, accs, inter.at[0], dims[2])
 
 
 def rest_kernel(dims, count, *refs):
     lists = refs[:count]
     thetas = refs[count:2 * count]
-    left_ref, right_ref, start, out, sel, inter = refs[2 * count:]
-    out[...] = start[...]
-    for terms, theta in zip(lists, thetas):
-        picked = pick_entries(terms, sel)
-        apply_list(terms, sel, picked, theta[0], left_ref, right_ref, out, inter, dims)
+    left_ref, right_ref = refs[2 * count:2 * count + 2]
+    starts = refs[2 * count + 2:2 * count + 2 + BLOCKS]
+    out, *accs, words, inter = refs[2 * count + 2 + BLOCKS:]
+    picked = [pick_entries(terms, words.at[i], *dims[:2]) for i, terms in enumerate(lists)]
+    for acc, start in zip(accs, starts):
+        acc[...] = start[...]
+    for i, theta in enumerate(thetas):
+        apply_list(picked[i], theta[0], left_ref, right_ref, accs, inter.at[i], dims[2])
+    for rows, acc in blocks(accs):
+        out[:, rows] = acc[...]
 
 
 def second_kernel(dims, nr, nl, chip_pair, elements, *refs):
@@ -85,33 +119,38 @@
     tiles = refs[nr:2 * nr]
     sums = refs[2 * nr:2 * nr + nl]
     left_ref, right_ref = refs[2 * nr + nl:2 * nr + nl + 2]
-    outs = refs[2 * nr + nl + 2:-3]
-    acc, sel, inter = refs[-3:]
+    outs = refs[2 * nr + nl + 2:-2 - BLOCKS]
+    *accs, words, inter = refs[-2 - BLOCKS:]
+    picked = [pick_entries(terms, words.at[i], *dims[:2]) for i, terms in enumerate(lists)]
     me = lax.axis_index("mpo")
     total = sums[0][...]
     for part in sums[1:]:
         total = total + part[...]
-    scale = jnp.sqrt(jnp.sum(total, keepdims=True) / elements + 1e-06)
+    scale = 1.0 / jnp.sqrt(jnp.sum(total, keepdims=True) / elements + 1e-06)
     values = [t[...] for t in tiles]
     if chip_pair:
         values = [jnp.where(me == 0, values[1 - i], values[i]) for i in range(2)]
-    acc[...] = jnp.zeros_like(acc)
-    for terms, value in zip(lists, values):
-        vec = (value / scale).astype(jnp.bfloat16)
-        picked = pick_entries(terms, sel)
-        apply_list(terms, sel, picked, vec, left_ref, right_ref, acc, inter, dims)
+    for acc in accs:
+        acc[...] = jnp.zeros_like(acc)
+    for i, value in enumerate(values):
+        vec = (value * scale).astype(jnp.bfloat16)
+        apply_list(picked[i], vec, left_ref, right_ref, accs, inter.at[i], dims[2])
     if nl == 4:
         own, keep, give = outs
         tile = own.shape[0]
-        half = tile // 2
-        own[...] = acc[0]
-        keep[:tile] = acc[1 + me]
-        keep[tile:] = acc[3, pl.ds(pl.multiple_of(half * me, half), half)]
-        give[:tile] = acc[2 - me]
-        give[tile:] = acc[3, pl.ds(pl.multiple_of(half - half * me, half), half)]
+        for rows, acc in blocks(accs):
+            own[rows] = acc[0]
+            keep[rows] = acc[1 + me]
+            give[rows] = acc[2 - me]
+        half = len(accs) // 2
+        for (rows, low), (_, high) in zip(blocks(accs[:half]), blocks(accs[half:])):
+            rows = slice(tile + rows.start, tile + rows.stop)
+            keep[rows] = jnp.where(me == 0, low[3], high[3])
+            give[rows] = jnp.where(me == 0, high[3], low[3])
     else:
         for s in range(nl):
-            outs[s][...] = acc[s]
+            for rows, acc in blocks(accs):
+                outs[s][rows] = acc[s]
 
 
 def permute(value, target):
@@ -141,7 +180,9 @@
     lists = [entries] + [permute(entries, lambda p, t, m, s=s: (p, t ^ s, m)) for s in range(1, nr)]
     thetas = [theta] + [permute(theta, lambda p, t, m, s=s: (p, t ^ s, 1 - m)) for s in range(1, nr)]
     stack = jax.ShapeDtypeStruct((nl, tile, tile), jnp.float32)
-    scratch = [pltpu.SMEM((rows + 1,), jnp.int32), pltpu.VMEM((CAP, tile, tile), jnp.bfloat16)]
+    part_shapes = [((nl, tile // BLOCKS, tile), jnp.float32)] * BLOCKS
+    accs = [pltpu.VMEM(*shape) for shape in part_shapes]
+    scratch = [pltpu.SMEM((nr, 2, rows + 1), jnp.int32), pltpu.VMEM((nr, CAP, tile, tile), jnp.bfloat16)]
     params = pltpu.CompilerParams(vmem_limit_bytes=32 << 20)
 
     left_flat, right_flat = pl.pallas_call(
@@ -153,11 +194,11 @@
         compiler_params=pltpu.CompilerParams(vmem_limit_bytes=51 << 20),
         name="load",
     )(left_flat, right_flat)
-    own_part = pl.pallas_call(
+    own_parts = pl.pallas_call(
         functools.partial(own_kernel, dims),
-        out_shape=stack,
-        in_specs=[SMEM] + [VMEM] * 3,
-        out_specs=VMEM,
+        out_shape=[jax.ShapeDtypeStruct(*shape) for shape in part_shapes],
+        in_specs=[VMEM] * 4,
+        out_specs=[VMEM] * BLOCKS,
         scratch_shapes=scratch,
         compiler_params=params,
         name="first_own",
@@ -165,12 +206,12 @@
     part = pl.pallas_call(
         functools.partial(rest_kernel, dims, nr - 1),
         out_shape=stack,
-        in_specs=[SMEM] * (nr - 1) + [VMEM] * (nr + 2),
+        in_specs=[VMEM] * (2 * nr + BLOCKS),
         out_specs=VMEM,
-        scratch_shapes=scratch,
+        scratch_shapes=accs + scratch,
         compiler_params=params,
         name="first_rest",
-    )(*lists[1:], *thetas[1:], left_flat, right_flat, own_part)
+    )(*lists[1:], *thetas[1:], left_flat, right_flat, *own_parts)
 
     chip = part + swap_cores(part)
     if chip_pair:
@@ -198,9 +239,9 @@
     parts = pl.pallas_call(
         functools.partial(second_kernel, dims, nr, nl, chip_pair, nl * nr * tile * tile),
         out_shape=out_shape,
-        in_specs=[SMEM] * nr + [VMEM] * (nr + nl + 2),
+        in_specs=[VMEM] * (2 * nr + nl + 2),
         out_specs=[VMEM] * len(out_shape),
-        scratch_shapes=[pltpu.VMEM((nl, tile, tile), jnp.float32)] + scratch,
+        scratch_shapes=accs + scratch,
         compiler_params=params,
         name="second_product",
     )(*lists, *tiles, *sums, left_flat, right_flat)

time: 40.6 us -> 39.3 us (0.968)
  Pallas kernels: 6.72 us -> 5.12 us
  waiting for transfers between devices: 15.9 us -> 16.8 us
  starting transfers between devices: 15.7 us -> 15.1 us
    ppermute x15, waiting for transfers between devices: 15.9 us -> 16.8 us  [permute(): return lax.ppermute(value, ('left', 'right', 'mpo'), pairs)]
    pallas_call x1, Pallas kernels: 2.24 us -> 1.59 us  [local(): pl.pallas_call(functools.partial(second_kernel, dims, nr, nl, chip_pair,...]
    ppermute x15, starting transfers between devices: 15.7 us -> 15.1 us  [permute(): return lax.ppermute(value, ('left', 'right', 'mpo'), pairs)]
    pallas_call x1, Pallas kernels: 1.46 us -> 0.98 us  [local(): pl.pallas_call(functools.partial(rest_kernel, dims, nr - 1), out_shape=st...]
    pallas_call x1, Pallas kernels: 1.46 us -> 0.99 us  [local(): pl.pallas_call(functools.partial(own_kernel, dims), out_shape=[jax.ShapeD...]
  transfers between devices with their start and end apart: 15 -> 15, of which waited for: 12 -> 14; matrix products, arithmetic and copies ran while one was open for 2% -> 2% of each run, Pallas kernels for 7% -> 7%
where the time goes in v4:
time: 39.3 us; the launch traced here: 39.2 us
  waiting for transfers between devices  16.8 us (43%)
  starting transfers between devices  15.1 us (38%)
  Pallas kernels  5.12 us (13%)
  other arithmetic  1.39 us (4%)
  between operations  0.74 us (2%)
    ppermute x15, waiting for transfers between devices, permute(): return lax.ppermute(value, ('left', 'right', 'mpo'), pairs)  16.8 us
    ppermute x15, starting transfers between devices, permute(): return lax.ppermute(value, ('left', 'right', 'mpo'), pairs)  15.1 us
    pallas_call x1, Pallas kernels, local(): pl.pallas_call(functools.partial(second_kernel, dims, nr, nl, chip_pair,...  1.59 us
    pallas_call x1, Pallas kernels, local(): pl.pallas_call(load_kernel, out_shape=[jax.ShapeDtypeStruct(x.shape, x.dt...  1.56 us
    broadcast_in_dim x2, other arithmetic, local(): return (h_theta[None], h_second[None])  1.28 us
    pallas_call x1, Pallas kernels, local(): pl.pallas_call(functools.partial(own_kernel, dims), out_shape=[jax.ShapeD...  0.99 us
    pallas_call x1, Pallas kernels, local(): pl.pallas_call(functools.partial(rest_kernel, dims, nr - 1), out_shape=st...  0.98 us
  transfers between devices with their start and end apart: 15, of which 14 were waited for; matrix products, arithmetic and copies ran while one was open for 2% of the time, Pallas kernels for 7%

profile of v4, /device:TPU:0, one launch (start us, length us, event | category | flops | bytes accessed | tf_op | source)
XLA Modules:
  0.0 39.2 jit_solution(16798913504979088815)
XLA Ops:
  0.6 2.4 %collective-permute-start.1 = (bf16[1,128,128]{2,1,0:T(8,128)(2,1)}, bf16[1,128,128]{2,1,0:T(8,128)(2,1)S(1)}, u32[]{:S(2)}, u32[]{:S(2)}) collective-permute-start(bf16[1,128,128]{2,1,0:T(8,128)(2,1)} %theta.1), channel_id=1, source_target_pairs={{0,3},{1,2},{2,1},{3,0},{4,7},{5,6},{6,5},{7,4},{8,11},{9,10},{10,... | collective-permute-start | bytes 98312 | tf_op jit(solution)/shard_map/ppermute | solution.py:164
  3.1 0.6 %collective-permute-start = (s32[14,1,16]{2,1,0:T(1,128)}, s32[14,1,16]{2,1,0:T(1,128)S(1)}, u32[]{:S(2)}, u32[]{:S(2)}) collective-permute-start(s32[14,1,16]{2,1,0:T(1,128)} %bitcast.21), channel_id=1, source_target_pairs={{0,2},{1,3},{2,0},{3,1},{4,6},{5,7},{6,4},{7,5},{8,10},{9,11},{10,... | collective-permute-start | bytes 2696 | tf_op jit(solution)/shard_map/ppermute | solution.py:164
  3.7 1.6 %load.1 = (bf16[32,128,128]{2,1,0:T(8,128)(2,1)S(1)}, bf16[32,128,128]{2,1,0:T(8,128)(2,1)S(1)}) custom-call(bf16[32,128,128]{2,1,0:T(8,128)(2,1)} %bitcast.24, bf16[32,128,128]{2,1,0:T(8,128)(2,1)} %bitcast.25), custom_call_target="tpu_custom_call" | custom-call | tf_op jit(solution)/shard_map/load/pallas_call | solution.py:188
  5.3 1.0 %first_own.1 = (f32[4,32,128]{2,1,0:T(8,128)S(1)}, f32[4,32,128]{2,1,0:T(8,128)S(1)}, f32[4,32,128]{2,1,0:T(8,128)S(1)}, f32[4,32,128]{2,1,0:T(8,128)S(1)}) custom-call(s32[14,1,16]{2,1,0:T(1,128)S(1)} %bitcast.22, bf16[1,128,128]{2,1,0:T(8,128)(2,1)S(1)} %copy-done, bf16[32,128,128]{2,1,0:T(8,128)(2,1)S(1)} %get-tuple-element.11.left_ref.refs_2_.refs_8_, ...), custom_call_target="tpu_custom_call" | custom-call | tf_op jit(solution)/shard_map/first_own/pallas_call | solution.py:197
  6.9 1.0 %first_rest.1 = f32[4,128,128]{2,1,0:T(8,128)S(1)} custom-call(s32[14,1,16]{2,1,0:T(1,128)S(1)} %collective-permute-done.refs_0_.refs_1_, bf16[1,128,128]{2,1,0:T(8,128)(2,1)S(1)} %collective-permute-done.1.refs_1_, bf16[32,128,128]{2,1,0:T(8,128)(2,1)S(1)} %get-tuple-element.11.left_ref.refs_2_.refs_8_, ...), custom_call_target="tpu_custom_call" | custom-call | tf_op jit(solution)/shard_map/first_rest/pallas_call | solution.py:206
  8.0 1.5 %collective-permute-done.2 = f32[4,128,128]{2,1,0:T(8,128)S(1)} collective-permute-done((f32[4,128,128]{2,1,0:T(8,128)S(1)}, f32[4,128,128]{2,1,0:T(8,128)S(1)}, u32[]{:S(2)}, u32[]{:S(2)}) %collective-permute-start.2) | collective-permute-done | bytes 262176 | tf_op jit(solution)/shard_map/ppermute | solution.py:164
  9.6 3.4 %collective-permute-start.3 = (f32[128,128]{1,0:T(8,128)S(1)}, f32[128,128]{1,0:T(8,128)S(1)}, u32[]{:S(2)}, u32[]{:S(2)}) collective-permute-start(f32[128,128]{1,0:T(8,128)S(1)} %get-tuple-element.25), channel_id=1, source_target_pairs={{0,13},{1,14},{2,15},{3,12},{4,9},{5,10},{6,11},{7,8},{8,5},{9,6},... | collective-permute-start | bytes 196616 | tf_op jit(solution)/shard_map/ppermute | solution.py:164
  13.0 1.0 %collective-permute-start.5 = (f32[128,128]{1,0:T(8,128)S(1)}, f32[128,128]{1,0:T(8,128)S(1)}, u32[]{:S(2)}, u32[]{:S(2)}) collective-permute-start(f32[128,128]{1,0:T(8,128)S(1)} %get-tuple-element.24), channel_id=1, source_target_pairs={{0,9},{1,10},{2,11},{3,8},{4,13},{5,14},{6,15},{7,12},{8,1},{9,2},... | collective-permute-start | bytes 196616 | tf_op jit(solution)/shard_map/ppermute | solution.py:164
  13.9 0.8 %collective-permute-start.6 = (f32[128,128]{1,0:T(8,128)S(1)}, f32[128,128]{1,0:T(8,128)S(1)}, u32[]{:S(2)}, u32[]{:S(2)}) collective-permute-start(f32[128,128]{1,0:T(8,128)S(1)} %get-tuple-element.23), channel_id=1, source_target_pairs={{0,1},{1,2},{2,3},{3,0},{4,5},{5,6},{6,7},{7,4},{8,9},{9,10},{10,1... | collective-permute-start | bytes 196616 | tf_op jit(solution)/shard_map/ppermute | solution.py:164
  14.8 2.0 %collective-permute-done.3 = f32[128,128]{1,0:T(8,128)S(1)} collective-permute-done((f32[128,128]{1,0:T(8,128)S(1)}, f32[128,128]{1,0:T(8,128)S(1)}, u32[]{:S(2)}, u32[]{:S(2)}) %collective-permute-start.3) | collective-permute-done | bytes 65568 | tf_op jit(solution)/shard_map/ppermute | solution.py:164
  16.8 1.0 %collective-permute-done.4 = f32[128,128]{1,0:T(8,128)S(1)} collective-permute-done((f32[128,128]{1,0:T(8,128)S(1)}, f32[128,128]{1,0:T(8,128)S(1)}, u32[]{:S(2)}, u32[]{:S(2)}) %collective-permute-start.4) | collective-permute-done | bytes 65568 | tf_op jit(solution)/shard_map/ppermute | solution.py:164
  17.8 1.0 %collective-permute-done.5 = f32[128,128]{1,0:T(8,128)S(1)} collective-permute-done((f32[128,128]{1,0:T(8,128)S(1)}, f32[128,128]{1,0:T(8,128)S(1)}, u32[]{:S(2)}, u32[]{:S(2)}) %collective-permute-start.5) | collective-permute-done | bytes 65568 | tf_op jit(solution)/shard_map/ppermute | solution.py:164
  19.2 1.1 %collective-permute-done.7.refs_3_ = f32[128,128]{1,0:T(8,128)S(1)} collective-permute-done((f32[128,128]{1,0:T(8,128)S(1)}, f32[128,128]{1,0:T(8,128)S(1)}, u32[]{:S(2)}, u32[]{:S(2)}) %collective-permute-start.7) | collective-permute-done | bytes 65568 | tf_op jit(solution)/shard_map/ppermute | solution.py:164
  20.3 2.6 %collective-permute-start.10 = (f32[8,128]{1,0:T(8,128)S(1)}, f32[8,128]{1,0:T(8,128)S(1)}, u32[]{:S(2)}, u32[]{:S(2)}) collective-permute-start(f32[8,128]{1,0:T(8,128)S(1)} %add.31.refs_4_), channel_id=1, source_target_pairs={{0,13},{1,12},{2,15},{3,14},{4,9},{5,8},{6,11},{7,10},{8,5},{9,4},... | collective-permute-start | bytes 12296 | tf_op jit(solution)/shard_map/ppermute | solution.py:164
  22.9 1.0 %collective-permute-start.8 = (f32[8,128]{1,0:T(8,128)S(1)}, f32[8,128]{1,0:T(8,128)S(1)}, u32[]{:S(2)}, u32[]{:S(2)}) collective-permute-start(f32[8,128]{1,0:T(8,128)S(1)} %add.31.refs_4_), channel_id=1, source_target_pairs={{0,9},{1,8},{2,11},{3,10},{4,13},{5,12},{6,15},{7,14},{8,1},{9,0},... | collective-permute-start | bytes 12296 | tf_op jit(solution)/shard_map/ppermute | solution.py:164
  24.3 1.0 %collective-permute-done.10.refs_7_ = f32[8,128]{1,0:T(8,128)S(1)} collective-permute-done((f32[8,128]{1,0:T(8,128)S(1)}, f32[8,128]{1,0:T(8,128)S(1)}, u32[]{:S(2)}, u32[]{:S(2)}) %collective-permute-start.10) | collective-permute-done | bytes 4128 | tf_op jit(solution)/shard_map/ppermute | solution.py:164
  25.2 1.7 %collective-permute-done.8.refs_5_ = f32[8,128]{1,0:T(8,128)S(1)} collective-permute-done((f32[8,128]{1,0:T(8,128)S(1)}, f32[8,128]{1,0:T(8,128)S(1)}, u32[]{:S(2)}, u32[]{:S(2)}) %collective-permute-start.8) | collective-permute-done | bytes 4128 | tf_op jit(solution)/shard_map/ppermute | solution.py:164
  27.0 1.6 %second_product.1 = (f32[128,128]{1,0:T(8,128)S(1)}, f32[192,128]{1,0:T(8,128)S(1)}, f32[192,128]{1,0:T(8,128)S(1)}) custom-call(s32[14,1,16]{2,1,0:T(1,128)S(1)} %bitcast.23, s32[14,1,16]{2,1,0:T(1,128)S(1)} %collective-permute-done.refs_0_.refs_1_, f32[128,128]{1,0:T(8,128)S(1)} %get-tuple-element.21.refs_2_, ...), custom_call_target="tpu_custom_call" | custom-call | tf_op jit(solution)/shard_map/second_product/pallas_call | solution.py:239
  28.9 1.0 %collective-permute-done.11 = f32[192,128]{1,0:T(8,128)S(1)} collective-permute-done((f32[192,128]{1,0:T(8,128)S(1)}, f32[192,128]{1,0:T(8,128)S(1)}, u32[]{:S(2)}, u32[]{:S(2)}) %collective-permute-start.11) | collective-permute-done | bytes 98336 | tf_op jit(solution)/shard_map/ppermute | solution.py:164
  30.0 2.1 %collective-permute-start.13 = (f32[64,128]{1,0:T(8,128)S(1)}, f32[64,128]{1,0:T(8,128)S(1)}, u32[]{:S(2)}, u32[]{:S(2)}) collective-permute-start(f32[64,128]{1,0:T(8,128)S(1)} %slice.29), channel_id=1, source_target_pairs={{0,13},{1,12},{2,15},{3,14},{4,9},{5,8},{6,11},{7,10},{8,5},{9,4},... | collective-permute-start | bytes 98312 | tf_op jit(solution)/shard_map/ppermute | solution.py:164
  32.2 3.0 %collective-permute-done.13 = f32[64,128]{1,0:T(8,128)S(1)} collective-permute-done((f32[64,128]{1,0:T(8,128)S(1)}, f32[64,128]{1,0:T(8,128)S(1)}, u32[]{:S(2)}, u32[]{:S(2)}) %collective-permute-start.13) | collective-permute-done | bytes 32800 | tf_op jit(solution)/shard_map/ppermute | solution.py:164
  35.2 2.0 %collective-permute-done.12 = f32[128,128]{1,0:T(8,128)S(1)} collective-permute-done((f32[128,128]{1,0:T(8,128)S(1)}, f32[128,128]{1,0:T(8,128)S(1)}, u32[]{:S(2)}, u32[]{:S(2)}) %collective-permute-start.12) | collective-permute-done | bytes 65568 | tf_op jit(solution)/shard_map/ppermute | solution.py:164
  37.3 0.6 %select_bitcast_fusion = f32[1,128,128]{2,1,0:T(8,128)} fusion(f32[128,128]{1,0:T(8,128)S(1)} %get-tuple-element.21.refs_2_, f32[128,128]{1,0:T(8,128)S(1)} %collective-permute-done.7.refs_3_, pred[]{:T(512)S(6)} %eq.4), kind=kLoop, calls=%fused_computation.8 | loop fusion | flops 16384 | bytes 196609 | tf_op jit(solution)/shard_map/broadcast_in_dim | solution.py:262
  38.5 0.6 %add_bitcast_fusion = f32[1,128,128]{2,1,0:T(8,128)} fusion(f32[128,128]{1,0:T(8,128)S(1)} %maximum_add_fusion, f32[128,128]{1,0:T(8,128)S(1)} %collective-permute-done.14), kind=kLoop, calls=%fused_computation.7 | loop fusion | flops 16384 | bytes 196608 | tf_op jit(solution)/shard_map/broadcast_in_dim | solution.py:262
  (26 shorter events, 2.8 us)
Async XLA Ops:
  0.6 6.3 %collective-permute-start.1 = (bf16[1,128,128]{2,1,0:T(8,128)(2,1)}, bf16[1,128,128]{2,1,0:T(8,128)(2,1)S(1)}, u32[]{:S(2)}, u32[]{:S(2)}) collective-permute-start(bf16[1,128,128]{2,1,0:T(8,128)(2,1)} %theta.1), channel_id=1, source_target_pairs={{0,3},{1,2},{2,1},{3,0},{4,7},{5,6},{6,5},{7,4},{8,11},{9,10},{10,... | collective-permute-start | bytes 98312 | tf_op jit(solution)/shard_map/ppermute | solution.py:164
  3.1 3.9 %collective-permute-start = (s32[14,1,16]{2,1,0:T(1,128)}, s32[14,1,16]{2,1,0:T(1,128)S(1)}, u32[]{:S(2)}, u32[]{:S(2)}) collective-permute-start(s32[14,1,16]{2,1,0:T(1,128)} %bitcast.21), channel_id=1, source_target_pairs={{0,2},{1,3},{2,0},{3,1},{4,6},{5,7},{6,4},{7,5},{8,10},{9,11},{10,... | collective-permute-start | bytes 2696 | tf_op jit(solution)/shard_map/ppermute | solution.py:164
  3.7 1.6 %copy-start = (bf16[1,128,128]{2,1,0:T(8,128)(2,1)S(1)}, bf16[1,128,128]{2,1,0:T(8,128)(2,1)}, u32[]{:S(2)}) copy-start(bf16[1,128,128]{2,1,0:T(8,128)(2,1)} %theta.1) | copy-start | bytes 98308
  3.7 1.6 %copy-start.1 = (s32[1,1,1,16,14]{3,2,4,1,0:T(1,128)S(1)}, s32[1,1,1,16,14]{3,2,4,1,0:T(1,128)}, u32[]{:S(2)}) copy-start(s32[1,1,1,16,14]{3,2,4,1,0:T(1,128)} %param.7) | copy-start | bytes 2692
  7.9 1.6 %collective-permute-start.2 = (f32[4,128,128]{2,1,0:T(8,128)S(1)}, f32[4,128,128]{2,1,0:T(8,128)S(1)}, u32[]{:S(2)}, u32[]{:S(2)}) collective-permute-start(f32[4,128,128]{2,1,0:T(8,128)S(1)} %first_rest.1), channel_id=1, source_target_pairs={{0,1},{1,0},{2,3},{3,2},{4,5},{5,4},{6,7},{7,6},{8,9},{9,8},{10,11... | collective-permute-start | bytes 786440 | tf_op jit(solution)/shard_map/ppermute | solution.py:164
  9.6 7.2 %collective-permute-start.3 = (f32[128,128]{1,0:T(8,128)S(1)}, f32[128,128]{1,0:T(8,128)S(1)}, u32[]{:S(2)}, u32[]{:S(2)}) collective-permute-start(f32[128,128]{1,0:T(8,128)S(1)} %get-tuple-element.25), channel_id=1, source_target_pairs={{0,13},{1,14},{2,15},{3,12},{4,9},{5,10},{6,11},{7,8},{8,5},{9,6},... | collective-permute-start | bytes 196616 | tf_op jit(solution)/shard_map/ppermute | solution.py:164
  13.0 4.8 %collective-permute-start.4 = (f32[128,128]{1,0:T(8,128)S(1)}, f32[128,128]{1,0:T(8,128)S(1)}, u32[]{:S(2)}, u32[]{:S(2)}) collective-permute-start(f32[128,128]{1,0:T(8,128)S(1)} %get-tuple-element.22), channel_id=1, source_target_pairs={{0,5},{1,6},{2,7},{3,4},{4,1},{5,2},{6,3},{7,0},{8,13},{9,14},{10,... | collective-permute-start | bytes 196616 | tf_op jit(solution)/shard_map/ppermute | solution.py:164
  13.0 5.8 %collective-permute-start.5 = (f32[128,128]{1,0:T(8,128)S(1)}, f32[128,128]{1,0:T(8,128)S(1)}, u32[]{:S(2)}, u32[]{:S(2)}) collective-permute-start(f32[128,128]{1,0:T(8,128)S(1)} %get-tuple-element.24), channel_id=1, source_target_pairs={{0,9},{1,10},{2,11},{3,8},{4,13},{5,14},{6,15},{7,12},{8,1},{9,2},... | collective-permute-start | bytes 196616 | tf_op jit(solution)/shard_map/ppermute | solution.py:164
  13.9 5.0 %collective-permute-start.6 = (f32[128,128]{1,0:T(8,128)S(1)}, f32[128,128]{1,0:T(8,128)S(1)}, u32[]{:S(2)}, u32[]{:S(2)}) collective-permute-start(f32[128,128]{1,0:T(8,128)S(1)} %get-tuple-element.23), channel_id=1, source_target_pairs={{0,1},{1,2},{2,3},{3,0},{4,5},{5,6},{6,7},{7,4},{8,9},{9,10},{10,1... | collective-permute-start | bytes 196616 | tf_op jit(solution)/shard_map/ppermute | solution.py:164
  19.0 1.3 %collective-permute-start.7 = (f32[128,128]{1,0:T(8,128)S(1)}, f32[128,128]{1,0:T(8,128)S(1)}, u32[]{:S(2)}, u32[]{:S(2)}) collective-permute-start(f32[128,128]{1,0:T(8,128)S(1)} %get-tuple-element.21.refs_2_), channel_id=1, source_target_pairs={{0,1},{1,0},{2,3},{3,2},{4,5},{5,4},{6,7},{7,6},{8,9},{9,8},{10,11... | collective-permute-start | bytes 196616 | tf_op jit(solution)/shard_map/ppermute | solution.py:164
  20.3 4.9 %collective-permute-start.10 = (f32[8,128]{1,0:T(8,128)S(1)}, f32[8,128]{1,0:T(8,128)S(1)}, u32[]{:S(2)}, u32[]{:S(2)}) collective-permute-start(f32[8,128]{1,0:T(8,128)S(1)} %add.31.refs_4_), channel_id=1, source_target_pairs={{0,13},{1,12},{2,15},{3,14},{4,9},{5,8},{6,11},{7,10},{8,5},{9,4},... | collective-permute-start | bytes 12296 | tf_op jit(solution)/shard_map/ppermute | solution.py:164
  22.9 3.9 %collective-permute-start.8 = (f32[8,128]{1,0:T(8,128)S(1)}, f32[8,128]{1,0:T(8,128)S(1)}, u32[]{:S(2)}, u32[]{:S(2)}) collective-permute-start(f32[8,128]{1,0:T(8,128)S(1)} %add.31.refs_4_), channel_id=1, source_target_pairs={{0,9},{1,8},{2,11},{3,10},{4,13},{5,12},{6,15},{7,14},{8,1},{9,0},... | collective-permute-start | bytes 12296 | tf_op jit(solution)/shard_map/ppermute | solution.py:164
  23.9 3.0 %collective-permute-start.9 = (f32[8,128]{1,0:T(8,128)S(1)}, f32[8,128]{1,0:T(8,128)S(1)}, u32[]{:S(2)}, u32[]{:S(2)}) collective-permute-start(f32[8,128]{1,0:T(8,128)S(1)} %add.31.refs_4_), channel_id=1, source_target_pairs={{0,5},{1,4},{2,7},{3,6},{4,1},{5,0},{6,3},{7,2},{8,13},{9,12},{10,... | collective-permute-start | bytes 12296 | tf_op jit(solution)/shard_map/ppermute | solution.py:164
  28.6 1.4 %collective-permute-start.11 = (f32[192,128]{1,0:T(8,128)S(1)}, f32[192,128]{1,0:T(8,128)S(1)}, u32[]{:S(2)}, u32[]{:S(2)}) collective-permute-start(f32[192,128]{1,0:T(8,128)S(1)} %get-tuple-element.19), channel_id=1, source_target_pairs={{0,1},{1,0},{2,3},{3,2},{4,5},{5,4},{6,7},{7,6},{8,9},{9,8},{10,11... | collective-permute-start | bytes 294920 | tf_op jit(solution)/shard_map/ppermute | solution.py:164
  30.0 5.2 %collective-permute-start.13 = (f32[64,128]{1,0:T(8,128)S(1)}, f32[64,128]{1,0:T(8,128)S(1)}, u32[]{:S(2)}, u32[]{:S(2)}) collective-permute-start(f32[64,128]{1,0:T(8,128)S(1)} %slice.29), channel_id=1, source_target_pairs={{0,13},{1,12},{2,15},{3,14},{4,9},{5,8},{6,11},{7,10},{8,5},{9,4},... | collective-permute-start | bytes 98312 | tf_op jit(solution)/shard_map/ppermute | solution.py:164
  32.1 5.1 %collective-permute-start.12 = (f32[128,128]{1,0:T(8,128)S(1)}, f32[128,128]{1,0:T(8,128)S(1)}, u32[]{:S(2)}, u32[]{:S(2)}) collective-permute-start(f32[128,128]{1,0:T(8,128)S(1)} %slice.28), channel_id=1, source_target_pairs={{0,5},{1,8},{2,7},{3,10},{4,1},{5,12},{6,3},{7,14},{8,13},{9,0},{1... | collective-permute-start | bytes 196616 | tf_op jit(solution)/shard_map/ppermute | solution.py:164
  37.2 1.3 %collective-permute-start.14 = (f32[128,128]{1,0:T(8,128)S(1)}, f32[128,128]{1,0:T(8,128)S(1)}, u32[]{:S(2)}, u32[]{:S(2)}) collective-permute-start(f32[128,128]{1,0:T(8,128)S(1)} %maximum_add_fusion), channel_id=1, source_target_pairs={{0,1},{1,0},{2,3},{3,2},{4,5},{5,4},{6,7},{7,6},{8,9},{9,8},{10,11... | collective-permute-start | bytes 196616 | tf_op jit(solution)/shard_map/ppermute | solution.py:164

commit v5 on v4

--- a/solution.py
+++ b/solution.py
@@ -91,51 +91,13 @@
         copy.wait()
 
 
-def own_kernel(dims, terms, theta, left_ref, right_ref, *refs):
-    *accs, words, inter = refs
-    picked = pick_entries(terms, words.at[0], *dims[:2])
-    for acc in accs:
-        acc[...] = jnp.zeros_like(acc)
-    apply_list(picked, theta[0], left_ref, right_ref, accs, inter.at[0], dims[2])
-
-
-def rest_kernel(dims, count, *refs):
-    lists = refs[:count]
-    thetas = refs[count:2 * count]
-    left_ref, right_ref = refs[2 * count:2 * count + 2]
-    starts = refs[2 * count + 2:2 * count + 2 + BLOCKS]
-    out, *accs, words, inter = refs[2 * count + 2 + BLOCKS:]
-    picked = [pick_entries(terms, words.at[i], *dims[:2]) for i, terms in enumerate(lists)]
-    for acc, start in zip(accs, starts):
-        acc[...] = start[...]
-    for i, theta in enumerate(thetas):
-        apply_list(picked[i], theta[0], left_ref, right_ref, accs, inter.at[i], dims[2])
-    for rows, acc in blocks(accs):
-        out[:, rows] = acc[...]
-
-
-def second_kernel(dims, nr, nl, chip_pair, elements, *refs):
-    lists = refs[:nr]
-    tiles = refs[nr:2 * nr]
-    sums = refs[2 * nr:2 * nr + nl]
-    left_ref, right_ref = refs[2 * nr + nl:2 * nr + nl + 2]
-    outs = refs[2 * nr + nl + 2:-2 - BLOCKS]
-    *accs, words, inter = refs[-2 - BLOCKS:]
-    picked = [pick_entries(terms, words.at[i], *dims[:2]) for i, terms in enumerate(lists)]
-    me = lax.axis_index("mpo")
-    total = sums[0][...]
-    for part in sums[1:]:
-        total = total + part[...]
-    scale = 1.0 / jnp.sqrt(jnp.sum(total, keepdims=True) / elements + 1e-06)
-    values = [t[...] for t in tiles]
-    if chip_pair:
-        values = [jnp.where(me == 0, values[1 - i], values[i]) for i in range(2)]
-    for acc in accs:
-        acc[...] = jnp.zeros_like(acc)
-    for i, value in enumerate(values):
-        vec = (value * scale).astype(jnp.bfloat16)
-        apply_list(picked[i], vec, left_ref, right_ref, accs, inter.at[i], dims[2])
-    if nl == 4:
+def fold_squares(value):
+    return jnp.sum((value * value).reshape(-1, 8, value.shape[-1]), axis=0)
+
+
+def emit(accs, outs):
+    if accs[0].shape[0] == 4:
+        me = lax.axis_index("mpo")
         own, keep, give = outs
         tile = own.shape[0]
         for rows, acc in blocks(accs):
@@ -148,9 +110,53 @@
             keep[rows] = jnp.where(me == 0, low[3], high[3])
             give[rows] = jnp.where(me == 0, high[3], low[3])
     else:
-        for s in range(nl):
+        for s, out in enumerate(outs):
             for rows, acc in blocks(accs):
-                outs[s][rows] = acc[s]
+                out[rows] = acc[s]
+
+
+def own_kernel(dims, terms, theta, left_ref, right_ref, *refs):
+    *accs, words, inter = refs
+    picked = pick_entries(terms, words.at[0], *dims[:2])
+    for acc in accs:
+        acc[...] = jnp.zeros_like(acc)
+    apply_list(picked, theta[0], left_ref, right_ref, accs, inter.at[0], dims[2])
+
+
+def rest_kernel(dims, count, *refs):
+    lists = refs[:count]
+    thetas = refs[count:2 * count]
+    left_ref, right_ref = refs[2 * count:2 * count + 2]
+    starts = refs[2 * count + 2:2 * count + 2 + BLOCKS]
+    outs = refs[2 * count + 2 + BLOCKS:-2 - BLOCKS]
+    *accs, words, inter = refs[-2 - BLOCKS:]
+    picked = [pick_entries(terms, words.at[i], *dims[:2]) for i, terms in enumerate(lists)]
+    for acc, start in zip(accs, starts):
+        acc[...] = start[...]
+    for i, theta in enumerate(thetas):
+        apply_list(picked[i], theta[0], left_ref, right_ref, accs, inter.at[i], dims[2])
+    emit(accs, outs)
+
+
+def second_kernel(dims, nr, count, elements, *refs):
+    lists = refs[:nr]
+    tiles = refs[nr:2 * nr]
+    sums = refs[2 * nr:2 * nr + count]
+    left_ref, right_ref = refs[2 * nr + count:2 * nr + count + 2]
+    outs = refs[2 * nr + count + 2:-2 - BLOCKS]
+    *accs, words, inter = refs[-2 - BLOCKS:]
+    picked = [pick_entries(terms, words.at[i], *dims[:2]) for i, terms in enumerate(lists)]
+    values = [t[...] for t in tiles]
+    total = sum(fold_squares(value) for value in values[1:])
+    for part in sums:
+        total = total + part[...]
+    scale = 1.0 / jnp.sqrt(jnp.sum(total, keepdims=True) / elements + 1e-06)
+    for acc in accs:
+        acc[...] = jnp.zeros_like(acc)
+    for i, value in enumerate(values):
+        vec = (value * scale).astype(jnp.bfloat16)
+        apply_list(picked[i], vec, left_ref, right_ref, accs, inter.at[i], dims[2])
+    emit(accs, outs)
 
 
 def permute(value, target):
@@ -172,18 +178,32 @@
     right_flat = right_env.reshape(-1, tile, tile)
     nl = lax.axis_size("left")
     nr = lax.axis_size("right")
-    chip_pair = nr == 2
     rows, fields = terms.shape[-2:]
     entries = jnp.transpose(terms, (0, 1, 4, 2, 3)).reshape(fields, 1, rows)
     dims = (lt_dev, rt_dev, CAP * nr == rows)
     swap_cores = lambda x: permute(x, lambda p, t, m: (p, t, 1 - m))
     lists = [entries] + [permute(entries, lambda p, t, m, s=s: (p, t ^ s, m)) for s in range(1, nr)]
     thetas = [theta] + [permute(theta, lambda p, t, m, s=s: (p, t ^ s, 1 - m)) for s in range(1, nr)]
-    stack = jax.ShapeDtypeStruct((nl, tile, tile), jnp.float32)
     part_shapes = [((nl, tile // BLOCKS, tile), jnp.float32)] * BLOCKS
     accs = [pltpu.VMEM(*shape) for shape in part_shapes]
     scratch = [pltpu.SMEM((nr, 2, rows + 1), jnp.int32), pltpu.VMEM((nr, CAP, tile, tile), jnp.bfloat16)]
     params = pltpu.CompilerParams(vmem_limit_bytes=32 << 20)
+
+    def reduce_tiles(parts):
+        half = parts[0]
+        if nl == 4:
+            _, keep, give = parts
+            chip = keep + swap_cores(give)
+            near = permute(chip[:tile], lambda p, t, m: (p ^ (1 + m), t, 1 - m))
+            far = permute(chip[tile:], lambda p, t, m: (p ^ 3, t, 1 - m))
+            first = lax.axis_index("mpo") == 1
+            none = jnp.zeros_like(far)
+            placed = jnp.concatenate([jnp.where(first, far, none), jnp.where(first, none, far)], axis=0)
+            half = half + near + placed
+        else:
+            for s in range(1, nl):
+                half = half + permute(parts[s], lambda p, t, m: (p ^ s, t, 1 - m))
+        return half
 
     left_flat, right_flat = pl.pallas_call(
         load_kernel,
@@ -203,61 +223,42 @@
         compiler_params=params,
         name="first_own",
     )(entries, theta, left_flat, right_flat)
-    part = pl.pallas_call(
+    flat = lambda rows: jax.ShapeDtypeStruct((rows, tile), jnp.float32)
+    out_shape = [flat(tile), flat(tile * 3 // 2), flat(tile * 3 // 2)] if nl == 4 else [flat(tile)] * nl
+    parts = pl.pallas_call(
         functools.partial(rest_kernel, dims, nr - 1),
-        out_shape=stack,
+        out_shape=out_shape,
         in_specs=[VMEM] * (2 * nr + BLOCKS),
-        out_specs=VMEM,
+        out_specs=[VMEM] * len(out_shape),
         scratch_shapes=accs + scratch,
         compiler_params=params,
         name="first_rest",
     )(*lists[1:], *thetas[1:], left_flat, right_flat, *own_parts)
 
-    chip = part + swap_cores(part)
-    if chip_pair:
-        mine = None
-        for s in [3, 1, 2, 0] if nl == 4 else range(nl):
-            got = permute(chip[s], lambda p, t, m: (p ^ s, t ^ m, 1 - m))
-            mine = got if mine is None else mine + got
-        other = swap_cores(mine)
-        tiles = [mine, other]
-        h_theta = jnp.where(lax.axis_index("mpo") == 1, mine, other)
+    half = reduce_tiles(parts)
+    halves = [permute(half, lambda p, t, m: (p, t ^ s, m)) for s in range(1, nr)]
+    h_theta = half + swap_cores(half)
+    neighbours = [x + swap_cores(x) for x in halves]
+    squares = fold_squares(h_theta)
+    if nr == 2:
+        sums = [permute(squares, lambda p, t, m: (p ^ s, t ^ m, m)) for s in range(1, nl)]
+        others = sum(sums[1:], sums[0])
+        sums = [squares, others, swap_cores(others)]
     else:
-        h_theta = chip[0]
-        for s in range(1, nl):
-            h_theta = h_theta + permute(chip[s], lambda p, t, m: (p ^ s, t, 1 - m))
-        tiles = [h_theta]
-        for s in range(1, nr):
-            tiles.append(permute(h_theta, lambda p, t, m: (p, t ^ s, 1 - m)))
-    squares = sum(jnp.sum((x * x).reshape(tile // 8, 8, tile), axis=0) for x in tiles)
-    sums = [squares]
-    for s in [2, 1, 3] if nl == 4 else range(1, nl):
-        sums.append(permute(squares, lambda p, t, m: (p ^ s, t, 1 - m)))
-
-    flat = lambda rows: jax.ShapeDtypeStruct((rows, tile), jnp.float32)
-    out_shape = [flat(tile), flat(tile * 3 // 2), flat(tile * 3 // 2)] if nl == 4 else [flat(tile)] * nl
+        row = squares + sum(fold_squares(x) for x in neighbours)
+        sums = [squares] + [permute(row, lambda p, t, m: (p ^ s, t, 1 - m)) for s in range(1, nl)]
+    tiles = [h_theta] + neighbours
+
     parts = pl.pallas_call(
-        functools.partial(second_kernel, dims, nr, nl, chip_pair, nl * nr * tile * tile),
+        functools.partial(second_kernel, dims, nr, len(sums), nl * nr * tile * tile),
         out_shape=out_shape,
-        in_specs=[VMEM] * (2 * nr + nl + 2),
+        in_specs=[VMEM] * (2 * nr + len(sums) + 2),
         out_specs=[VMEM] * len(out_shape),
         scratch_shapes=accs + scratch,
         compiler_params=params,
         name="second_product",
     )(*lists, *tiles, *sums, left_flat, right_flat)
-    half = parts[0]
-    if nl == 4:
-        _, keep, give = parts
-        chip = keep + swap_cores(give)
-        near = permute(chip[:tile], lambda p, t, m: (p ^ (1 + m), t, 1 - m))
-        far = permute(chip[tile:], lambda p, t, m: (p ^ 3, t, 1 - m))
-        first = lax.axis_index("mpo") == 1
-        none = jnp.zeros_like(far)
-        placed = jnp.concatenate([jnp.where(first, far, none), jnp.where(first, none, far)], axis=0)
-        half = half + near + placed
-    else:
-        for s in range(1, nl):
-            half = half + permute(parts[s], lambda p, t, m: (p ^ s, t, 1 - m))
+    half = reduce_tiles(parts)
     h_second = half + swap_cores(half)
     return h_theta[None], h_second[None]
 

time: 39.3 us -> 38 us (0.967)
  waiting for transfers between devices: 16.8 us -> 14.5 us
  starting transfers between devices: 15.1 us -> 16.7 us
  other arithmetic: 1.39 us -> 0.74 us
    ppermute x15 -> x16, waiting for transfers between devices: 16.8 us -> 14.5 us  [permute(): return lax.ppermute(value, ('left', 'right', 'mpo'), pairs)]
    ppermute x15 -> x16, starting transfers between devices: 15.1 us -> 16.7 us  [permute(): return lax.ppermute(value, ('left', 'right', 'mpo'), pairs)]
    broadcast_in_dim x2 -> x1, other arithmetic: 1.28 us -> 0.64 us  [local(): return (h_theta[None], h_second[None])]
  transfers between devices with their start and end apart: 15 -> 16, of which waited for: 14 -> 12; matrix products, arithmetic and copies ran while one was open for 2% -> 0% of each run, Pallas kernels for 7% -> 7%
where the time goes in v5:
time: 38 us; the launch traced here: 37.9 us
  starting transfers between devices  16.7 us (44%)
  waiting for transfers between devices  14.5 us (38%)
  Pallas kernels  5.16 us (14%)
  other arithmetic  0.74 us (2%)
  between operations  0.74 us (2%)
    ppermute x16, starting transfers between devices, permute(): return lax.ppermute(value, ('left', 'right', 'mpo'), pairs)  16.7 us
    ppermute x16, waiting for transfers between devices, permute(): return lax.ppermute(value, ('left', 'right', 'mpo'), pairs)  14.5 us
    pallas_call x1, Pallas kernels, local(): pl.pallas_call(functools.partial(second_kernel, dims, nr, len(sums), nl *...  1.62 us
    pallas_call x1, Pallas kernels, local(): pl.pallas_call(load_kernel, out_shape=[jax.ShapeDtypeStruct(x.shape, x.dt...  1.56 us
    pallas_call x1, Pallas kernels, local(): pl.pallas_call(functools.partial(own_kernel, dims), out_shape=[jax.ShapeD...  1 us
    pallas_call x1, Pallas kernels, local(): pl.pallas_call(functools.partial(rest_kernel, dims, nr - 1), out_shape=ou...  0.97 us
  transfers between devices with their start and end apart: 16, of which 12 were waited for; matrix products, arithmetic and copies ran while one was open for 0% of the time, Pallas kernels for 7%

profile of v5, /device:TPU:0, one launch (start us, length us, event | category | flops | bytes accessed | tf_op | source)
XLA Modules:
  0.0 37.9 jit_solution(7686777224594901273)
XLA Ops:
  0.6 2.4 %collective-permute-start.1 = (bf16[1,128,128]{2,1,0:T(8,128)(2,1)}, bf16[1,128,128]{2,1,0:T(8,128)(2,1)S(1)}, u32[]{:S(2)}, u32[]{:S(2)}) collective-permute-start(bf16[1,128,128]{2,1,0:T(8,128)(2,1)} %theta.1), channel_id=1, source_target_pairs={{0,3},{1,2},{2,1},{3,0},{4,7},{5,6},{6,5},{7,4},{8,11},{9,10},{10,... | collective-permute-start | bytes 98312 | tf_op jit(solution)/shard_map/ppermute | solution.py:170
  3.1 0.6 %collective-permute-start = (s32[14,1,16]{2,1,0:T(1,128)}, s32[14,1,16]{2,1,0:T(1,128)S(1)}, u32[]{:S(2)}, u32[]{:S(2)}) collective-permute-start(s32[14,1,16]{2,1,0:T(1,128)} %bitcast.11), channel_id=1, source_target_pairs={{0,2},{1,3},{2,0},{3,1},{4,6},{5,7},{6,4},{7,5},{8,10},{9,11},{10,... | collective-permute-start | bytes 2696 | tf_op jit(solution)/shard_map/ppermute | solution.py:170
  3.7 1.6 %load.1 = (bf16[32,128,128]{2,1,0:T(8,128)(2,1)S(1)}, bf16[32,128,128]{2,1,0:T(8,128)(2,1)S(1)}) custom-call(bf16[32,128,128]{2,1,0:T(8,128)(2,1)} %bitcast.14, bf16[32,128,128]{2,1,0:T(8,128)(2,1)} %bitcast.15), custom_call_target="tpu_custom_call" | custom-call | tf_op jit(solution)/shard_map/load/pallas_call | solution.py:208
  5.3 1.0 %first_own.1 = (f32[4,32,128]{2,1,0:T(8,128)S(1)}, f32[4,32,128]{2,1,0:T(8,128)S(1)}, f32[4,32,128]{2,1,0:T(8,128)S(1)}, f32[4,32,128]{2,1,0:T(8,128)S(1)}) custom-call(s32[14,1,16]{2,1,0:T(1,128)S(1)} %bitcast.12, bf16[1,128,128]{2,1,0:T(8,128)(2,1)S(1)} %copy-done.1, bf16[32,128,128]{2,1,0:T(8,128)(2,1)S(1)} %get-tuple-element.14.left_ref.refs_2_.refs_7_, ...), custom_call_target="tpu_custom_call" | custom-call | tf_op jit(solution)/shard_map/first_own/pallas_call | solution.py:217
  6.9 1.0 %first_rest.1 = (f32[128,128]{1,0:T(8,128)S(1)}, f32[192,128]{1,0:T(8,128)S(1)}, f32[192,128]{1,0:T(8,128)S(1)}) custom-call(s32[14,1,16]{2,1,0:T(1,128)S(1)} %collective-permute-done.refs_0_.refs_1_, bf16[1,128,128]{2,1,0:T(8,128)(2,1)S(1)} %collective-permute-done.1.refs_1_, bf16[32,128,128]{2,1,0:T(8,128)(2,1)S(1)} %get-tuple-element.14.left_ref.refs_2_.refs_7_, ...), custom_call_target="tpu_custom_call" | custom-call | tf_op jit(solution)/shard_map/first_rest/pallas_call | solution.py:228
  8.0 1.3 %collective-permute-done.2 = f32[192,128]{1,0:T(8,128)S(1)} collective-permute-done((f32[192,128]{1,0:T(8,128)S(1)}, f32[192,128]{1,0:T(8,128)S(1)}, u32[]{:S(2)}, u32[]{:S(2)}) %collective-permute-start.2) | collective-permute-done | bytes 98336 | tf_op jit(solution)/shard_map/ppermute | solution.py:170
  9.3 3.4 %collective-permute-start.4 = (f32[64,128]{1,0:T(8,128)S(1)}, f32[64,128]{1,0:T(8,128)S(1)}, u32[]{:S(2)}, u32[]{:S(2)}) collective-permute-start(f32[64,128]{1,0:T(8,128)S(1)} %slice.17), channel_id=1, source_target_pairs={{0,13},{1,12},{2,15},{3,14},{4,9},{5,8},{6,11},{7,10},{8,5},{9,4},... | collective-permute-start | bytes 98312 | tf_op jit(solution)/shard_map/ppermute | solution.py:170
  12.8 1.8 %collective-permute-done.4 = f32[64,128]{1,0:T(8,128)S(1)} collective-permute-done((f32[64,128]{1,0:T(8,128)S(1)}, f32[64,128]{1,0:T(8,128)S(1)}, u32[]{:S(2)}, u32[]{:S(2)}) %collective-permute-start.4) | collective-permute-done | bytes 32800 | tf_op jit(solution)/shard_map/ppermute | solution.py:170
  14.5 2.9 %collective-permute-done.3 = f32[128,128]{1,0:T(8,128)S(1)} collective-permute-done((f32[128,128]{1,0:T(8,128)S(1)}, f32[128,128]{1,0:T(8,128)S(1)}, u32[]{:S(2)}, u32[]{:S(2)}) %collective-permute-start.3) | collective-permute-done | bytes 65568 | tf_op jit(solution)/shard_map/ppermute | solution.py:170
  17.6 1.0 %collective-permute-start.6 = (f32[128,128]{1,0:T(8,128)S(1)}, f32[128,128]{1,0:T(8,128)S(1)}, u32[]{:S(2)}, u32[]{:S(2)}) collective-permute-start(f32[128,128]{1,0:T(8,128)S(1)} %maximum_add_fusion), channel_id=1, source_target_pairs={{0,2},{1,3},{2,0},{3,1},{4,6},{5,7},{6,4},{7,5},{8,10},{9,11},{10,... | collective-permute-start | bytes 196616 | tf_op jit(solution)/shard_map/ppermute | solution.py:170
  18.8 1.0 %collective-permute-start.10 = (f32[8,128]{1,0:T(8,128)S(1)}, f32[8,128]{1,0:T(8,128)S(1)}, u32[]{:S(2)}, u32[]{:S(2)}) collective-permute-start(f32[8,128]{1,0:T(8,128)S(1)} %get-tuple-element.26.refs_4_), channel_id=1, source_target_pairs={{0,12},{1,15},{2,14},{3,13},{4,8},{5,11},{6,10},{7,9},{8,4},{9,7},... | collective-permute-start | bytes 12296 | tf_op jit(solution)/shard_map/ppermute | solution.py:170
  19.8 0.8 %collective-permute-start.8 = (f32[8,128]{1,0:T(8,128)S(1)}, f32[8,128]{1,0:T(8,128)S(1)}, u32[]{:S(2)}, u32[]{:S(2)}) collective-permute-start(f32[8,128]{1,0:T(8,128)S(1)} %get-tuple-element.26.refs_4_), channel_id=1, source_target_pairs={{0,4},{1,7},{2,6},{3,5},{4,0},{5,3},{6,2},{7,1},{8,12},{9,15},{10,... | collective-permute-start | bytes 12296 | tf_op jit(solution)/shard_map/ppermute | solution.py:170
  20.6 2.6 %collective-permute-start.9 = (f32[8,128]{1,0:T(8,128)S(1)}, f32[8,128]{1,0:T(8,128)S(1)}, u32[]{:S(2)}, u32[]{:S(2)}) collective-permute-start(f32[8,128]{1,0:T(8,128)S(1)} %get-tuple-element.26.refs_4_), channel_id=1, source_target_pairs={{0,8},{1,11},{2,10},{3,9},{4,12},{5,15},{6,14},{7,13},{8,0},{9,3},... | collective-permute-start | bytes 12296 | tf_op jit(solution)/shard_map/ppermute | solution.py:170
  23.3 0.6 %collective-permute-start.7 = (f32[128,128]{1,0:T(8,128)S(1)}, f32[128,128]{1,0:T(8,128)S(1)}, u32[]{:S(2)}, u32[]{:S(2)}) collective-permute-start(f32[128,128]{1,0:T(8,128)S(1)} %collective-permute-done.6), channel_id=1, source_target_pairs={{0,1},{1,0},{2,3},{3,2},{4,5},{5,4},{6,7},{7,6},{8,9},{9,8},{10,11... | collective-permute-start | bytes 196616 | tf_op jit(solution)/shard_map/ppermute | solution.py:170
  24.3 0.9 %collective-permute-done.9 = f32[8,128]{1,0:T(8,128)S(1)} collective-permute-done((f32[8,128]{1,0:T(8,128)S(1)}, f32[8,128]{1,0:T(8,128)S(1)}, u32[]{:S(2)}, u32[]{:S(2)}) %collective-permute-start.9) | collective-permute-done | bytes 4128 | tf_op jit(solution)/shard_map/ppermute | solution.py:170
  25.4 0.9 %collective-permute-done.11.refs_6_ = f32[8,128]{1,0:T(8,128)S(1)} collective-permute-done((f32[8,128]{1,0:T(8,128)S(1)}, f32[8,128]{1,0:T(8,128)S(1)}, u32[]{:S(2)}, u32[]{:S(2)}) %collective-permute-start.11) | collective-permute-done | bytes 4128 | tf_op jit(solution)/shard_map/ppermute | solution.py:170
  26.3 1.6 %second_product.1 = (f32[128,128]{1,0:T(8,128)S(1)}, f32[192,128]{1,0:T(8,128)S(1)}, f32[192,128]{1,0:T(8,128)S(1)}) custom-call(s32[14,1,16]{2,1,0:T(1,128)S(1)} %bitcast.13, s32[14,1,16]{2,1,0:T(1,128)S(1)} %collective-permute-done.refs_0_.refs_1_, f32[128,128]{1,0:T(8,128)S(1)} %get-tuple-element.27.refs_2_, f32[128,128]{1,0:T(8,128)S(1)} %add.37.refs_3_, ...), custom_call_target="tpu_custom_call" | custom-call | tf_op jit(solution)/shard_map/second_product/pallas_call | solution.py:252
  28.2 1.1 %collective-permute-done.12 = f32[192,128]{1,0:T(8,128)S(1)} collective-permute-done((f32[192,128]{1,0:T(8,128)S(1)}, f32[192,128]{1,0:T(8,128)S(1)}, u32[]{:S(2)}, u32[]{:S(2)}) %collective-permute-start.12) | collective-permute-done | bytes 98336 | tf_op jit(solution)/shard_map/ppermute | solution.py:170
  29.3 1.9 %collective-permute-start.14 = (f32[64,128]{1,0:T(8,128)S(1)}, f32[64,128]{1,0:T(8,128)S(1)}, u32[]{:S(2)}, u32[]{:S(2)}) collective-permute-start(f32[64,128]{1,0:T(8,128)S(1)} %slice.19), channel_id=1, source_target_pairs={{0,13},{1,12},{2,15},{3,14},{4,9},{5,8},{6,11},{7,10},{8,5},{9,4},... | collective-permute-start | bytes 98312 | tf_op jit(solution)/shard_map/ppermute | solution.py:170
  31.2 1.1 %collective-permute-start.13 = (f32[128,128]{1,0:T(8,128)S(1)}, f32[128,128]{1,0:T(8,128)S(1)}, u32[]{:S(2)}, u32[]{:S(2)}) collective-permute-start(f32[128,128]{1,0:T(8,128)S(1)} %slice.18), channel_id=1, source_target_pairs={{0,5},{1,8},{2,7},{3,10},{4,1},{5,12},{6,3},{7,14},{8,13},{9,0},{1... | collective-permute-start | bytes 196616 | tf_op jit(solution)/shard_map/ppermute | solution.py:170
  32.3 2.2 %collective-permute-done.14 = f32[64,128]{1,0:T(8,128)S(1)} collective-permute-done((f32[64,128]{1,0:T(8,128)S(1)}, f32[64,128]{1,0:T(8,128)S(1)}, u32[]{:S(2)}, u32[]{:S(2)}) %collective-permute-start.14) | collective-permute-done | bytes 32800 | tf_op jit(solution)/shard_map/ppermute | solution.py:170
  34.6 1.3 %collective-permute-done.13 = f32[128,128]{1,0:T(8,128)S(1)} collective-permute-done((f32[128,128]{1,0:T(8,128)S(1)}, f32[128,128]{1,0:T(8,128)S(1)}, u32[]{:S(2)}, u32[]{:S(2)}) %collective-permute-start.13) | collective-permute-done | bytes 65568 | tf_op jit(solution)/shard_map/ppermute | solution.py:170
  36.2 1.0 %collective-permute-done.15 = f32[128,128]{1,0:T(8,128)S(1)} collective-permute-done((f32[128,128]{1,0:T(8,128)S(1)}, f32[128,128]{1,0:T(8,128)S(1)}, u32[]{:S(2)}, u32[]{:S(2)}) %collective-permute-start.15) | collective-permute-done | bytes 65568 | tf_op jit(solution)/shard_map/ppermute | solution.py:170
  37.2 0.6 %add_bitcast_fusion = f32[1,128,128]{2,1,0:T(8,128)} fusion(f32[128,128]{1,0:T(8,128)S(1)} %maximum_add_fusion.1, f32[128,128]{1,0:T(8,128)S(1)} %collective-permute-done.15), kind=kLoop, calls=%fused_computation.3 | loop fusion | flops 16384 | bytes 196608 | tf_op jit(solution)/shard_map/broadcast_in_dim | solution.py:263
  (32 shorter events, 2.4 us)
Async XLA Ops:
  0.6 6.3 %collective-permute-start.1 = (bf16[1,128,128]{2,1,0:T(8,128)(2,1)}, bf16[1,128,128]{2,1,0:T(8,128)(2,1)S(1)}, u32[]{:S(2)}, u32[]{:S(2)}) collective-permute-start(bf16[1,128,128]{2,1,0:T(8,128)(2,1)} %theta.1), channel_id=1, source_target_pairs={{0,3},{1,2},{2,1},{3,0},{4,7},{5,6},{6,5},{7,4},{8,11},{9,10},{10,... | collective-permute-start | bytes 98312 | tf_op jit(solution)/shard_map/ppermute | solution.py:170
  3.1 3.9 %collective-permute-start = (s32[14,1,16]{2,1,0:T(1,128)}, s32[14,1,16]{2,1,0:T(1,128)S(1)}, u32[]{:S(2)}, u32[]{:S(2)}) collective-permute-start(s32[14,1,16]{2,1,0:T(1,128)} %bitcast.11), channel_id=1, source_target_pairs={{0,2},{1,3},{2,0},{3,1},{4,6},{5,7},{6,4},{7,5},{8,10},{9,11},{10,... | collective-permute-start | bytes 2696 | tf_op jit(solution)/shard_map/ppermute | solution.py:170
  3.7 1.6 %copy-start.1 = (bf16[1,128,128]{2,1,0:T(8,128)(2,1)S(1)}, bf16[1,128,128]{2,1,0:T(8,128)(2,1)}, u32[]{:S(2)}) copy-start(bf16[1,128,128]{2,1,0:T(8,128)(2,1)} %theta.1) | copy-start | bytes 98308
  3.7 1.6 %copy-start.2 = (s32[1,1,1,16,14]{3,2,4,1,0:T(1,128)S(1)}, s32[1,1,1,16,14]{3,2,4,1,0:T(1,128)}, u32[]{:S(2)}) copy-start(s32[1,1,1,16,14]{3,2,4,1,0:T(1,128)} %param.7) | copy-start | bytes 2692
  7.9 1.4 %collective-permute-start.2 = (f32[192,128]{1,0:T(8,128)S(1)}, f32[192,128]{1,0:T(8,128)S(1)}, u32[]{:S(2)}, u32[]{:S(2)}) collective-permute-start(f32[192,128]{1,0:T(8,128)S(1)} %get-tuple-element.22), channel_id=1, source_target_pairs={{0,1},{1,0},{2,3},{3,2},{4,5},{5,4},{6,7},{7,6},{8,9},{9,8},{10,11... | collective-permute-start | bytes 294920 | tf_op jit(solution)/shard_map/ppermute | solution.py:170
  9.3 5.2 %collective-permute-start.4 = (f32[64,128]{1,0:T(8,128)S(1)}, f32[64,128]{1,0:T(8,128)S(1)}, u32[]{:S(2)}, u32[]{:S(2)}) collective-permute-start(f32[64,128]{1,0:T(8,128)S(1)} %slice.17), channel_id=1, source_target_pairs={{0,13},{1,12},{2,15},{3,14},{4,9},{5,8},{6,11},{7,10},{8,5},{9,4},... | collective-permute-start | bytes 98312 | tf_op jit(solution)/shard_map/ppermute | solution.py:170
  12.7 4.7 %collective-permute-start.3 = (f32[128,128]{1,0:T(8,128)S(1)}, f32[128,128]{1,0:T(8,128)S(1)}, u32[]{:S(2)}, u32[]{:S(2)}) collective-permute-start(f32[128,128]{1,0:T(8,128)S(1)} %slice.16), channel_id=1, source_target_pairs={{0,5},{1,8},{2,7},{3,10},{4,1},{5,12},{6,3},{7,14},{8,13},{9,0},{1... | collective-permute-start | bytes 196616 | tf_op jit(solution)/shard_map/ppermute | solution.py:170
  17.5 1.3 %collective-permute-start.5 = (f32[128,128]{1,0:T(8,128)S(1)}, f32[128,128]{1,0:T(8,128)S(1)}, u32[]{:S(2)}, u32[]{:S(2)}) collective-permute-start(f32[128,128]{1,0:T(8,128)S(1)} %maximum_add_fusion), channel_id=1, source_target_pairs={{0,1},{1,0},{2,3},{3,2},{4,5},{5,4},{6,7},{7,6},{8,9},{9,8},{10,11... | collective-permute-start | bytes 196616 | tf_op jit(solution)/shard_map/ppermute | solution.py:170
  17.6 5.7 %collective-permute-start.6 = (f32[128,128]{1,0:T(8,128)S(1)}, f32[128,128]{1,0:T(8,128)S(1)}, u32[]{:S(2)}, u32[]{:S(2)}) collective-permute-start(f32[128,128]{1,0:T(8,128)S(1)} %maximum_add_fusion), channel_id=1, source_target_pairs={{0,2},{1,3},{2,0},{3,1},{4,6},{5,7},{6,4},{7,5},{8,10},{9,11},{10,... | collective-permute-start | bytes 196616 | tf_op jit(solution)/shard_map/ppermute | solution.py:170
  18.8 7.5 %copy-start = (f32[128,128]{1,0:T(8,128)}, f32[128,128]{1,0:T(8,128)S(1)}, u32[]{:S(2)}) copy-start(f32[128,128]{1,0:T(8,128)S(1)} %get-tuple-element.27.refs_2_) | copy-start | bytes 196612
  18.8 5.5 %collective-permute-start.10 = (f32[8,128]{1,0:T(8,128)S(1)}, f32[8,128]{1,0:T(8,128)S(1)}, u32[]{:S(2)}, u32[]{:S(2)}) collective-permute-start(f32[8,128]{1,0:T(8,128)S(1)} %get-tuple-element.26.refs_4_), channel_id=1, source_target_pairs={{0,12},{1,15},{2,14},{3,13},{4,8},{5,11},{6,10},{7,9},{8,4},{9,7},... | collective-permute-start | bytes 12296 | tf_op jit(solution)/shard_map/ppermute | solution.py:170
  19.8 4.5 %collective-permute-start.8 = (f32[8,128]{1,0:T(8,128)S(1)}, f32[8,128]{1,0:T(8,128)S(1)}, u32[]{:S(2)}, u32[]{:S(2)}) collective-permute-start(f32[8,128]{1,0:T(8,128)S(1)} %get-tuple-element.26.refs_4_), channel_id=1, source_target_pairs={{0,4},{1,7},{2,6},{3,5},{4,0},{5,3},{6,2},{7,1},{8,12},{9,15},{10,... | collective-permute-start | bytes 12296 | tf_op jit(solution)/shard_map/ppermute | solution.py:170
  20.6 4.5 %collective-permute-start.9 = (f32[8,128]{1,0:T(8,128)S(1)}, f32[8,128]{1,0:T(8,128)S(1)}, u32[]{:S(2)}, u32[]{:S(2)}) collective-permute-start(f32[8,128]{1,0:T(8,128)S(1)} %get-tuple-element.26.refs_4_), channel_id=1, source_target_pairs={{0,8},{1,11},{2,10},{3,9},{4,12},{5,15},{6,14},{7,13},{8,0},{9,3},... | collective-permute-start | bytes 12296 | tf_op jit(solution)/shard_map/ppermute | solution.py:170
  23.3 2.1 %collective-permute-start.7 = (f32[128,128]{1,0:T(8,128)S(1)}, f32[128,128]{1,0:T(8,128)S(1)}, u32[]{:S(2)}, u32[]{:S(2)}) collective-permute-start(f32[128,128]{1,0:T(8,128)S(1)} %collective-permute-done.6), channel_id=1, source_target_pairs={{0,1},{1,0},{2,3},{3,2},{4,5},{5,4},{6,7},{7,6},{8,9},{9,8},{10,11... | collective-permute-start | bytes 196616 | tf_op jit(solution)/shard_map/ppermute | solution.py:170
  25.2 1.2 %collective-permute-start.11 = (f32[8,128]{1,0:T(8,128)S(1)}, f32[8,128]{1,0:T(8,128)S(1)}, u32[]{:S(2)}, u32[]{:S(2)}) collective-permute-start(f32[8,128]{1,0:T(8,128)S(1)} %add_add_fusion.refs_5_), channel_id=1, source_target_pairs={{0,1},{1,0},{2,3},{3,2},{4,5},{5,4},{6,7},{7,6},{8,9},{9,8},{10,11... | collective-permute-start | bytes 12296 | tf_op jit(solution)/shard_map/ppermute | solution.py:170
  28.0 1.4 %collective-permute-start.12 = (f32[192,128]{1,0:T(8,128)S(1)}, f32[192,128]{1,0:T(8,128)S(1)}, u32[]{:S(2)}, u32[]{:S(2)}) collective-permute-start(f32[192,128]{1,0:T(8,128)S(1)} %get-tuple-element.25), channel_id=1, source_target_pairs={{0,1},{1,0},{2,3},{3,2},{4,5},{5,4},{6,7},{7,6},{8,9},{9,8},{10,11... | collective-permute-start | bytes 294920 | tf_op jit(solution)/shard_map/ppermute | solution.py:170
  29.3 5.2 %collective-permute-start.14 = (f32[64,128]{1,0:T(8,128)S(1)}, f32[64,128]{1,0:T(8,128)S(1)}, u32[]{:S(2)}, u32[]{:S(2)}) collective-permute-start(f32[64,128]{1,0:T(8,128)S(1)} %slice.19), channel_id=1, source_target_pairs={{0,13},{1,12},{2,15},{3,14},{4,9},{5,8},{6,11},{7,10},{8,5},{9,4},... | collective-permute-start | bytes 98312 | tf_op jit(solution)/shard_map/ppermute | solution.py:170
  31.2 4.6 %collective-permute-start.13 = (f32[128,128]{1,0:T(8,128)S(1)}, f32[128,128]{1,0:T(8,128)S(1)}, u32[]{:S(2)}, u32[]{:S(2)}) collective-permute-start(f32[128,128]{1,0:T(8,128)S(1)} %slice.18), channel_id=1, source_target_pairs={{0,5},{1,8},{2,7},{3,10},{4,1},{5,12},{6,3},{7,14},{8,13},{9,0},{1... | collective-permute-start | bytes 196616 | tf_op jit(solution)/shard_map/ppermute | solution.py:170
  35.9 1.3 %collective-permute-start.15 = (f32[128,128]{1,0:T(8,128)S(1)}, f32[128,128]{1,0:T(8,128)S(1)}, u32[]{:S(2)}, u32[]{:S(2)}) collective-permute-start(f32[128,128]{1,0:T(8,128)S(1)} %maximum_add_fusion.1), channel_id=1, source_target_pairs={{0,1},{1,0},{2,3},{3,2},{4,5},{5,4},{6,7},{7,6},{8,9},{9,8},{10,11... | collective-permute-start | bytes 196616 | tf_op jit(solution)/shard_map/ppermute | solution.py:170

commit v6 on v5

--- a/solution.py
+++ b/solution.py
@@ -96,23 +96,13 @@
 
 
 def emit(accs, outs):
+    me = lax.axis_index("mpo")
+    offsets = range(len(outs))
     if accs[0].shape[0] == 4:
-        me = lax.axis_index("mpo")
-        own, keep, give = outs
-        tile = own.shape[0]
+        offsets = (0, 2 - me, 1 + me, 3)
+    for s, out in zip(offsets, outs):
         for rows, acc in blocks(accs):
-            own[rows] = acc[0]
-            keep[rows] = acc[1 + me]
-            give[rows] = acc[2 - me]
-        half = len(accs) // 2
-        for (rows, low), (_, high) in zip(blocks(accs[:half]), blocks(accs[half:])):
-            rows = slice(tile + rows.start, tile + rows.stop)
-            keep[rows] = jnp.where(me == 0, low[3], high[3])
-            give[rows] = jnp.where(me == 0, high[3], low[3])
-    else:
-        for s, out in enumerate(outs):
-            for rows, acc in blocks(accs):
-                out[rows] = acc[s]
+            out[rows] = acc[s]
 
 
 def own_kernel(dims, terms, theta, left_ref, right_ref, *refs):
@@ -192,14 +182,10 @@
     def reduce_tiles(parts):
         half = parts[0]
         if nl == 4:
-            _, keep, give = parts
-            chip = keep + swap_cores(give)
-            near = permute(chip[:tile], lambda p, t, m: (p ^ (1 + m), t, 1 - m))
-            far = permute(chip[tile:], lambda p, t, m: (p ^ 3, t, 1 - m))
-            first = lax.axis_index("mpo") == 1
-            none = jnp.zeros_like(far)
-            placed = jnp.concatenate([jnp.where(first, far, none), jnp.where(first, none, far)], axis=0)
-            half = half + near + placed
+            _, keep, give, far = parts
+            far = permute(far, lambda p, t, m: (p ^ 3, t, 1 - m))
+            near = permute(keep + swap_cores(give), lambda p, t, m: (p ^ (2 - m), t, 1 - m))
+            half = half + near + far
         else:
             for s in range(1, nl):
                 half = half + permute(parts[s], lambda p, t, m: (p ^ s, t, 1 - m))
@@ -223,8 +209,7 @@
         compiler_params=params,
         name="first_own",
     )(entries, theta, left_flat, right_flat)
-    flat = lambda rows: jax.ShapeDtypeStruct((rows, tile), jnp.float32)
-    out_shape = [flat(tile), flat(tile * 3 // 2), flat(tile * 3 // 2)] if nl == 4 else [flat(tile)] * nl
+    out_shape = [jax.ShapeDtypeStruct((tile, tile), jnp.float32)] * nl
     parts = pl.pallas_call(
         functools.partial(rest_kernel, dims, nr - 1),
         out_shape=out_shape,

time: 38 us -> 37.1 us (0.976)
  waiting for transfers between devices: 14.5 us -> 12.4 us
  starting transfers between devices: 16.7 us -> 18 us
    ppermute x16, waiting for transfers between devices: 14.5 us -> 12.4 us  [permute(): return lax.ppermute(value, ('left', 'right', 'mpo'), pairs)]
    ppermute x16, starting transfers between devices: 16.7 us -> 18 us  [permute(): return lax.ppermute(value, ('left', 'right', 'mpo'), pairs)]
  transfers between devices with their start and end apart: 16 -> 16, of which waited for: 12 -> 9; matrix products, arithmetic and copies ran while one was open for 0% -> 0% of each run, Pallas kernels for 7% -> 7%
where the time goes in v6:
time: 37.1 us; the launch traced here: 37 us
  starting transfers between devices  18 us (49%)
  waiting for transfers between devices  12.4 us (33%)
  Pallas kernels  5.11 us (14%)
  between operations  0.74 us (2%)
  other arithmetic  0.72 us (2%)
    ppermute x16, starting transfers between devices, permute(): return lax.ppermute(value, ('left', 'right', 'mpo'), pairs)  18 us
    ppermute x16, waiting for transfers between devices, permute(): return lax.ppermute(value, ('left', 'right', 'mpo'), pairs)  12.4 us
    pallas_call x1, Pallas kernels, local(): pl.pallas_call(functools.partial(second_kernel, dims, nr, len(sums), nl *...  1.59 us
    pallas_call x1, Pallas kernels, local(): pl.pallas_call(load_kernel, out_shape=[jax.ShapeDtypeStruct(x.shape, x.dt...  1.56 us
    pallas_call x1, Pallas kernels, local(): pl.pallas_call(functools.partial(own_kernel, dims), out_shape=[jax.ShapeD...  0.99 us
    pallas_call x1, Pallas kernels, local(): pl.pallas_call(functools.partial(rest_kernel, dims, nr - 1), out_shape=ou...  0.96 us
  transfers between devices with their start and end apart: 16, of which 9 were waited for; matrix products, arithmetic and copies ran while one was open for 0% of the time, Pallas kernels for 7%

profile of v6, /device:TPU:0, one launch (start us, length us, event | category | flops | bytes accessed | tf_op | source)
XLA Modules:
  0.0 37.0 jit_solution(11621587006931747743)
XLA Ops:
  0.6 2.4 %collective-permute-start.1 = (bf16[1,128,128]{2,1,0:T(8,128)(2,1)}, bf16[1,128,128]{2,1,0:T(8,128)(2,1)S(1)}, u32[]{:S(2)}, u32[]{:S(2)}) collective-permute-start(bf16[1,128,128]{2,1,0:T(8,128)(2,1)} %theta.1), channel_id=1, source_target_pairs={{0,3},{1,2},{2,1},{3,0},{4,7},{5,6},{6,5},{7,4},{8,11},{9,10},{10,... | collective-permute-start | bytes 98312 | tf_op jit(solution)/shard_map/ppermute | solution.py:160
  3.1 0.6 %collective-permute-start = (s32[14,1,16]{2,1,0:T(1,128)}, s32[14,1,16]{2,1,0:T(1,128)S(1)}, u32[]{:S(2)}, u32[]{:S(2)}) collective-permute-start(s32[14,1,16]{2,1,0:T(1,128)} %bitcast.11), channel_id=1, source_target_pairs={{0,2},{1,3},{2,0},{3,1},{4,6},{5,7},{6,4},{7,5},{8,10},{9,11},{10,... | collective-permute-start | bytes 2696 | tf_op jit(solution)/shard_map/ppermute | solution.py:160
  3.7 1.6 %load.1 = (bf16[32,128,128]{2,1,0:T(8,128)(2,1)S(1)}, bf16[32,128,128]{2,1,0:T(8,128)(2,1)S(1)}) custom-call(bf16[32,128,128]{2,1,0:T(8,128)(2,1)} %bitcast.14, bf16[32,128,128]{2,1,0:T(8,128)(2,1)} %bitcast.15), custom_call_target="tpu_custom_call" | custom-call | tf_op jit(solution)/shard_map/load/pallas_call | solution.py:194
  5.3 1.0 %first_own.1 = (f32[4,32,128]{2,1,0:T(8,128)S(1)}, f32[4,32,128]{2,1,0:T(8,128)S(1)}, f32[4,32,128]{2,1,0:T(8,128)S(1)}, f32[4,32,128]{2,1,0:T(8,128)S(1)}) custom-call(s32[14,1,16]{2,1,0:T(1,128)S(1)} %bitcast.12, bf16[1,128,128]{2,1,0:T(8,128)(2,1)S(1)} %copy-done.1, bf16[32,128,128]{2,1,0:T(8,128)(2,1)S(1)} %get-tuple-element.16.left_ref.refs_2_.refs_7_, ...), custom_call_target="tpu_custom_call" | custom-call | tf_op jit(solution)/shard_map/first_own/pallas_call | solution.py:203
  6.3 0.6 %collective-permute-done.refs_0_.refs_1_ = s32[14,1,16]{2,1,0:T(1,128)S(1)} collective-permute-done((s32[14,1,16]{2,1,0:T(1,128)}, s32[14,1,16]{2,1,0:T(1,128)S(1)}, u32[]{:S(2)}, u32[]{:S(2)}) %collective-permute-start) | collective-permute-done | bytes 928 | tf_op jit(solution)/shard_map/ppermute | solution.py:160
  6.9 1.0 %first_rest.1 = (f32[128,128]{1,0:T(8,128)S(1)}, f32[128,128]{1,0:T(8,128)S(1)}, f32[128,128]{1,0:T(8,128)S(1)}, f32[128,128]{1,0:T(8,128)S(1)}) custom-call(s32[14,1,16]{2,1,0:T(1,128)S(1)} %collective-permute-done.refs_0_.refs_1_, bf16[1,128,128]{2,1,0:T(8,128)(2,1)S(1)} %collective-permute-done.1.refs_1_, ...), custom_call_target="tpu_custom_call" | custom-call | tf_op jit(solution)/shard_map/first_rest/pallas_call | solution.py:213
  8.0 3.7 %collective-permute-start.4 = (f32[128,128]{1,0:T(8,128)S(1)}, f32[128,128]{1,0:T(8,128)S(1)}, u32[]{:S(2)}, u32[]{:S(2)}) collective-permute-start(f32[128,128]{1,0:T(8,128)S(1)} %get-tuple-element.25), channel_id=1, source_target_pairs={{0,13},{1,12},{2,15},{3,14},{4,9},{5,8},{6,11},{7,10},{8,5},{9,4},... | collective-permute-start | bytes 196616 | tf_op jit(solution)/shard_map/ppermute | solution.py:160
  11.8 2.3 %collective-permute-done.4 = f32[128,128]{1,0:T(8,128)S(1)} collective-permute-done((f32[128,128]{1,0:T(8,128)S(1)}, f32[128,128]{1,0:T(8,128)S(1)}, u32[]{:S(2)}, u32[]{:S(2)}) %collective-permute-start.4) | collective-permute-done | bytes 65568 | tf_op jit(solution)/shard_map/ppermute | solution.py:160
  14.1 1.3 %collective-permute-done.3 = f32[128,128]{1,0:T(8,128)S(1)} collective-permute-done((f32[128,128]{1,0:T(8,128)S(1)}, f32[128,128]{1,0:T(8,128)S(1)}, u32[]{:S(2)}, u32[]{:S(2)}) %collective-permute-start.3) | collective-permute-done | bytes 65568 | tf_op jit(solution)/shard_map/ppermute | solution.py:160
  15.5 1.0 %collective-permute-start.5 = (f32[128,128]{1,0:T(8,128)S(1)}, f32[128,128]{1,0:T(8,128)S(1)}, u32[]{:S(2)}, u32[]{:S(2)}) collective-permute-start(f32[128,128]{1,0:T(8,128)S(1)} %add_add_fusion.1), channel_id=1, source_target_pairs={{0,1},{1,0},{2,3},{3,2},{4,5},{5,4},{6,7},{7,6},{8,9},{9,8},{10,11... | collective-permute-start | bytes 196616 | tf_op jit(solution)/shard_map/ppermute | solution.py:160
  16.5 1.1 %collective-permute-start.6 = (f32[128,128]{1,0:T(8,128)S(1)}, f32[128,128]{1,0:T(8,128)S(1)}, u32[]{:S(2)}, u32[]{:S(2)}) collective-permute-start(f32[128,128]{1,0:T(8,128)S(1)} %add_add_fusion.1), channel_id=1, source_target_pairs={{0,2},{1,3},{2,0},{3,1},{4,6},{5,7},{6,4},{7,5},{8,10},{9,11},{10,... | collective-permute-start | bytes 196616 | tf_op jit(solution)/shard_map/ppermute | solution.py:160
  17.7 2.6 %collective-permute-start.10 = (f32[8,128]{1,0:T(8,128)S(1)}, f32[8,128]{1,0:T(8,128)S(1)}, u32[]{:S(2)}, u32[]{:S(2)}) collective-permute-start(f32[8,128]{1,0:T(8,128)S(1)} %get-tuple-element.30.refs_4_), channel_id=1, source_target_pairs={{0,12},{1,15},{2,14},{3,13},{4,8},{5,11},{6,10},{7,9},{8,4},{9,7},... | collective-permute-start | bytes 12296 | tf_op jit(solution)/shard_map/ppermute | solution.py:160
  20.2 1.9 %collective-permute-start.8 = (f32[8,128]{1,0:T(8,128)S(1)}, f32[8,128]{1,0:T(8,128)S(1)}, u32[]{:S(2)}, u32[]{:S(2)}) collective-permute-start(f32[8,128]{1,0:T(8,128)S(1)} %get-tuple-element.30.refs_4_), channel_id=1, source_target_pairs={{0,4},{1,7},{2,6},{3,5},{4,0},{5,3},{6,2},{7,1},{8,12},{9,15},{10,... | collective-permute-start | bytes 12296 | tf_op jit(solution)/shard_map/ppermute | solution.py:160
  22.1 0.7 %collective-permute-start.7 = (f32[128,128]{1,0:T(8,128)S(1)}, f32[128,128]{1,0:T(8,128)S(1)}, u32[]{:S(2)}, u32[]{:S(2)}) collective-permute-start(f32[128,128]{1,0:T(8,128)S(1)} %collective-permute-done.6), channel_id=1, source_target_pairs={{0,1},{1,0},{2,3},{3,2},{4,5},{5,4},{6,7},{7,6},{8,9},{9,8},{10,11... | collective-permute-start | bytes 196616 | tf_op jit(solution)/shard_map/ppermute | solution.py:160
  23.1 1.6 %collective-permute-done.9 = f32[8,128]{1,0:T(8,128)S(1)} collective-permute-done((f32[8,128]{1,0:T(8,128)S(1)}, f32[8,128]{1,0:T(8,128)S(1)}, u32[]{:S(2)}, u32[]{:S(2)}) %collective-permute-start.9) | collective-permute-done | bytes 4128 | tf_op jit(solution)/shard_map/ppermute | solution.py:160
  24.8 1.1 %collective-permute-done.11.refs_6_ = f32[8,128]{1,0:T(8,128)S(1)} collective-permute-done((f32[8,128]{1,0:T(8,128)S(1)}, f32[8,128]{1,0:T(8,128)S(1)}, u32[]{:S(2)}, u32[]{:S(2)}) %collective-permute-start.11) | collective-permute-done | bytes 4128 | tf_op jit(solution)/shard_map/ppermute | solution.py:160
  25.9 1.6 %second_product.1 = (f32[128,128]{1,0:T(8,128)S(1)}, f32[128,128]{1,0:T(8,128)S(1)}, f32[128,128]{1,0:T(8,128)S(1)}, f32[128,128]{1,0:T(8,128)S(1)}) custom-call(s32[14,1,16]{2,1,0:T(1,128)S(1)} %bitcast.13, s32[14,1,16]{2,1,0:T(1,128)S(1)} %collective-permute-done.refs_0_.refs_1_, f32[128,128]{1,0:T(8,128)S(1)} %get-tuple-element.31.refs_2_, ...), custom_call_target="tpu_custom_call" | custom-call | tf_op jit(solution)/shard_map/second_product/pallas_call | solution.py:237
  27.8 1.4 %collective-permute-start.14 = (f32[128,128]{1,0:T(8,128)S(1)}, f32[128,128]{1,0:T(8,128)S(1)}, u32[]{:S(2)}, u32[]{:S(2)}) collective-permute-start(f32[128,128]{1,0:T(8,128)S(1)} %get-tuple-element.29), channel_id=1, source_target_pairs={{0,13},{1,12},{2,15},{3,14},{4,9},{5,8},{6,11},{7,10},{8,5},{9,4},... | collective-permute-start | bytes 196616 | tf_op jit(solution)/shard_map/ppermute | solution.py:160
  29.2 1.7 %collective-permute-start.13 = (f32[128,128]{1,0:T(8,128)S(1)}, f32[128,128]{1,0:T(8,128)S(1)}, u32[]{:S(2)}, u32[]{:S(2)}) collective-permute-start(f32[128,128]{1,0:T(8,128)S(1)} %add.40), channel_id=1, source_target_pairs={{0,9},{1,4},{2,11},{3,6},{4,13},{5,0},{6,15},{7,2},{8,1},{9,12},{1... | collective-permute-start | bytes 196616 | tf_op jit(solution)/shard_map/ppermute | solution.py:160
  31.0 2.7 %collective-permute-done.14 = f32[128,128]{1,0:T(8,128)S(1)} collective-permute-done((f32[128,128]{1,0:T(8,128)S(1)}, f32[128,128]{1,0:T(8,128)S(1)}, u32[]{:S(2)}, u32[]{:S(2)}) %collective-permute-start.14) | collective-permute-done | bytes 65568 | tf_op jit(solution)/shard_map/ppermute | solution.py:160
  33.7 1.3 %collective-permute-done.13 = f32[128,128]{1,0:T(8,128)S(1)} collective-permute-done((f32[128,128]{1,0:T(8,128)S(1)}, f32[128,128]{1,0:T(8,128)S(1)}, u32[]{:S(2)}, u32[]{:S(2)}) %collective-permute-start.13) | collective-permute-done | bytes 65568 | tf_op jit(solution)/shard_map/ppermute | solution.py:160
  35.0 0.3 collective-permute-start.15
  35.4 1.0 %collective-permute-done.15 = f32[128,128]{1,0:T(8,128)S(1)} collective-permute-done((f32[128,128]{1,0:T(8,128)S(1)}, f32[128,128]{1,0:T(8,128)S(1)}, u32[]{:S(2)}, u32[]{:S(2)}) %collective-permute-start.15) | collective-permute-done | bytes 65568 | tf_op jit(solution)/shard_map/ppermute | solution.py:160
  36.3 0.6 %add_bitcast_fusion = f32[1,128,128]{2,1,0:T(8,128)} fusion(f32[128,128]{1,0:T(8,128)S(1)} %add_add_fusion, f32[128,128]{1,0:T(8,128)S(1)} %collective-permute-done.15), kind=kLoop, calls=%fused_computation.1 | loop fusion | flops 16384 | bytes 196608 | tf_op jit(solution)/shard_map/broadcast_in_dim | solution.py:248
  (26 shorter events, 0.8 us)
Async XLA Ops:
  0.6 6.3 %collective-permute-start.1 = (bf16[1,128,128]{2,1,0:T(8,128)(2,1)}, bf16[1,128,128]{2,1,0:T(8,128)(2,1)S(1)}, u32[]{:S(2)}, u32[]{:S(2)}) collective-permute-start(bf16[1,128,128]{2,1,0:T(8,128)(2,1)} %theta.1), channel_id=1, source_target_pairs={{0,3},{1,2},{2,1},{3,0},{4,7},{5,6},{6,5},{7,4},{8,11},{9,10},{10,... | collective-permute-start | bytes 98312 | tf_op jit(solution)/shard_map/ppermute | solution.py:160
  3.1 3.9 %collective-permute-start = (s32[14,1,16]{2,1,0:T(1,128)}, s32[14,1,16]{2,1,0:T(1,128)S(1)}, u32[]{:S(2)}, u32[]{:S(2)}) collective-permute-start(s32[14,1,16]{2,1,0:T(1,128)} %bitcast.11), channel_id=1, source_target_pairs={{0,2},{1,3},{2,0},{3,1},{4,6},{5,7},{6,4},{7,5},{8,10},{9,11},{10,... | collective-permute-start | bytes 2696 | tf_op jit(solution)/shard_map/ppermute | solution.py:160
  3.7 1.6 %copy-start.1 = (bf16[1,128,128]{2,1,0:T(8,128)(2,1)S(1)}, bf16[1,128,128]{2,1,0:T(8,128)(2,1)}, u32[]{:S(2)}) copy-start(bf16[1,128,128]{2,1,0:T(8,128)(2,1)} %theta.1) | copy-start | bytes 98308
  3.7 1.6 %copy-start.2 = (s32[1,1,1,16,14]{3,2,4,1,0:T(1,128)S(1)}, s32[1,1,1,16,14]{3,2,4,1,0:T(1,128)}, u32[]{:S(2)}) copy-start(s32[1,1,1,16,14]{3,2,4,1,0:T(1,128)} %param.7) | copy-start | bytes 2692
  7.9 3.8 %collective-permute-start.2 = (f32[128,128]{1,0:T(8,128)S(1)}, f32[128,128]{1,0:T(8,128)S(1)}, u32[]{:S(2)}, u32[]{:S(2)}) collective-permute-start(f32[128,128]{1,0:T(8,128)S(1)} %get-tuple-element.24), channel_id=1, source_target_pairs={{0,1},{1,0},{2,3},{3,2},{4,5},{5,4},{6,7},{7,6},{8,9},{9,8},{10,11... | collective-permute-start | bytes 196616 | tf_op jit(solution)/shard_map/ppermute | solution.py:160
  8.0 6.2 %collective-permute-start.4 = (f32[128,128]{1,0:T(8,128)S(1)}, f32[128,128]{1,0:T(8,128)S(1)}, u32[]{:S(2)}, u32[]{:S(2)}) collective-permute-start(f32[128,128]{1,0:T(8,128)S(1)} %get-tuple-element.25), channel_id=1, source_target_pairs={{0,13},{1,12},{2,15},{3,14},{4,9},{5,8},{6,11},{7,10},{8,5},{9,4},... | collective-permute-start | bytes 196616 | tf_op jit(solution)/shard_map/ppermute | solution.py:160
  11.7 3.7 %collective-permute-start.3 = (f32[128,128]{1,0:T(8,128)S(1)}, f32[128,128]{1,0:T(8,128)S(1)}, u32[]{:S(2)}, u32[]{:S(2)}) collective-permute-start(f32[128,128]{1,0:T(8,128)S(1)} %add.33), channel_id=1, source_target_pairs={{0,9},{1,4},{2,11},{3,6},{4,13},{5,0},{6,15},{7,2},{8,1},{9,12},{1... | collective-permute-start | bytes 196616 | tf_op jit(solution)/shard_map/ppermute | solution.py:160
  15.5 2.1 %collective-permute-start.5 = (f32[128,128]{1,0:T(8,128)S(1)}, f32[128,128]{1,0:T(8,128)S(1)}, u32[]{:S(2)}, u32[]{:S(2)}) collective-permute-start(f32[128,128]{1,0:T(8,128)S(1)} %add_add_fusion.1), channel_id=1, source_target_pairs={{0,1},{1,0},{2,3},{3,2},{4,5},{5,4},{6,7},{7,6},{8,9},{9,8},{10,11... | collective-permute-start | bytes 196616 | tf_op jit(solution)/shard_map/ppermute | solution.py:160
  16.5 5.6 %collective-permute-start.6 = (f32[128,128]{1,0:T(8,128)S(1)}, f32[128,128]{1,0:T(8,128)S(1)}, u32[]{:S(2)}, u32[]{:S(2)}) collective-permute-start(f32[128,128]{1,0:T(8,128)S(1)} %add_add_fusion.1), channel_id=1, source_target_pairs={{0,2},{1,3},{2,0},{3,1},{4,6},{5,7},{6,4},{7,5},{8,10},{9,11},{10,... | collective-permute-start | bytes 196616 | tf_op jit(solution)/shard_map/ppermute | solution.py:160
  17.6 8.3 %copy-start = (f32[128,128]{1,0:T(8,128)}, f32[128,128]{1,0:T(8,128)S(1)}, u32[]{:S(2)}) copy-start(f32[128,128]{1,0:T(8,128)S(1)} %get-tuple-element.31.refs_2_) | copy-start | bytes 196612
  17.7 5.5 %collective-permute-start.10 = (f32[8,128]{1,0:T(8,128)S(1)}, f32[8,128]{1,0:T(8,128)S(1)}, u32[]{:S(2)}, u32[]{:S(2)}) collective-permute-start(f32[8,128]{1,0:T(8,128)S(1)} %get-tuple-element.30.refs_4_), channel_id=1, source_target_pairs={{0,12},{1,15},{2,14},{3,13},{4,8},{5,11},{6,10},{7,9},{8,4},{9,7},... | collective-permute-start | bytes 12296 | tf_op jit(solution)/shard_map/ppermute | solution.py:160
  20.2 4.5 %collective-permute-start.9 = (f32[8,128]{1,0:T(8,128)S(1)}, f32[8,128]{1,0:T(8,128)S(1)}, u32[]{:S(2)}, u32[]{:S(2)}) collective-permute-start(f32[8,128]{1,0:T(8,128)S(1)} %get-tuple-element.30.refs_4_), channel_id=1, source_target_pairs={{0,8},{1,11},{2,10},{3,9},{4,12},{5,15},{6,14},{7,13},{8,0},{9,3},... | collective-permute-start | bytes 12296 | tf_op jit(solution)/shard_map/ppermute | solution.py:160
  20.2 4.5 %collective-permute-start.8 = (f32[8,128]{1,0:T(8,128)S(1)}, f32[8,128]{1,0:T(8,128)S(1)}, u32[]{:S(2)}, u32[]{:S(2)}) collective-permute-start(f32[8,128]{1,0:T(8,128)S(1)} %get-tuple-element.30.refs_4_), channel_id=1, source_target_pairs={{0,4},{1,7},{2,6},{3,5},{4,0},{5,3},{6,2},{7,1},{8,12},{9,15},{10,... | collective-permute-start | bytes 12296 | tf_op jit(solution)/shard_map/ppermute | solution.py:160
  22.1 2.7 %collective-permute-start.7 = (f32[128,128]{1,0:T(8,128)S(1)}, f32[128,128]{1,0:T(8,128)S(1)}, u32[]{:S(2)}, u32[]{:S(2)}) collective-permute-start(f32[128,128]{1,0:T(8,128)S(1)} %collective-permute-done.6), channel_id=1, source_target_pairs={{0,1},{1,0},{2,3},{3,2},{4,5},{5,4},{6,7},{7,6},{8,9},{9,8},{10,11... | collective-permute-start | bytes 196616 | tf_op jit(solution)/shard_map/ppermute | solution.py:160
  24.8 1.2 %collective-permute-start.11 = (f32[8,128]{1,0:T(8,128)S(1)}, f32[8,128]{1,0:T(8,128)S(1)}, u32[]{:S(2)}, u32[]{:S(2)}) collective-permute-start(f32[8,128]{1,0:T(8,128)S(1)} %add_add_fusion.2.refs_5_), channel_id=1, source_target_pairs={{0,1},{1,0},{2,3},{3,2},{4,5},{5,4},{6,7},{7,6},{8,9},{9,8},{10,11... | collective-permute-start | bytes 12296 | tf_op jit(solution)/shard_map/ppermute | solution.py:160
  27.5 1.7 %collective-permute-start.12 = (f32[128,128]{1,0:T(8,128)S(1)}, f32[128,128]{1,0:T(8,128)S(1)}, u32[]{:S(2)}, u32[]{:S(2)}) collective-permute-start(f32[128,128]{1,0:T(8,128)S(1)} %get-tuple-element.28), channel_id=1, source_target_pairs={{0,1},{1,0},{2,3},{3,2},{4,5},{5,4},{6,7},{7,6},{8,9},{9,8},{10,11... | collective-permute-start | bytes 196616 | tf_op jit(solution)/shard_map/ppermute | solution.py:160
  27.8 5.9 %collective-permute-start.14 = (f32[128,128]{1,0:T(8,128)S(1)}, f32[128,128]{1,0:T(8,128)S(1)}, u32[]{:S(2)}, u32[]{:S(2)}) collective-permute-start(f32[128,128]{1,0:T(8,128)S(1)} %get-tuple-element.29), channel_id=1, source_target_pairs={{0,13},{1,12},{2,15},{3,14},{4,9},{5,8},{6,11},{7,10},{8,5},{9,4},... | collective-permute-start | bytes 196616 | tf_op jit(solution)/shard_map/ppermute | solution.py:160
  29.2 5.8 %collective-permute-start.13 = (f32[128,128]{1,0:T(8,128)S(1)}, f32[128,128]{1,0:T(8,128)S(1)}, u32[]{:S(2)}, u32[]{:S(2)}) collective-permute-start(f32[128,128]{1,0:T(8,128)S(1)} %add.40), channel_id=1, source_target_pairs={{0,9},{1,4},{2,11},{3,6},{4,13},{5,0},{6,15},{7,2},{8,1},{9,12},{1... | collective-permute-start | bytes 196616 | tf_op jit(solution)/shard_map/ppermute | solution.py:160
  35.0 1.3 %collective-permute-start.15 = (f32[128,128]{1,0:T(8,128)S(1)}, f32[128,128]{1,0:T(8,128)S(1)}, u32[]{:S(2)}, u32[]{:S(2)}) collective-permute-start(f32[128,128]{1,0:T(8,128)S(1)} %add_add_fusion), channel_id=1, source_target_pairs={{0,1},{1,0},{2,3},{3,2},{4,5},{5,4},{6,7},{7,6},{8,9},{9,8},{10,11... | collective-permute-start | bytes 196616 | tf_op jit(solution)/shard_map/ppermute | solution.py:160

commit v7 on v6

--- a/solution.py
+++ b/solution.py
@@ -15,6 +15,21 @@
 
 def dot(a, b):
     return jnp.dot(a, b, preferred_element_type=jnp.float32)
+
+
+def reader(words, per, lt_dev, rt_dev):
+    bits = lambda count: (count - 1).bit_length()
+    left_bits, tile_bits, out_bits = bits(2 * lt_dev), bits(rt_dev), bits(lax.axis_size("left"))
+    shift = left_bits + bits(lax.axis_size("right"))
+
+    def read(n):
+        word, outs = words(0, n), words(1, n)
+        left = word & ((1 << left_bits) - 1)
+        base = (left // lt_dev) * rt_dev
+        rights = [base + ((word >> (shift + j * tile_bits)) & ((1 << tile_bits) - 1)) for j in range(per)]
+        return left, rights, [(outs >> (j * out_bits)) & ((1 << out_bits) - 1) for j in range(per)]
+
+    return read
 
 
 def pick_entries(terms, words, lt_dev, rt_dev):
@@ -40,13 +55,7 @@
         target = (word >> left_bits) & ((1 << target_bits) - 1)
         count = count + (target == me_right).astype(jnp.int32)
 
-    def read(n):
-        word, outs = words[0, n], words[1, n]
-        left = word & ((1 << left_bits) - 1)
-        base = (left // lt_dev) * rt_dev
-        rights = [base + ((word >> (shift + j * tile_bits)) & ((1 << tile_bits) - 1)) for j in range(per)]
-        return left, rights, [(outs >> (j * out_bits)) & ((1 << out_bits) - 1) for j in range(per)]
-
+    read = reader(lambda row, n: words[row, n], per, lt_dev, rt_dev)
     return count, read
 
 
@@ -78,6 +87,22 @@
             spread(rights, outs, dot(left_ref[left], vec).astype(jnp.bfloat16))
 
         pl.loop(0, count)(one)
+
+
+def write_plan(words, out):
+    lane = lax.broadcasted_iota(jnp.int32, (1, out.shape[1]), 1)
+    for k in range(2):
+        row = jnp.zeros((1, out.shape[1]), jnp.int32)
+        for n in range(CAP):
+            row = jnp.where(lane == n, words[k, n], row)
+        out[k:k + 1] = row
+
+
+def picked_of(key, words, dims):
+    if not dims[2]:
+        return pick_entries(key, words, *dims[:2])
+    rows = [key[k:k + 1] for k in range(2)]
+    return CAP, reader(lambda row, n: rows[row][0, n], dims[3], *dims[:2])
 
 
 def load_kernel(left_hbm, right_hbm, left_ref, right_ref, sems):
@@ -106,8 +131,9 @@
 
 
 def own_kernel(dims, terms, theta, left_ref, right_ref, *refs):
-    *accs, words, inter = refs
+    *accs, plan, words, inter = refs
     picked = pick_entries(terms, words.at[0], *dims[:2])
+    write_plan(words.at[0], plan)
     for acc in accs:
         acc[...] = jnp.zeros_like(acc)
     apply_list(picked, theta[0], left_ref, right_ref, accs, inter.at[0], dims[2])
@@ -118,9 +144,11 @@
     thetas = refs[count:2 * count]
     left_ref, right_ref = refs[2 * count:2 * count + 2]
     starts = refs[2 * count + 2:2 * count + 2 + BLOCKS]
-    outs = refs[2 * count + 2 + BLOCKS:-2 - BLOCKS]
+    *outs, plans = refs[2 * count + 2 + BLOCKS:-2 - BLOCKS]
     *accs, words, inter = refs[-2 - BLOCKS:]
     picked = [pick_entries(terms, words.at[i], *dims[:2]) for i, terms in enumerate(lists)]
+    for i in range(count):
+        write_plan(words.at[i], plans.at[i])
     for acc, start in zip(accs, starts):
         acc[...] = start[...]
     for i, theta in enumerate(thetas):
@@ -129,16 +157,16 @@
 
 
 def second_kernel(dims, nr, count, elements, *refs):
-    lists = refs[:nr]
+    keys = refs[:nr]
     tiles = refs[nr:2 * nr]
     sums = refs[2 * nr:2 * nr + count]
     left_ref, right_ref = refs[2 * nr + count:2 * nr + count + 2]
     outs = refs[2 * nr + count + 2:-2 - BLOCKS]
     *accs, words, inter = refs[-2 - BLOCKS:]
-    picked = [pick_entries(terms, words.at[i], *dims[:2]) for i, terms in enumerate(lists)]
+    picked = [picked_of(key, words.at[i], dims) for i, key in enumerate(keys)]
     values = [t[...] for t in tiles]
-    total = sum(fold_squares(value) for value in values[1:])
-    for part in sums:
+    total = sums[0][...]
+    for part in sums[1:]:
         total = total + part[...]
     scale = 1.0 / jnp.sqrt(jnp.sum(total, keepdims=True) / elements + 1e-06)
     for acc in accs:
@@ -170,7 +198,7 @@
     nr = lax.axis_size("right")
     rows, fields = terms.shape[-2:]
     entries = jnp.transpose(terms, (0, 1, 4, 2, 3)).reshape(fields, 1, rows)
-    dims = (lt_dev, rt_dev, CAP * nr == rows)
+    dims = (lt_dev, rt_dev, CAP * nr == rows, (fields - 2) // 2)
     swap_cores = lambda x: permute(x, lambda p, t, m: (p, t, 1 - m))
     lists = [entries] + [permute(entries, lambda p, t, m, s=s: (p, t ^ s, m)) for s in range(1, nr)]
     thetas = [theta] + [permute(theta, lambda p, t, m, s=s: (p, t ^ s, 1 - m)) for s in range(1, nr)]
@@ -200,25 +228,27 @@
         compiler_params=pltpu.CompilerParams(vmem_limit_bytes=51 << 20),
         name="load",
     )(left_flat, right_flat)
-    own_parts = pl.pallas_call(
+    plan_shape = jax.ShapeDtypeStruct((2, tile), jnp.int32)
+    *own_parts, own_plan = pl.pallas_call(
         functools.partial(own_kernel, dims),
-        out_shape=[jax.ShapeDtypeStruct(*shape) for shape in part_shapes],
+        out_shape=[jax.ShapeDtypeStruct(*shape) for shape in part_shapes] + [plan_shape],
         in_specs=[VMEM] * 4,
-        out_specs=[VMEM] * BLOCKS,
+        out_specs=[VMEM] * (BLOCKS + 1),
         scratch_shapes=scratch,
         compiler_params=params,
         name="first_own",
     )(entries, theta, left_flat, right_flat)
     out_shape = [jax.ShapeDtypeStruct((tile, tile), jnp.float32)] * nl
-    parts = pl.pallas_call(
+    *parts, plans = pl.pallas_call(
         functools.partial(rest_kernel, dims, nr - 1),
-        out_shape=out_shape,
+        out_shape=out_shape + [jax.ShapeDtypeStruct((nr - 1, 2, tile), jnp.int32)],
         in_specs=[VMEM] * (2 * nr + BLOCKS),
-        out_specs=[VMEM] * len(out_shape),
+        out_specs=[VMEM] * (nl + 1),
         scratch_shapes=accs + scratch,
         compiler_params=params,
         name="first_rest",
     )(*lists[1:], *thetas[1:], left_flat, right_flat, *own_parts)
+    keys = [own_plan, *plans] if dims[2] else lists
 
     half = reduce_tiles(parts)
     halves = [permute(half, lambda p, t, m: (p, t ^ s, m)) for s in range(1, nr)]
@@ -228,10 +258,10 @@
     if nr == 2:
         sums = [permute(squares, lambda p, t, m: (p ^ s, t ^ m, m)) for s in range(1, nl)]
         others = sum(sums[1:], sums[0])
-        sums = [squares, others, swap_cores(others)]
+        sums = [squares + fold_squares(neighbours[0]), others, swap_cores(others)]
     else:
         row = squares + sum(fold_squares(x) for x in neighbours)
-        sums = [squares] + [permute(row, lambda p, t, m: (p ^ s, t, 1 - m)) for s in range(1, nl)]
+        sums = [row] + [permute(row, lambda p, t, m: (p ^ s, t, 1 - m)) for s in range(1, nl)]
     tiles = [h_theta] + neighbours
 
     parts = pl.pallas_call(
@@ -242,7 +272,7 @@
         scratch_shapes=accs + scratch,
         compiler_params=params,
         name="second_product",
-    )(*lists, *tiles, *sums, left_flat, right_flat)
+    )(*keys, *tiles, *sums, left_flat, right_flat)
     half = reduce_tiles(parts)
     h_second = half + swap_cores(half)
     return h_theta[None], h_second[None]

time: 37.1 us -> 37 us (level)
  no operation moved by 1% of the time
where the time goes in v7:
time: 37 us; the launch traced here: 36.9 us
  starting transfers between devices  18 us (49%)
  waiting for transfers between devices  12.3 us (33%)
  Pallas kernels  5.06 us (14%)
  between operations  0.75 us (2%)
  other arithmetic  0.74 us (2%)
    ppermute x16, starting transfers between devices, permute(): return lax.ppermute(value, ('left', 'right', 'mpo'), pairs)  18 us
    ppermute x16, waiting for transfers between devices, permute(): return lax.ppermute(value, ('left', 'right', 'mpo'), pairs)  12.3 us
    pallas_call x1, Pallas kernels, local(): pl.pallas_call(load_kernel, out_shape=[jax.ShapeDtypeStruct(x.shape, x.dt...  1.56 us
    pallas_call x1, Pallas kernels, local(): pl.pallas_call(functools.partial(second_kernel, dims, nr, len(sums), nl *...  1.53 us
    pallas_call x1, Pallas kernels, local(): pl.pallas_call(functools.partial(rest_kernel, dims, nr - 1), out_shape=ou...  0.98 us
    pallas_call x1, Pallas kernels, local(): pl.pallas_call(functools.partial(own_kernel, dims), out_shape=[jax.ShapeD...  0.98 us
  transfers between devices with their start and end apart: 16, of which 9 were waited for; matrix products, arithmetic and copies ran while one was open for 0% of the time, Pallas kernels for 7%

profile of v7, /device:TPU:0, one launch (start us, length us, event | category | flops | bytes accessed | tf_op | source)
XLA Modules:
  0.0 36.9 jit_solution(17520411752917626494)
XLA Ops:
  0.6 2.4 %collective-permute-start.1 = (bf16[1,128,128]{2,1,0:T(8,128)(2,1)}, bf16[1,128,128]{2,1,0:T(8,128)(2,1)S(1)}, u32[]{:S(2)}, u32[]{:S(2)}) collective-permute-start(bf16[1,128,128]{2,1,0:T(8,128)(2,1)} %theta.1), channel_id=1, source_target_pairs={{0,3},{1,2},{2,1},{3,0},{4,7},{5,6},{6,5},{7,4},{8,11},{9,10},{10,... | collective-permute-start | bytes 98312 | tf_op jit(solution)/shard_map/ppermute | solution.py:188
  3.1 0.6 %collective-permute-start = (s32[14,1,16]{2,1,0:T(1,128)}, s32[14,1,16]{2,1,0:T(1,128)S(1)}, u32[]{:S(2)}, u32[]{:S(2)}) collective-permute-start(s32[14,1,16]{2,1,0:T(1,128)} %bitcast.14), channel_id=1, source_target_pairs={{0,2},{1,3},{2,0},{3,1},{4,6},{5,7},{6,4},{7,5},{8,10},{9,11},{10,... | collective-permute-start | bytes 2696 | tf_op jit(solution)/shard_map/ppermute | solution.py:188
  3.7 1.6 %load.1 = (bf16[32,128,128]{2,1,0:T(8,128)(2,1)S(1)}, bf16[32,128,128]{2,1,0:T(8,128)(2,1)S(1)}) custom-call(bf16[32,128,128]{2,1,0:T(8,128)(2,1)} %bitcast.17, bf16[32,128,128]{2,1,0:T(8,128)(2,1)} %bitcast.18), custom_call_target="tpu_custom_call" | custom-call | tf_op jit(solution)/shard_map/load/pallas_call | solution.py:222
  5.3 1.0 %first_own.1 = (f32[4,32,128]{2,1,0:T(8,128)S(1)}, f32[4,32,128]{2,1,0:T(8,128)S(1)}, f32[4,32,128]{2,1,0:T(8,128)S(1)}, f32[4,32,128]{2,1,0:T(8,128)S(1)}, s32[2,128]{1,0:T(2,128)S(1)}) custom-call(s32[14,1,16]{2,1,0:T(1,128)S(1)} %bitcast.15, bf16[1,128,128]{2,1,0:T(8,128)(2,1)S(1)} %copy-done.1, ...), custom_call_target="tpu_custom_call" | custom-call | tf_op jit(solution)/shard_map/first_own/pallas_call | solution.py:232
  6.3 0.6 %collective-permute-done.refs_0_ = s32[14,1,16]{2,1,0:T(1,128)S(1)} collective-permute-done((s32[14,1,16]{2,1,0:T(1,128)}, s32[14,1,16]{2,1,0:T(1,128)S(1)}, u32[]{:S(2)}, u32[]{:S(2)}) %collective-permute-start) | collective-permute-done | bytes 928 | tf_op jit(solution)/shard_map/ppermute | solution.py:188
  6.9 1.0 %first_rest.1 = (f32[128,128]{1,0:T(8,128)S(1)}, f32[128,128]{1,0:T(8,128)S(1)}, f32[128,128]{1,0:T(8,128)S(1)}, f32[128,128]{1,0:T(8,128)S(1)}, s32[1,2,128]{2,1,0:T(2,128)S(1)}) custom-call(s32[14,1,16]{2,1,0:T(1,128)S(1)} %collective-permute-done.refs_0_, bf16[1,128,128]{2,1,0:T(8,128)(2,1)S(1)} %collective-permute-done.1.refs_1_, ...), custom_call_target="tpu_custom_call" | custom-call | tf_op jit(solution)/shard_map/first_rest/pallas_call | solution.py:242
  8.0 3.7 %collective-permute-start.4 = (f32[128,128]{1,0:T(8,128)S(1)}, f32[128,128]{1,0:T(8,128)S(1)}, u32[]{:S(2)}, u32[]{:S(2)}) collective-permute-start(f32[128,128]{1,0:T(8,128)S(1)} %get-tuple-element.27), channel_id=1, source_target_pairs={{0,13},{1,12},{2,15},{3,14},{4,9},{5,8},{6,11},{7,10},{8,5},{9,4},... | collective-permute-start | bytes 196616 | tf_op jit(solution)/shard_map/ppermute | solution.py:188
  11.8 2.3 %collective-permute-done.4 = f32[128,128]{1,0:T(8,128)S(1)} collective-permute-done((f32[128,128]{1,0:T(8,128)S(1)}, f32[128,128]{1,0:T(8,128)S(1)}, u32[]{:S(2)}, u32[]{:S(2)}) %collective-permute-start.4) | collective-permute-done | bytes 65568 | tf_op jit(solution)/shard_map/ppermute | solution.py:188
  14.1 1.3 %collective-permute-done.3 = f32[128,128]{1,0:T(8,128)S(1)} collective-permute-done((f32[128,128]{1,0:T(8,128)S(1)}, f32[128,128]{1,0:T(8,128)S(1)}, u32[]{:S(2)}, u32[]{:S(2)}) %collective-permute-start.3) | collective-permute-done | bytes 65568 | tf_op jit(solution)/shard_map/ppermute | solution.py:188
  15.5 1.0 %collective-permute-start.5 = (f32[128,128]{1,0:T(8,128)S(1)}, f32[128,128]{1,0:T(8,128)S(1)}, u32[]{:S(2)}, u32[]{:S(2)}) collective-permute-start(f32[128,128]{1,0:T(8,128)S(1)} %add_add_fusion.1), channel_id=1, source_target_pairs={{0,1},{1,0},{2,3},{3,2},{4,5},{5,4},{6,7},{7,6},{8,9},{9,8},{10,11... | collective-permute-start | bytes 196616 | tf_op jit(solution)/shard_map/ppermute | solution.py:188
  16.5 1.1 %collective-permute-start.6 = (f32[128,128]{1,0:T(8,128)S(1)}, f32[128,128]{1,0:T(8,128)S(1)}, u32[]{:S(2)}, u32[]{:S(2)}) collective-permute-start(f32[128,128]{1,0:T(8,128)S(1)} %add_add_fusion.1), channel_id=1, source_target_pairs={{0,2},{1,3},{2,0},{3,1},{4,6},{5,7},{6,4},{7,5},{8,10},{9,11},{10,... | collective-permute-start | bytes 196616 | tf_op jit(solution)/shard_map/ppermute | solution.py:188
  17.7 2.5 %collective-permute-start.10 = (f32[8,128]{1,0:T(8,128)S(1)}, f32[8,128]{1,0:T(8,128)S(1)}, u32[]{:S(2)}, u32[]{:S(2)}) collective-permute-start(f32[8,128]{1,0:T(8,128)S(1)} %get-tuple-element.36), channel_id=1, source_target_pairs={{0,12},{1,15},{2,14},{3,13},{4,8},{5,11},{6,10},{7,9},{8,4},{9,7},... | collective-permute-start | bytes 12296 | tf_op jit(solution)/shard_map/ppermute | solution.py:188
  20.2 1.9 %collective-permute-start.8 = (f32[8,128]{1,0:T(8,128)S(1)}, f32[8,128]{1,0:T(8,128)S(1)}, u32[]{:S(2)}, u32[]{:S(2)}) collective-permute-start(f32[8,128]{1,0:T(8,128)S(1)} %get-tuple-element.36), channel_id=1, source_target_pairs={{0,4},{1,7},{2,6},{3,5},{4,0},{5,3},{6,2},{7,1},{8,12},{9,15},{10,... | collective-permute-start | bytes 12296 | tf_op jit(solution)/shard_map/ppermute | solution.py:188
  22.1 0.7 %collective-permute-start.7 = (f32[128,128]{1,0:T(8,128)S(1)}, f32[128,128]{1,0:T(8,128)S(1)}, u32[]{:S(2)}, u32[]{:S(2)}) collective-permute-start(f32[128,128]{1,0:T(8,128)S(1)} %collective-permute-done.6), channel_id=1, source_target_pairs={{0,1},{1,0},{2,3},{3,2},{4,5},{5,4},{6,7},{7,6},{8,9},{9,8},{10,11... | collective-permute-start | bytes 196616 | tf_op jit(solution)/shard_map/ppermute | solution.py:188
  23.1 1.6 %collective-permute-done.9 = f32[8,128]{1,0:T(8,128)S(1)} collective-permute-done((f32[8,128]{1,0:T(8,128)S(1)}, f32[8,128]{1,0:T(8,128)S(1)}, u32[]{:S(2)}, u32[]{:S(2)}) %collective-permute-start.9) | collective-permute-done | bytes 4128 | tf_op jit(solution)/shard_map/ppermute | solution.py:188
  24.8 1.1 %collective-permute-done.11.refs_6_ = f32[8,128]{1,0:T(8,128)S(1)} collective-permute-done((f32[8,128]{1,0:T(8,128)S(1)}, f32[8,128]{1,0:T(8,128)S(1)}, u32[]{:S(2)}, u32[]{:S(2)}) %collective-permute-start.11) | collective-permute-done | bytes 4128 | tf_op jit(solution)/shard_map/ppermute | solution.py:188
  25.9 1.5 %second_product.1 = (f32[128,128]{1,0:T(8,128)S(1)}, f32[128,128]{1,0:T(8,128)S(1)}, f32[128,128]{1,0:T(8,128)S(1)}, f32[128,128]{1,0:T(8,128)S(1)}) custom-call(s32[2,128]{1,0:T(2,128)S(1)} %get-tuple-element.28.refs_0_, s32[2,128]{1,0:T(2,128)S(1)} %bitcast.16, f32[128,128]{1,0:T(8,128)S(1)} %get-tuple-element.37.refs_2_, ...), custom_call_target="tpu_custom_call" | custom-call | tf_op jit(solution)/shard_map/second_product/pallas_call | solution.py:267
  27.7 1.4 %collective-permute-start.14 = (f32[128,128]{1,0:T(8,128)S(1)}, f32[128,128]{1,0:T(8,128)S(1)}, u32[]{:S(2)}, u32[]{:S(2)}) collective-permute-start(f32[128,128]{1,0:T(8,128)S(1)} %get-tuple-element.33), channel_id=1, source_target_pairs={{0,13},{1,12},{2,15},{3,14},{4,9},{5,8},{6,11},{7,10},{8,5},{9,4},... | collective-permute-start | bytes 196616 | tf_op jit(solution)/shard_map/ppermute | solution.py:188
  29.1 1.8 %collective-permute-start.13 = (f32[128,128]{1,0:T(8,128)S(1)}, f32[128,128]{1,0:T(8,128)S(1)}, u32[]{:S(2)}, u32[]{:S(2)}) collective-permute-start(f32[128,128]{1,0:T(8,128)S(1)} %add.44), channel_id=1, source_target_pairs={{0,9},{1,4},{2,11},{3,6},{4,13},{5,0},{6,15},{7,2},{8,1},{9,12},{1... | collective-permute-start | bytes 196616 | tf_op jit(solution)/shard_map/ppermute | solution.py:188
  30.9 2.7 %collective-permute-done.14 = f32[128,128]{1,0:T(8,128)S(1)} collective-permute-done((f32[128,128]{1,0:T(8,128)S(1)}, f32[128,128]{1,0:T(8,128)S(1)}, u32[]{:S(2)}, u32[]{:S(2)}) %collective-permute-start.14) | collective-permute-done | bytes 65568 | tf_op jit(solution)/shard_map/ppermute | solution.py:188
  33.6 1.3 %collective-permute-done.13 = f32[128,128]{1,0:T(8,128)S(1)} collective-permute-done((f32[128,128]{1,0:T(8,128)S(1)}, f32[128,128]{1,0:T(8,128)S(1)}, u32[]{:S(2)}, u32[]{:S(2)}) %collective-permute-start.13) | collective-permute-done | bytes 65568 | tf_op jit(solution)/shard_map/ppermute | solution.py:188
  34.9 0.4 %collective-permute-start.15 = (f32[128,128]{1,0:T(8,128)S(1)}, f32[128,128]{1,0:T(8,128)S(1)}, u32[]{:S(2)}, u32[]{:S(2)}) collective-permute-start(f32[128,128]{1,0:T(8,128)S(1)} %add_add_fusion), channel_id=1, source_target_pairs={{0,1},{1,0},{2,3},{3,2},{4,5},{5,4},{6,7},{7,6},{8,9},{9,8},{10,11... | collective-permute-start | bytes 196616 | tf_op jit(solution)/shard_map/ppermute | solution.py:188
  35.3 0.9 %collective-permute-done.15 = f32[128,128]{1,0:T(8,128)S(1)} collective-permute-done((f32[128,128]{1,0:T(8,128)S(1)}, f32[128,128]{1,0:T(8,128)S(1)}, u32[]{:S(2)}, u32[]{:S(2)}) %collective-permute-start.15) | collective-permute-done | bytes 65568 | tf_op jit(solution)/shard_map/ppermute | solution.py:188
  36.2 0.6 %add_bitcast_fusion = f32[1,128,128]{2,1,0:T(8,128)} fusion(f32[128,128]{1,0:T(8,128)S(1)} %add_add_fusion, f32[128,128]{1,0:T(8,128)S(1)} %collective-permute-done.15), kind=kLoop, calls=%fused_computation.2 | loop fusion | flops 16384 | bytes 196608 | tf_op jit(solution)/shard_map/broadcast_in_dim | solution.py:278
  (27 shorter events, 0.8 us)
Async XLA Ops:
  0.6 6.3 %collective-permute-start.1 = (bf16[1,128,128]{2,1,0:T(8,128)(2,1)}, bf16[1,128,128]{2,1,0:T(8,128)(2,1)S(1)}, u32[]{:S(2)}, u32[]{:S(2)}) collective-permute-start(bf16[1,128,128]{2,1,0:T(8,128)(2,1)} %theta.1), channel_id=1, source_target_pairs={{0,3},{1,2},{2,1},{3,0},{4,7},{5,6},{6,5},{7,4},{8,11},{9,10},{10,... | collective-permute-start | bytes 98312 | tf_op jit(solution)/shard_map/ppermute | solution.py:188
  3.1 3.9 %collective-permute-start = (s32[14,1,16]{2,1,0:T(1,128)}, s32[14,1,16]{2,1,0:T(1,128)S(1)}, u32[]{:S(2)}, u32[]{:S(2)}) collective-permute-start(s32[14,1,16]{2,1,0:T(1,128)} %bitcast.14), channel_id=1, source_target_pairs={{0,2},{1,3},{2,0},{3,1},{4,6},{5,7},{6,4},{7,5},{8,10},{9,11},{10,... | collective-permute-start | bytes 2696 | tf_op jit(solution)/shard_map/ppermute | solution.py:188
  3.7 1.6 %copy-start.1 = (bf16[1,128,128]{2,1,0:T(8,128)(2,1)S(1)}, bf16[1,128,128]{2,1,0:T(8,128)(2,1)}, u32[]{:S(2)}) copy-start(bf16[1,128,128]{2,1,0:T(8,128)(2,1)} %theta.1) | copy-start | bytes 98308
  3.7 1.6 %copy-start.2 = (s32[1,1,1,16,14]{3,2,4,1,0:T(1,128)S(1)}, s32[1,1,1,16,14]{3,2,4,1,0:T(1,128)}, u32[]{:S(2)}) copy-start(s32[1,1,1,16,14]{3,2,4,1,0:T(1,128)} %param.7) | copy-start | bytes 2692
  7.9 3.8 %collective-permute-start.2 = (f32[128,128]{1,0:T(8,128)S(1)}, f32[128,128]{1,0:T(8,128)S(1)}, u32[]{:S(2)}, u32[]{:S(2)}) collective-permute-start(f32[128,128]{1,0:T(8,128)S(1)} %get-tuple-element.26), channel_id=1, source_target_pairs={{0,1},{1,0},{2,3},{3,2},{4,5},{5,4},{6,7},{7,6},{8,9},{9,8},{10,11... | collective-permute-start | bytes 196616 | tf_op jit(solution)/shard_map/ppermute | solution.py:188
  8.0 6.1 %collective-permute-start.4 = (f32[128,128]{1,0:T(8,128)S(1)}, f32[128,128]{1,0:T(8,128)S(1)}, u32[]{:S(2)}, u32[]{:S(2)}) collective-permute-start(f32[128,128]{1,0:T(8,128)S(1)} %get-tuple-element.27), channel_id=1, source_target_pairs={{0,13},{1,12},{2,15},{3,14},{4,9},{5,8},{6,11},{7,10},{8,5},{9,4},... | collective-permute-start | bytes 196616 | tf_op jit(solution)/shard_map/ppermute | solution.py:188
  11.7 3.7 %collective-permute-start.3 = (f32[128,128]{1,0:T(8,128)S(1)}, f32[128,128]{1,0:T(8,128)S(1)}, u32[]{:S(2)}, u32[]{:S(2)}) collective-permute-start(f32[128,128]{1,0:T(8,128)S(1)} %add.36), channel_id=1, source_target_pairs={{0,9},{1,4},{2,11},{3,6},{4,13},{5,0},{6,15},{7,2},{8,1},{9,12},{1... | collective-permute-start | bytes 196616 | tf_op jit(solution)/shard_map/ppermute | solution.py:188
  15.5 2.1 %collective-permute-start.5 = (f32[128,128]{1,0:T(8,128)S(1)}, f32[128,128]{1,0:T(8,128)S(1)}, u32[]{:S(2)}, u32[]{:S(2)}) collective-permute-start(f32[128,128]{1,0:T(8,128)S(1)} %add_add_fusion.1), channel_id=1, source_target_pairs={{0,1},{1,0},{2,3},{3,2},{4,5},{5,4},{6,7},{7,6},{8,9},{9,8},{10,11... | collective-permute-start | bytes 196616 | tf_op jit(solution)/shard_map/ppermute | solution.py:188
  16.5 5.6 %collective-permute-start.6 = (f32[128,128]{1,0:T(8,128)S(1)}, f32[128,128]{1,0:T(8,128)S(1)}, u32[]{:S(2)}, u32[]{:S(2)}) collective-permute-start(f32[128,128]{1,0:T(8,128)S(1)} %add_add_fusion.1), channel_id=1, source_target_pairs={{0,2},{1,3},{2,0},{3,1},{4,6},{5,7},{6,4},{7,5},{8,10},{9,11},{10,... | collective-permute-start | bytes 196616 | tf_op jit(solution)/shard_map/ppermute | solution.py:188
  17.7 8.3 %copy-start = (f32[128,128]{1,0:T(8,128)}, f32[128,128]{1,0:T(8,128)S(1)}, u32[]{:S(2)}) copy-start(f32[128,128]{1,0:T(8,128)S(1)} %get-tuple-element.37.refs_2_) | copy-start | bytes 196612
  17.7 5.5 %collective-permute-start.10 = (f32[8,128]{1,0:T(8,128)S(1)}, f32[8,128]{1,0:T(8,128)S(1)}, u32[]{:S(2)}, u32[]{:S(2)}) collective-permute-start(f32[8,128]{1,0:T(8,128)S(1)} %get-tuple-element.36), channel_id=1, source_target_pairs={{0,12},{1,15},{2,14},{3,13},{4,8},{5,11},{6,10},{7,9},{8,4},{9,7},... | collective-permute-start | bytes 12296 | tf_op jit(solution)/shard_map/ppermute | solution.py:188
  20.2 4.5 %collective-permute-start.9 = (f32[8,128]{1,0:T(8,128)S(1)}, f32[8,128]{1,0:T(8,128)S(1)}, u32[]{:S(2)}, u32[]{:S(2)}) collective-permute-start(f32[8,128]{1,0:T(8,128)S(1)} %get-tuple-element.36), channel_id=1, source_target_pairs={{0,8},{1,11},{2,10},{3,9},{4,12},{5,15},{6,14},{7,13},{8,0},{9,3},... | collective-permute-start | bytes 12296 | tf_op jit(solution)/shard_map/ppermute | solution.py:188
  20.2 4.5 %collective-permute-start.8 = (f32[8,128]{1,0:T(8,128)S(1)}, f32[8,128]{1,0:T(8,128)S(1)}, u32[]{:S(2)}, u32[]{:S(2)}) collective-permute-start(f32[8,128]{1,0:T(8,128)S(1)} %get-tuple-element.36), channel_id=1, source_target_pairs={{0,4},{1,7},{2,6},{3,5},{4,0},{5,3},{6,2},{7,1},{8,12},{9,15},{10,... | collective-permute-start | bytes 12296 | tf_op jit(solution)/shard_map/ppermute | solution.py:188
  22.1 2.7 %collective-permute-start.7 = (f32[128,128]{1,0:T(8,128)S(1)}, f32[128,128]{1,0:T(8,128)S(1)}, u32[]{:S(2)}, u32[]{:S(2)}) collective-permute-start(f32[128,128]{1,0:T(8,128)S(1)} %collective-permute-done.6), channel_id=1, source_target_pairs={{0,1},{1,0},{2,3},{3,2},{4,5},{5,4},{6,7},{7,6},{8,9},{9,8},{10,11... | collective-permute-start | bytes 196616 | tf_op jit(solution)/shard_map/ppermute | solution.py:188
  24.8 1.2 %collective-permute-start.11 = (f32[8,128]{1,0:T(8,128)S(1)}, f32[8,128]{1,0:T(8,128)S(1)}, u32[]{:S(2)}, u32[]{:S(2)}) collective-permute-start(f32[8,128]{1,0:T(8,128)S(1)} %add_add_fusion.2.refs_5_), channel_id=1, source_target_pairs={{0,1},{1,0},{2,3},{3,2},{4,5},{5,4},{6,7},{7,6},{8,9},{9,8},{10,11... | collective-permute-start | bytes 12296 | tf_op jit(solution)/shard_map/ppermute | solution.py:188
  27.5 1.6 %collective-permute-start.12 = (f32[128,128]{1,0:T(8,128)S(1)}, f32[128,128]{1,0:T(8,128)S(1)}, u32[]{:S(2)}, u32[]{:S(2)}) collective-permute-start(f32[128,128]{1,0:T(8,128)S(1)} %get-tuple-element.32), channel_id=1, source_target_pairs={{0,1},{1,0},{2,3},{3,2},{4,5},{5,4},{6,7},{7,6},{8,9},{9,8},{10,11... | collective-permute-start | bytes 196616 | tf_op jit(solution)/shard_map/ppermute | solution.py:188
  27.7 5.9 %collective-permute-start.14 = (f32[128,128]{1,0:T(8,128)S(1)}, f32[128,128]{1,0:T(8,128)S(1)}, u32[]{:S(2)}, u32[]{:S(2)}) collective-permute-start(f32[128,128]{1,0:T(8,128)S(1)} %get-tuple-element.33), channel_id=1, source_target_pairs={{0,13},{1,12},{2,15},{3,14},{4,9},{5,8},{6,11},{7,10},{8,5},{9,4},... | collective-permute-start | bytes 196616 | tf_op jit(solution)/shard_map/ppermute | solution.py:188
  29.1 5.8 %collective-permute-start.13 = (f32[128,128]{1,0:T(8,128)S(1)}, f32[128,128]{1,0:T(8,128)S(1)}, u32[]{:S(2)}, u32[]{:S(2)}) collective-permute-start(f32[128,128]{1,0:T(8,128)S(1)} %add.44), channel_id=1, source_target_pairs={{0,9},{1,4},{2,11},{3,6},{4,13},{5,0},{6,15},{7,2},{8,1},{9,12},{1... | collective-permute-start | bytes 196616 | tf_op jit(solution)/shard_map/ppermute | solution.py:188
  34.9 1.3 %collective-permute-start.15 = (f32[128,128]{1,0:T(8,128)S(1)}, f32[128,128]{1,0:T(8,128)S(1)}, u32[]{:S(2)}, u32[]{:S(2)}) collective-permute-start(f32[128,128]{1,0:T(8,128)S(1)} %add_add_fusion), channel_id=1, source_target_pairs={{0,1},{1,0},{2,3},{3,2},{4,5},{5,4},{6,7},{7,6},{8,9},{9,8},{10,11... | collective-permute-start | bytes 196616 | tf_op jit(solution)/shard_map/ppermute | solution.py:188

commit v8 on v7

--- a/solution.py
+++ b/solution.py
@@ -251,7 +251,7 @@
     keys = [own_plan, *plans] if dims[2] else lists
 
     half = reduce_tiles(parts)
-    halves = [permute(half, lambda p, t, m: (p, t ^ s, m)) for s in range(1, nr)]
+    halves = [permute(half, lambda p, t, m: (p, t ^ s, 1 - m)) for s in range(1, nr)]
     h_theta = half + swap_cores(half)
     neighbours = [x + swap_cores(x) for x in halves]
     squares = fold_squares(h_theta)

time: 37 us -> 37 us (level)
  transfers between devices with their start and end apart: 16 -> 16, of which waited for: 9 -> 10; matrix products, arithmetic and copies ran while one was open for 0% -> 0% of each run, Pallas kernels for 7% -> 7%
where the time goes in v8:
time: 37 us; the launch traced here: 36.9 us
  starting transfers between devices  18 us (49%)
  waiting for transfers between devices  12.3 us (33%)
  Pallas kernels  5.07 us (14%)
  other arithmetic  0.74 us (2%)
  between operations  0.74 us (2%)
    ppermute x16, starting transfers between devices, permute(): return lax.ppermute(value, ('left', 'right', 'mpo'), pairs)  18 us
    ppermute x16, waiting for transfers between devices, permute(): return lax.ppermute(value, ('left', 'right', 'mpo'), pairs)  12.3 us
    pallas_call x1, Pallas kernels, local(): pl.pallas_call(load_kernel, out_shape=[jax.ShapeDtypeStruct(x.shape, x.dt...  1.56 us
    pallas_call x1, Pallas kernels, local(): pl.pallas_call(functools.partial(second_kernel, dims, nr, len(sums), nl *...  1.54 us
    pallas_call x1, Pallas kernels, local(): pl.pallas_call(functools.partial(rest_kernel, dims, nr - 1), out_shape=ou...  0.99 us
    pallas_call x1, Pallas kernels, local(): pl.pallas_call(functools.partial(own_kernel, dims), out_shape=[jax.ShapeD...  0.98 us
  transfers between devices with their start and end apart: 16, of which 10 were waited for; matrix products, arithmetic and copies ran while one was open for 0% of the time, Pallas kernels for 7%

profile of v8, /device:TPU:0, one launch (start us, length us, event | category | flops | bytes accessed | tf_op | source)
XLA Modules:
  0.0 36.9 jit_solution(12028864148642208744)
XLA Ops:
  0.6 2.4 %collective-permute-start.1 = (bf16[1,128,128]{2,1,0:T(8,128)(2,1)}, bf16[1,128,128]{2,1,0:T(8,128)(2,1)S(1)}, u32[]{:S(2)}, u32[]{:S(2)}) collective-permute-start(bf16[1,128,128]{2,1,0:T(8,128)(2,1)} %theta.1), channel_id=1, source_target_pairs={{0,3},{1,2},{2,1},{3,0},{4,7},{5,6},{6,5},{7,4},{8,11},{9,10},{10,... | collective-permute-start | bytes 98312 | tf_op jit(solution)/shard_map/ppermute | solution.py:188
  3.1 0.6 %collective-permute-start = (s32[14,1,16]{2,1,0:T(1,128)}, s32[14,1,16]{2,1,0:T(1,128)S(1)}, u32[]{:S(2)}, u32[]{:S(2)}) collective-permute-start(s32[14,1,16]{2,1,0:T(1,128)} %bitcast.14), channel_id=1, source_target_pairs={{0,2},{1,3},{2,0},{3,1},{4,6},{5,7},{6,4},{7,5},{8,10},{9,11},{10,... | collective-permute-start | bytes 2696 | tf_op jit(solution)/shard_map/ppermute | solution.py:188
  3.7 1.6 %load.1 = (bf16[32,128,128]{2,1,0:T(8,128)(2,1)S(1)}, bf16[32,128,128]{2,1,0:T(8,128)(2,1)S(1)}) custom-call(bf16[32,128,128]{2,1,0:T(8,128)(2,1)} %bitcast.17, bf16[32,128,128]{2,1,0:T(8,128)(2,1)} %bitcast.18), custom_call_target="tpu_custom_call" | custom-call | tf_op jit(solution)/shard_map/load/pallas_call | solution.py:222
  5.3 1.0 %first_own.1 = (f32[4,32,128]{2,1,0:T(8,128)S(1)}, f32[4,32,128]{2,1,0:T(8,128)S(1)}, f32[4,32,128]{2,1,0:T(8,128)S(1)}, f32[4,32,128]{2,1,0:T(8,128)S(1)}, s32[2,128]{1,0:T(2,128)S(1)}) custom-call(s32[14,1,16]{2,1,0:T(1,128)S(1)} %bitcast.15, bf16[1,128,128]{2,1,0:T(8,128)(2,1)S(1)} %copy-done.1, ...), custom_call_target="tpu_custom_call" | custom-call | tf_op jit(solution)/shard_map/first_own/pallas_call | solution.py:232
  6.3 0.6 %collective-permute-done.refs_0_ = s32[14,1,16]{2,1,0:T(1,128)S(1)} collective-permute-done((s32[14,1,16]{2,1,0:T(1,128)}, s32[14,1,16]{2,1,0:T(1,128)S(1)}, u32[]{:S(2)}, u32[]{:S(2)}) %collective-permute-start) | collective-permute-done | bytes 928 | tf_op jit(solution)/shard_map/ppermute | solution.py:188
  6.9 1.0 %first_rest.1 = (f32[128,128]{1,0:T(8,128)S(1)}, f32[128,128]{1,0:T(8,128)S(1)}, f32[128,128]{1,0:T(8,128)S(1)}, f32[128,128]{1,0:T(8,128)S(1)}, s32[1,2,128]{2,1,0:T(2,128)S(1)}) custom-call(s32[14,1,16]{2,1,0:T(1,128)S(1)} %collective-permute-done.refs_0_, bf16[1,128,128]{2,1,0:T(8,128)(2,1)S(1)} %collective-permute-done.1.refs_1_, ...), custom_call_target="tpu_custom_call" | custom-call | tf_op jit(solution)/shard_map/first_rest/pallas_call | solution.py:242
  8.0 3.7 %collective-permute-start.4 = (f32[128,128]{1,0:T(8,128)S(1)}, f32[128,128]{1,0:T(8,128)S(1)}, u32[]{:S(2)}, u32[]{:S(2)}) collective-permute-start(f32[128,128]{1,0:T(8,128)S(1)} %get-tuple-element.27), channel_id=1, source_target_pairs={{0,13},{1,12},{2,15},{3,14},{4,9},{5,8},{6,11},{7,10},{8,5},{9,4},... | collective-permute-start | bytes 196616 | tf_op jit(solution)/shard_map/ppermute | solution.py:188
  11.8 2.3 %collective-permute-done.4 = f32[128,128]{1,0:T(8,128)S(1)} collective-permute-done((f32[128,128]{1,0:T(8,128)S(1)}, f32[128,128]{1,0:T(8,128)S(1)}, u32[]{:S(2)}, u32[]{:S(2)}) %collective-permute-start.4) | collective-permute-done | bytes 65568 | tf_op jit(solution)/shard_map/ppermute | solution.py:188
  14.1 1.3 %collective-permute-done.3 = f32[128,128]{1,0:T(8,128)S(1)} collective-permute-done((f32[128,128]{1,0:T(8,128)S(1)}, f32[128,128]{1,0:T(8,128)S(1)}, u32[]{:S(2)}, u32[]{:S(2)}) %collective-permute-start.3) | collective-permute-done | bytes 65568 | tf_op jit(solution)/shard_map/ppermute | solution.py:188
  15.5 1.0 %collective-permute-start.5 = (f32[128,128]{1,0:T(8,128)S(1)}, f32[128,128]{1,0:T(8,128)S(1)}, u32[]{:S(2)}, u32[]{:S(2)}) collective-permute-start(f32[128,128]{1,0:T(8,128)S(1)} %add_add_fusion.1), channel_id=1, source_target_pairs={{0,1},{1,0},{2,3},{3,2},{4,5},{5,4},{6,7},{7,6},{8,9},{9,8},{10,11... | collective-permute-start | bytes 196616 | tf_op jit(solution)/shard_map/ppermute | solution.py:188
  16.5 0.8 %collective-permute-start.6 = (f32[128,128]{1,0:T(8,128)S(1)}, f32[128,128]{1,0:T(8,128)S(1)}, u32[]{:S(2)}, u32[]{:S(2)}) collective-permute-start(f32[128,128]{1,0:T(8,128)S(1)} %add_add_fusion.1), channel_id=1, source_target_pairs={{0,3},{1,2},{2,1},{3,0},{4,7},{5,6},{6,5},{7,4},{8,11},{9,10},{10,... | collective-permute-start | bytes 196616 | tf_op jit(solution)/shard_map/ppermute | solution.py:188
  17.4 2.8 %collective-permute-start.10 = (f32[8,128]{1,0:T(8,128)S(1)}, f32[8,128]{1,0:T(8,128)S(1)}, u32[]{:S(2)}, u32[]{:S(2)}) collective-permute-start(f32[8,128]{1,0:T(8,128)S(1)} %get-tuple-element.36), channel_id=1, source_target_pairs={{0,12},{1,15},{2,14},{3,13},{4,8},{5,11},{6,10},{7,9},{8,4},{9,7},... | collective-permute-start | bytes 12296 | tf_op jit(solution)/shard_map/ppermute | solution.py:188
  20.2 1.7 %collective-permute-start.8 = (f32[8,128]{1,0:T(8,128)S(1)}, f32[8,128]{1,0:T(8,128)S(1)}, u32[]{:S(2)}, u32[]{:S(2)}) collective-permute-start(f32[8,128]{1,0:T(8,128)S(1)} %get-tuple-element.36), channel_id=1, source_target_pairs={{0,4},{1,7},{2,6},{3,5},{4,0},{5,3},{6,2},{7,1},{8,12},{9,15},{10,... | collective-permute-start | bytes 12296 | tf_op jit(solution)/shard_map/ppermute | solution.py:188
  21.9 1.0 %collective-permute-start.7 = (f32[128,128]{1,0:T(8,128)S(1)}, f32[128,128]{1,0:T(8,128)S(1)}, u32[]{:S(2)}, u32[]{:S(2)}) collective-permute-start(f32[128,128]{1,0:T(8,128)S(1)} %collective-permute-done.6), channel_id=1, source_target_pairs={{0,1},{1,0},{2,3},{3,2},{4,5},{5,4},{6,7},{7,6},{8,9},{9,8},{10,11... | collective-permute-start | bytes 196616 | tf_op jit(solution)/shard_map/ppermute | solution.py:188
  22.9 1.8 %collective-permute-done.9 = f32[8,128]{1,0:T(8,128)S(1)} collective-permute-done((f32[8,128]{1,0:T(8,128)S(1)}, f32[8,128]{1,0:T(8,128)S(1)}, u32[]{:S(2)}, u32[]{:S(2)}) %collective-permute-start.9) | collective-permute-done | bytes 4128 | tf_op jit(solution)/shard_map/ppermute | solution.py:188
  24.9 1.0 %collective-permute-done.11.refs_6_ = f32[8,128]{1,0:T(8,128)S(1)} collective-permute-done((f32[8,128]{1,0:T(8,128)S(1)}, f32[8,128]{1,0:T(8,128)S(1)}, u32[]{:S(2)}, u32[]{:S(2)}) %collective-permute-start.11) | collective-permute-done | bytes 4128 | tf_op jit(solution)/shard_map/ppermute | solution.py:188
  25.9 1.5 %second_product.1 = (f32[128,128]{1,0:T(8,128)S(1)}, f32[128,128]{1,0:T(8,128)S(1)}, f32[128,128]{1,0:T(8,128)S(1)}, f32[128,128]{1,0:T(8,128)S(1)}) custom-call(s32[2,128]{1,0:T(2,128)S(1)} %get-tuple-element.28.refs_0_, s32[2,128]{1,0:T(2,128)S(1)} %bitcast.16, f32[128,128]{1,0:T(8,128)S(1)} %get-tuple-element.37.refs_2_, ...), custom_call_target="tpu_custom_call" | custom-call | tf_op jit(solution)/shard_map/second_product/pallas_call | solution.py:267
  27.7 1.4 %collective-permute-start.14 = (f32[128,128]{1,0:T(8,128)S(1)}, f32[128,128]{1,0:T(8,128)S(1)}, u32[]{:S(2)}, u32[]{:S(2)}) collective-permute-start(f32[128,128]{1,0:T(8,128)S(1)} %get-tuple-element.33), channel_id=1, source_target_pairs={{0,13},{1,12},{2,15},{3,14},{4,9},{5,8},{6,11},{7,10},{8,5},{9,4},... | collective-permute-start | bytes 196616 | tf_op jit(solution)/shard_map/ppermute | solution.py:188
  29.1 1.7 %collective-permute-start.13 = (f32[128,128]{1,0:T(8,128)S(1)}, f32[128,128]{1,0:T(8,128)S(1)}, u32[]{:S(2)}, u32[]{:S(2)}) collective-permute-start(f32[128,128]{1,0:T(8,128)S(1)} %add.44), channel_id=1, source_target_pairs={{0,9},{1,4},{2,11},{3,6},{4,13},{5,0},{6,15},{7,2},{8,1},{9,12},{1... | collective-permute-start | bytes 196616 | tf_op jit(solution)/shard_map/ppermute | solution.py:188
  30.9 2.7 %collective-permute-done.14 = f32[128,128]{1,0:T(8,128)S(1)} collective-permute-done((f32[128,128]{1,0:T(8,128)S(1)}, f32[128,128]{1,0:T(8,128)S(1)}, u32[]{:S(2)}, u32[]{:S(2)}) %collective-permute-start.14) | collective-permute-done | bytes 65568 | tf_op jit(solution)/shard_map/ppermute | solution.py:188
  33.5 1.3 %collective-permute-done.13 = f32[128,128]{1,0:T(8,128)S(1)} collective-permute-done((f32[128,128]{1,0:T(8,128)S(1)}, f32[128,128]{1,0:T(8,128)S(1)}, u32[]{:S(2)}, u32[]{:S(2)}) %collective-permute-start.13) | collective-permute-done | bytes 65568 | tf_op jit(solution)/shard_map/ppermute | solution.py:188
  34.9 0.4 collective-permute-start.15
  35.3 1.0 %collective-permute-done.15 = f32[128,128]{1,0:T(8,128)S(1)} collective-permute-done((f32[128,128]{1,0:T(8,128)S(1)}, f32[128,128]{1,0:T(8,128)S(1)}, u32[]{:S(2)}, u32[]{:S(2)}) %collective-permute-start.15) | collective-permute-done | bytes 65568 | tf_op jit(solution)/shard_map/ppermute | solution.py:188
  36.2 0.6 %add_bitcast_fusion = f32[1,128,128]{2,1,0:T(8,128)} fusion(f32[128,128]{1,0:T(8,128)S(1)} %add_add_fusion, f32[128,128]{1,0:T(8,128)S(1)} %collective-permute-done.15), kind=kLoop, calls=%fused_computation.2 | loop fusion | flops 16384 | bytes 196608 | tf_op jit(solution)/shard_map/broadcast_in_dim | solution.py:278
  (27 shorter events, 0.7 us)
Async XLA Ops:
  0.6 6.3 %collective-permute-start.1 = (bf16[1,128,128]{2,1,0:T(8,128)(2,1)}, bf16[1,128,128]{2,1,0:T(8,128)(2,1)S(1)}, u32[]{:S(2)}, u32[]{:S(2)}) collective-permute-start(bf16[1,128,128]{2,1,0:T(8,128)(2,1)} %theta.1), channel_id=1, source_target_pairs={{0,3},{1,2},{2,1},{3,0},{4,7},{5,6},{6,5},{7,4},{8,11},{9,10},{10,... | collective-permute-start | bytes 98312 | tf_op jit(solution)/shard_map/ppermute | solution.py:188
  3.1 3.9 %collective-permute-start = (s32[14,1,16]{2,1,0:T(1,128)}, s32[14,1,16]{2,1,0:T(1,128)S(1)}, u32[]{:S(2)}, u32[]{:S(2)}) collective-permute-start(s32[14,1,16]{2,1,0:T(1,128)} %bitcast.14), channel_id=1, source_target_pairs={{0,2},{1,3},{2,0},{3,1},{4,6},{5,7},{6,4},{7,5},{8,10},{9,11},{10,... | collective-permute-start | bytes 2696 | tf_op jit(solution)/shard_map/ppermute | solution.py:188
  3.7 1.6 %copy-start.1 = (bf16[1,128,128]{2,1,0:T(8,128)(2,1)S(1)}, bf16[1,128,128]{2,1,0:T(8,128)(2,1)}, u32[]{:S(2)}) copy-start(bf16[1,128,128]{2,1,0:T(8,128)(2,1)} %theta.1) | copy-start | bytes 98308
  3.7 1.6 %copy-start.2 = (s32[1,1,1,16,14]{3,2,4,1,0:T(1,128)S(1)}, s32[1,1,1,16,14]{3,2,4,1,0:T(1,128)}, u32[]{:S(2)}) copy-start(s32[1,1,1,16,14]{3,2,4,1,0:T(1,128)} %param.7) | copy-start | bytes 2692
  7.9 3.8 %collective-permute-start.2 = (f32[128,128]{1,0:T(8,128)S(1)}, f32[128,128]{1,0:T(8,128)S(1)}, u32[]{:S(2)}, u32[]{:S(2)}) collective-permute-start(f32[128,128]{1,0:T(8,128)S(1)} %get-tuple-element.26), channel_id=1, source_target_pairs={{0,1},{1,0},{2,3},{3,2},{4,5},{5,4},{6,7},{7,6},{8,9},{9,8},{10,11... | collective-permute-start | bytes 196616 | tf_op jit(solution)/shard_map/ppermute | solution.py:188
  8.0 6.1 %collective-permute-start.4 = (f32[128,128]{1,0:T(8,128)S(1)}, f32[128,128]{1,0:T(8,128)S(1)}, u32[]{:S(2)}, u32[]{:S(2)}) collective-permute-start(f32[128,128]{1,0:T(8,128)S(1)} %get-tuple-element.27), channel_id=1, source_target_pairs={{0,13},{1,12},{2,15},{3,14},{4,9},{5,8},{6,11},{7,10},{8,5},{9,4},... | collective-permute-start | bytes 196616 | tf_op jit(solution)/shard_map/ppermute | solution.py:188
  11.7 3.7 %collective-permute-start.3 = (f32[128,128]{1,0:T(8,128)S(1)}, f32[128,128]{1,0:T(8,128)S(1)}, u32[]{:S(2)}, u32[]{:S(2)}) collective-permute-start(f32[128,128]{1,0:T(8,128)S(1)} %add.36), channel_id=1, source_target_pairs={{0,9},{1,4},{2,11},{3,6},{4,13},{5,0},{6,15},{7,2},{8,1},{9,12},{1... | collective-permute-start | bytes 196616 | tf_op jit(solution)/shard_map/ppermute | solution.py:188
  15.5 1.9 %collective-permute-start.5 = (f32[128,128]{1,0:T(8,128)S(1)}, f32[128,128]{1,0:T(8,128)S(1)}, u32[]{:S(2)}, u32[]{:S(2)}) collective-permute-start(f32[128,128]{1,0:T(8,128)S(1)} %add_add_fusion.1), channel_id=1, source_target_pairs={{0,1},{1,0},{2,3},{3,2},{4,5},{5,4},{6,7},{7,6},{8,9},{9,8},{10,11... | collective-permute-start | bytes 196616 | tf_op jit(solution)/shard_map/ppermute | solution.py:188
  16.5 5.4 %collective-permute-start.6 = (f32[128,128]{1,0:T(8,128)S(1)}, f32[128,128]{1,0:T(8,128)S(1)}, u32[]{:S(2)}, u32[]{:S(2)}) collective-permute-start(f32[128,128]{1,0:T(8,128)S(1)} %add_add_fusion.1), channel_id=1, source_target_pairs={{0,3},{1,2},{2,1},{3,0},{4,7},{5,6},{6,5},{7,4},{8,11},{9,10},{10,... | collective-permute-start | bytes 196616 | tf_op jit(solution)/shard_map/ppermute | solution.py:188
  17.4 8.5 %copy-start = (f32[128,128]{1,0:T(8,128)}, f32[128,128]{1,0:T(8,128)S(1)}, u32[]{:S(2)}) copy-start(f32[128,128]{1,0:T(8,128)S(1)} %get-tuple-element.37.refs_2_) | copy-start | bytes 196612
  17.4 5.5 %collective-permute-start.10 = (f32[8,128]{1,0:T(8,128)S(1)}, f32[8,128]{1,0:T(8,128)S(1)}, u32[]{:S(2)}, u32[]{:S(2)}) collective-permute-start(f32[8,128]{1,0:T(8,128)S(1)} %get-tuple-element.36), channel_id=1, source_target_pairs={{0,12},{1,15},{2,14},{3,13},{4,8},{5,11},{6,10},{7,9},{8,4},{9,7},... | collective-permute-start | bytes 12296 | tf_op jit(solution)/shard_map/ppermute | solution.py:188
  20.2 4.5 %collective-permute-start.9 = (f32[8,128]{1,0:T(8,128)S(1)}, f32[8,128]{1,0:T(8,128)S(1)}, u32[]{:S(2)}, u32[]{:S(2)}) collective-permute-start(f32[8,128]{1,0:T(8,128)S(1)} %get-tuple-element.36), channel_id=1, source_target_pairs={{0,8},{1,11},{2,10},{3,9},{4,12},{5,15},{6,14},{7,13},{8,0},{9,3},... | collective-permute-start | bytes 12296 | tf_op jit(solution)/shard_map/ppermute | solution.py:188
  20.2 4.5 %collective-permute-start.8 = (f32[8,128]{1,0:T(8,128)S(1)}, f32[8,128]{1,0:T(8,128)S(1)}, u32[]{:S(2)}, u32[]{:S(2)}) collective-permute-start(f32[8,128]{1,0:T(8,128)S(1)} %get-tuple-element.36), channel_id=1, source_target_pairs={{0,4},{1,7},{2,6},{3,5},{4,0},{5,3},{6,2},{7,1},{8,12},{9,15},{10,... | collective-permute-start | bytes 12296 | tf_op jit(solution)/shard_map/ppermute | solution.py:188
  21.9 3.0 %collective-permute-start.7 = (f32[128,128]{1,0:T(8,128)S(1)}, f32[128,128]{1,0:T(8,128)S(1)}, u32[]{:S(2)}, u32[]{:S(2)}) collective-permute-start(f32[128,128]{1,0:T(8,128)S(1)} %collective-permute-done.6), channel_id=1, source_target_pairs={{0,1},{1,0},{2,3},{3,2},{4,5},{5,4},{6,7},{7,6},{8,9},{9,8},{10,11... | collective-permute-start | bytes 196616 | tf_op jit(solution)/shard_map/ppermute | solution.py:188
  24.8 1.2 %collective-permute-start.11 = (f32[8,128]{1,0:T(8,128)S(1)}, f32[8,128]{1,0:T(8,128)S(1)}, u32[]{:S(2)}, u32[]{:S(2)}) collective-permute-start(f32[8,128]{1,0:T(8,128)S(1)} %add_add_fusion.2.refs_5_), channel_id=1, source_target_pairs={{0,1},{1,0},{2,3},{3,2},{4,5},{5,4},{6,7},{7,6},{8,9},{9,8},{10,11... | collective-permute-start | bytes 12296 | tf_op jit(solution)/shard_map/ppermute | solution.py:188
  27.5 1.6 %collective-permute-start.12 = (f32[128,128]{1,0:T(8,128)S(1)}, f32[128,128]{1,0:T(8,128)S(1)}, u32[]{:S(2)}, u32[]{:S(2)}) collective-permute-start(f32[128,128]{1,0:T(8,128)S(1)} %get-tuple-element.32), channel_id=1, source_target_pairs={{0,1},{1,0},{2,3},{3,2},{4,5},{5,4},{6,7},{7,6},{8,9},{9,8},{10,11... | collective-permute-start | bytes 196616 | tf_op jit(solution)/shard_map/ppermute | solution.py:188
  27.7 5.9 %collective-permute-start.14 = (f32[128,128]{1,0:T(8,128)S(1)}, f32[128,128]{1,0:T(8,128)S(1)}, u32[]{:S(2)}, u32[]{:S(2)}) collective-permute-start(f32[128,128]{1,0:T(8,128)S(1)} %get-tuple-element.33), channel_id=1, source_target_pairs={{0,13},{1,12},{2,15},{3,14},{4,9},{5,8},{6,11},{7,10},{8,5},{9,4},... | collective-permute-start | bytes 196616 | tf_op jit(solution)/shard_map/ppermute | solution.py:188
  29.1 5.8 %collective-permute-start.13 = (f32[128,128]{1,0:T(8,128)S(1)}, f32[128,128]{1,0:T(8,128)S(1)}, u32[]{:S(2)}, u32[]{:S(2)}) collective-permute-start(f32[128,128]{1,0:T(8,128)S(1)} %add.44), channel_id=1, source_target_pairs={{0,9},{1,4},{2,11},{3,6},{4,13},{5,0},{6,15},{7,2},{8,1},{9,12},{1... | collective-permute-start | bytes 196616 | tf_op jit(solution)/shard_map/ppermute | solution.py:188
  34.9 1.3 %collective-permute-start.15 = (f32[128,128]{1,0:T(8,128)S(1)}, f32[128,128]{1,0:T(8,128)S(1)}, u32[]{:S(2)}, u32[]{:S(2)}) collective-permute-start(f32[128,128]{1,0:T(8,128)S(1)} %add_add_fusion), channel_id=1, source_target_pairs={{0,1},{1,0},{2,3},{3,2},{4,5},{5,4},{6,7},{7,6},{8,9},{9,8},{10,11... | collective-permute-start | bytes 196616 | tf_op jit(solution)/shard_map/ppermute | solution.py:188
